TPU v7x, 32 devices: a whole 2x2x4 slice. The times are simulated.
32 devices in a mesh: section: 2 (over y), dp: 4 (over x, core), tensor: 4 (over z).
Axes of the slice: x: 2, y: 2, z: 4, core: 2. Of those that a mesh axis runs over, the one named last changes fastest.
Arguments:
- inputs: bfloat16 [8, 1024, 1024], P('dp', 'tensor'), may hold values from -6 to 6
- segment_ids: int32 [8, 1024], P('dp'), may hold values from 0 to 3, as said below
- valid_frames: int32 [8, 1024], P('dp'), may hold values from 0 to 1, as said below
- segment_codes: int32 [8, 4], P('dp'), may hold values from 0 to 7
- norm_table: float32 [2, 8, 4, 1024], P('section'), may hold values from -1.5 to 1.5
- entry_weight: bfloat16 [2, 1024, 3, 1024], P('section', 'dp', None, 'tensor'), may hold values from -0.1875 to 0.1875
- mixing_weight: bfloat16 [2, 1024, 1024], P('section', 'tensor', 'dp'), may hold values from -3 to 3
- expand_weight: bfloat16 [2, 1024, 4096], P('section', 'dp', 'tensor'), may hold values from -0.1875 to 0.1875
- contract_weight: bfloat16 [2, 4096, 1024], P('section', 'tensor', 'dp'), may hold values from -0.09375 to 0.09375
- cotangent: bfloat16 [2, 8, 1024, 1024], P('section', 'dp', 'tensor'), may hold values from -6 to 6
Outputs:
- layer_outputs: bfloat16 [2, 8, 1024, 1024], P('section', 'dp', 'tensor')
- input_grads: float32 [2, 8, 1024, 1024], P('section', 'dp', 'tensor')
- entry_grad: float32 [2, 1024, 3, 1024], P('section', 'dp', None, 'tensor')
- mixing_grad: float32 [2, 1024, 1024], P('section', 'tensor', 'dp')
- expand_grad: float32 [2, 1024, 4096], P('section', 'dp', 'tensor')
- contract_grad: float32 [2, 4096, 1024], P('section', 'tensor', 'dp')
- table_grad: float32 [2, 8, 4, 1024], P('section')
Inputs may be any that keep to these rules, and one draw needn't show every extreme that they name: `segment_ids`: Non-decreasing along each row from 0; a row has 4 segments or a single one, and of the 2 rows of each index of dp exactly one has a single segment. `valid_frames`: in each row ones, then at most 64 zeros.
All inputs are finite; a program needn't handle non-finite values.
Results may differ from a plain program's by a relative error of at most 0.02.
Values may be sent and summed in bfloat16 or wider, within the bound.
No kernel may reach another device: no remote copies, remote signals or barrier semaphores. Data moves between devices by JAX's collectives and lax.ppermute only.
A program may use at most 128 MiB of HBM per device.

v0:
```python
import math

import jax
import jax.numpy as jnp
from jax import lax
from jax.sharding import PartitionSpec as P

HEAD_DIM = 64


NORM_EPS = 1e-05
MASKED = -1e30
HIGHEST = lax.Precision.HIGHEST


def shifted(block, axis, distance):
    devices = range(lax.axis_size(axis))
    route = [(i - distance, i) for i in devices if i - distance in devices]
    return lax.ppermute(block, axis, route)


def product(left, right, left_dim, right_dim):
    return lax.dot_general(
        left, right, (((left_dim,), (right_dim,)), ((), ())), preferred_element_type=jnp.float32
    )


def positions_table(segment_row, features):
    places = jnp.arange(segment_row.shape[0], dtype=jnp.int32)
    earlier = jnp.concatenate([segment_row[:1] - 1, segment_row[:-1]])
    starts = lax.cummax(jnp.where(segment_row != earlier, places, 0), axis=0)
    offset = (places - starts).astype(jnp.float32)
    column = jnp.arange(features, dtype=jnp.int32)
    frequency = jnp.exp(-math.log(10000.0) * (2 * (column // 2)).astype(jnp.float32) / features)
    angles = offset[:, None] * frequency[None, :]
    return jnp.where(column[None, :] % 2 == 0, jnp.sin(angles), jnp.cos(angles))


def code_weights(segment_row, code_row, code_count):
    slots = jnp.arange(code_row.shape[0], dtype=jnp.int32)
    token_code = jnp.sum(
        jnp.where(segment_row[:, None] == slots[None, :], code_row[None, :], 0), axis=1
    )
    return (token_code[:, None] == jnp.arange(code_count, dtype=jnp.int32)[None, :]).astype(
        jnp.float32
    )


def allowed_keys(segment_row, valid_row, first_row, block_rows, causal_flag):
    query_place = first_row + jnp.arange(block_rows, dtype=jnp.int32)
    key_place = jnp.arange(segment_row.shape[0], dtype=jnp.int32)
    query_segment = lax.dynamic_slice_in_dim(segment_row, first_row, block_rows, 0)
    permitted = (query_segment[:, None] == segment_row[None, :]) & (valid_row[None, :] == 1)
    permitted = permitted & (
        (key_place[None, :] <= query_place[:, None]) | jnp.logical_not(causal_flag)
    )
    return permitted | (key_place[None, :] == query_place[:, None])


def adaptive_norm(values_in, scale, shift):
    centred = values_in - jnp.mean(values_in, axis=-1, keepdims=True)
    spread = jnp.mean(centred * centred, axis=-1, keepdims=True)
    return centred * lax.rsqrt(spread + NORM_EPS) * (1.0 + scale) + shift


def block_layout(frame_count):
    blocks = max(1, frame_count // 512)
    return (blocks, frame_count // blocks)


def masked_scores(query_part, keys_all, segment_row, valid_row, first_row, block_rows, causal_flag):
    scores = jnp.einsum(
        "qhe,khe->hqk", query_part, keys_all, preferred_element_type=jnp.float32
    ) * (1.0 / math.sqrt(HEAD_DIM))
    permitted = allowed_keys(segment_row, valid_row, first_row, block_rows, causal_flag)
    return jnp.where(permitted[None], scores, MASKED)


def attend(queries, keys_all, values_all, segment_row, valid_row, causal_flag):
    frame_count = queries.shape[0]
    blocks, block_rows = block_layout(frame_count)

    def one_block(first_row):
        query_part = lax.dynamic_slice_in_dim(queries, first_row, block_rows, 0)
        scores = masked_scores(
            query_part, keys_all, segment_row, valid_row, first_row, block_rows, causal_flag
        )
        row_peak = jnp.max(scores, axis=-1, keepdims=True)
        totals = jnp.sum(jnp.exp(scores - row_peak), axis=-1, keepdims=True)
        logsum = row_peak + jnp.log(totals)
        weights = jnp.exp(scores - logsum).astype(jnp.bfloat16)
        mixture = jnp.einsum(
            "hqk,khe->qhe", weights, values_all, preferred_element_type=jnp.float32
        )
        return (mixture, logsum[:, :, 0])

    starts = jnp.arange(blocks, dtype=jnp.int32) * block_rows
    mixture, logsum = lax.map(one_block, starts)
    return (mixture.reshape(frame_count, -1), logsum)


def attend_back(
    queries, keys_all, values_all, mixture_grad, logsum, segment_row, valid_row, causal_flag
):
    frame_count, head_count, head_width = queries.shape
    blocks, block_rows = block_layout(frame_count)
    query_scale = 1.0 / math.sqrt(HEAD_DIM)

    def one_block(carried, block_index):
        key_grad, value_grad = carried
        first_row = block_index * block_rows
        query_part = lax.dynamic_slice_in_dim(queries, first_row, block_rows, 0)
        grad_part = lax.dynamic_slice_in_dim(mixture_grad, first_row, block_rows, 0)
        scores = masked_scores(
            query_part, keys_all, segment_row, valid_row, first_row, block_rows, causal_flag
        )
        weights = jnp.exp(scores - logsum[block_index][:, :, None])
        value_grad = value_grad + jnp.einsum(
            "hqk,qhe->khe",
            weights.astype(jnp.bfloat16),
            grad_part,
            preferred_element_type=jnp.float32,
        )
        weight_grad = jnp.einsum(
            "qhe,khe->hqk", grad_part, values_all, preferred_element_type=jnp.float32
        )
        row_inner = jnp.sum(weights * weight_grad, axis=-1, keepdims=True)
        score_grad = (weights * (weight_grad - row_inner)).astype(jnp.bfloat16)
        query_grad = (
            jnp.einsum("hqk,khe->qhe", score_grad, keys_all, preferred_element_type=jnp.float32)
            * query_scale
        )
        key_grad = (
            key_grad
            + jnp.einsum("hqk,qhe->khe", score_grad, query_part, preferred_element_type=jnp.float32)
            * query_scale
        )
        return ((key_grad, value_grad), query_grad)

    empty = jnp.zeros((frame_count, head_count, head_width), jnp.float32)
    carried, query_grad = lax.scan(one_block, (empty, empty), jnp.arange(blocks, dtype=jnp.int32))
    return (query_grad.reshape(frame_count, head_count, head_width), carried[0], carried[1])


def spread_rows(normed):
    return lax.all_gather(normed, "tensor", axis=0, tiled=True)


def fold_rows(term_rows):
    return lax.psum_scatter(
        term_rows.astype(jnp.bfloat16), "tensor", scatter_dimension=0, tiled=True
    ).astype(jnp.float32)


def spread_grads(gradient):
    return lax.all_gather(gradient, "tensor", axis=0, tiled=True)


def fold_grads(term_rows):
    return lax.psum_scatter(
        term_rows.astype(jnp.bfloat16), "tensor", scatter_dimension=0, tiled=True
    ).astype(jnp.float32)


def layer_forward(stream, segment_row, valid_row, coefficients, weights, causal_flag):
    entry_all, mixing_all, expand_all, contract_all = weights
    features = stream.shape[1]
    normed = adaptive_norm(stream, coefficients[:, 0], coefficients[:, 1]).astype(jnp.bfloat16)
    full_normed = spread_rows(normed)
    frame_count = full_normed.shape[0]
    projected = jnp.dot(
        full_normed, entry_all.reshape(features, -1), preferred_element_type=jnp.float32
    ).astype(jnp.bfloat16)
    projected = projected.reshape(frame_count, 3, -1, HEAD_DIM)
    mixture, logsum = attend(
        projected[:, 0], projected[:, 1], projected[:, 2], segment_row, valid_row, causal_flag
    )
    mixture = mixture.astype(jnp.bfloat16)
    middle = stream + fold_rows(jnp.dot(mixture, mixing_all, preferred_element_type=jnp.float32))
    second = adaptive_norm(middle, coefficients[:, 2], coefficients[:, 3]).astype(jnp.bfloat16)
    full_second = spread_rows(second)
    gate_pre = jnp.dot(full_second, expand_all, preferred_element_type=jnp.float32)
    hidden = jax.nn.gelu(gate_pre).astype(jnp.bfloat16)
    result = middle + fold_rows(jnp.dot(hidden, contract_all, preferred_element_type=jnp.float32))
    return (
        result,
        (
            full_normed,
            projected,
            mixture,
            mixing_all,
            logsum,
            middle,
            full_second,
            gate_pre,
            hidden,
        ),
    )


def layer_backward(stream, segment_row, valid_row, coefficients, weights, causal_flag, upstream):
    entry_all, mixing_all, expand_all, contract_all = weights
    features = stream.shape[1]
    result, saved = layer_forward(
        stream, segment_row, valid_row, coefficients, weights, causal_flag
    )
    (
        full_normed,
        projected,
        mix_operand,
        mixing_used,
        logsum,
        middle,
        full_second,
        gate_pre,
        hidden,
    ) = saved
    frame_count = full_normed.shape[0]
    branch_grad = spread_grads(upstream.astype(jnp.bfloat16))
    hidden_grad = product(branch_grad, contract_all, 1, 1)
    contract_term = product(hidden, branch_grad, 0, 0)
    gelu_value, gelu_back = jax.vjp(jax.nn.gelu, gate_pre)
    gate_grad = gelu_back(hidden_grad)[0].astype(jnp.bfloat16)
    expand_term = product(full_second, gate_grad, 0, 0)
    second_grad = fold_grads(product(gate_grad, expand_all, 1, 1))
    second_value, second_back = jax.vjp(
        adaptive_norm, middle, coefficients[:, 2], coefficients[:, 3]
    )
    middle_part, scale_two, shift_two = second_back(second_grad)
    middle_grad = upstream + middle_part
    mid_round = middle_grad.astype(jnp.bfloat16)
    attention_grad = spread_grads(mid_round)
    mixture_grad = product(attention_grad, mixing_all, 1, 1).astype(jnp.bfloat16)
    mixing_term = product(mix_operand, attention_grad, 0, 0)
    head_count = projected.shape[2]
    query_grad, key_grad, value_grad = attend_back(
        projected[:, 0],
        projected[:, 1],
        projected[:, 2],
        mixture_grad.reshape(frame_count, head_count, HEAD_DIM),
        logsum,
        segment_row,
        valid_row,
        causal_flag,
    )
    projected_grad = (
        jnp.stack((query_grad, key_grad, value_grad), axis=1)
        .reshape(frame_count, -1)
        .astype(jnp.bfloat16)
    )
    entry_term = product(full_normed, projected_grad, 0, 0).reshape(entry_all.shape)
    normed_grad = fold_grads(product(projected_grad, entry_all.reshape(features, -1), 1, 1))
    first_value, first_back = jax.vjp(adaptive_norm, stream, coefficients[:, 0], coefficients[:, 1])
    stream_part, scale_one, shift_one = first_back(normed_grad)
    coefficient_grad = jnp.stack((scale_one, shift_one, scale_two, shift_two), axis=1)
    return (
        middle_grad + stream_part,
        (entry_term, mixing_term, expand_term, contract_term),
        coefficient_grad,
    )


def local(
    inputs,
    segment_ids,
    valid_frames,
    segment_codes,
    norm_table,
    entry_weight,
    mixing_weight,
    expand_weight,
    contract_weight,
    cotangent,
):
    first_section = lax.axis_index("section") == 0
    micro_count, shard_rows, features = inputs.shape
    tensor_offset = lax.axis_index("tensor") * shard_rows
    code_count = norm_table.shape[1]
    table_local = norm_table[0].reshape(code_count, -1)

    def gather_weights():
        gathered = (
            lax.all_gather(entry_weight, "dp", axis=1, tiled=True),
            lax.all_gather(mixing_weight, "dp", axis=2, tiled=True),
            lax.all_gather(expand_weight, "dp", axis=1, tiled=True),
            lax.all_gather(contract_weight, "dp", axis=2, tiled=True),
        )
        return tuple((gathered_piece[0] for gathered_piece in gathered))

    def sum_weight_grads(weight_terms):
        mixing_term = weight_terms[1]
        return (
            lax.psum_scatter(
                weight_terms[0].astype(jnp.bfloat16), "dp", scatter_dimension=0, tiled=True
            ).astype(jnp.float32),
            lax.psum_scatter(
                mixing_term.astype(jnp.bfloat16), "dp", scatter_dimension=1, tiled=True
            ).astype(jnp.float32),
            lax.psum_scatter(
                weight_terms[2].astype(jnp.bfloat16), "dp", scatter_dimension=0, tiled=True
            ).astype(jnp.float32),
            lax.psum_scatter(
                weight_terms[3].astype(jnp.bfloat16), "dp", scatter_dimension=1, tiled=True
            ).astype(jnp.float32),
        )

    def row_context(row_index):
        segment_row = lax.dynamic_index_in_dim(segment_ids, row_index, 0, keepdims=False)
        valid_row = lax.dynamic_index_in_dim(valid_frames, row_index, 0, keepdims=False)
        code_row = lax.dynamic_index_in_dim(segment_codes, row_index, 0, keepdims=False)
        chooser = lax.dynamic_slice_in_dim(
            code_weights(segment_row, code_row, code_count), tensor_offset, shard_rows, 0
        )
        coefficients = jnp.dot(chooser, table_local, precision=HIGHEST).reshape(
            shard_rows, 4, features
        )
        return (segment_row, valid_row, chooser, coefficients)

    def current_weights():
        return gather_weights()

    def forward_tick(received, tick_index):
        row_index = jnp.clip(
            jnp.where(first_section, tick_index, tick_index - 1), 0, micro_count - 1
        )
        segment_row, valid_row, chooser, coefficients = row_context(row_index)
        own_rows = lax.dynamic_index_in_dim(inputs, row_index, 0, keepdims=False).astype(
            jnp.float32
        )
        own_rows = own_rows + lax.dynamic_slice_in_dim(
            positions_table(segment_row, features), tensor_offset, shard_rows, 0
        )
        stream = jnp.where(first_section, own_rows, received.astype(jnp.float32))
        result, saved = layer_forward(
            stream, segment_row, valid_row, coefficients, current_weights(), first_section
        )
        passed = shifted(result.astype(jnp.bfloat16), "section", 1)
        return (passed, (stream, result))

    ticks = jnp.arange(micro_count + 1, dtype=jnp.int32)
    start_rows = jnp.zeros((shard_rows, features), jnp.bfloat16)
    unused, (layer_inputs, layer_results) = lax.scan(forward_tick, start_rows, ticks)
    outputs = jnp.where(first_section, layer_results[:micro_count], layer_results[1:]).astype(
        jnp.bfloat16
    )[None]
    zero_terms = tuple(
        (
            jnp.zeros(weight_part.shape[1:], jnp.float32)
            for weight_part in (entry_weight, mixing_weight, expand_weight, contract_weight)
        )
    )

    def backward_tick(carried, tick_index):
        grad_received, table_term, weight_total = carried
        row_index = jnp.clip(
            jnp.where(first_section, tick_index - 1, tick_index), 0, micro_count - 1
        )
        active_tick = jnp.where(first_section, tick_index >= 1, tick_index < micro_count)
        segment_row, valid_row, chooser, coefficients = row_context(row_index)
        stream_index = jnp.where(
            first_section, jnp.maximum(tick_index - 1, 0), jnp.minimum(tick_index + 1, micro_count)
        )
        stream = lax.dynamic_index_in_dim(layer_inputs, stream_index, 0, keepdims=False)
        upstream = lax.dynamic_index_in_dim(cotangent[0], row_index, 0, keepdims=False).astype(
            jnp.float32
        )
        upstream = jnp.where(first_section, upstream + grad_received, upstream)
        upstream = jnp.where(active_tick, upstream, 0.0)
        stream_grad, weight_terms, coefficient_grad = layer_backward(
            stream, segment_row, valid_row, coefficients, current_weights(), first_section, upstream
        )
        table_term = table_term + jnp.dot(
            chooser.T, coefficient_grad.reshape(shard_rows, -1), precision=HIGHEST
        )
        weight_terms = sum_weight_grads(weight_terms)
        weight_total = tuple(
            (
                first_term + second_term
                for first_term, second_term in zip(weight_total, weight_terms)
            )
        )
        grad_passed = shifted(stream_grad.astype(jnp.bfloat16), "section", -1).astype(
            stream_grad.dtype
        )
        return ((grad_passed, table_term, weight_total), stream_grad)

    start_carry = (
        jnp.zeros((shard_rows, features), jnp.float32),
        jnp.zeros(table_local.shape, jnp.float32),
        zero_terms,
    )
    (unused_grad, table_term, weight_total), back_rows = lax.scan(backward_tick, start_carry, ticks)
    input_grads = jnp.where(first_section, back_rows[1:], back_rows[:micro_count])[None]
    table_grad = lax.psum(table_term, ("dp", "tensor")).reshape(norm_table.shape)
    return (
        outputs,
        input_grads,
        weight_total[0][None],
        weight_total[1][None],
        weight_total[2][None],
        weight_total[3][None],
        table_grad,
    )


def solution(mesh):
    placed = (
        P("dp", "tensor", None),
        P("dp", None),
        P("dp", None),
        P("dp", None),
        P("section", None, None, None),
        P("section", "dp", None, "tensor"),
        P("section", "tensor", "dp"),
        P("section", "dp", "tensor"),
        P("section", "tensor", "dp"),
        P("section", "dp", "tensor", None),
    )
    return jax.shard_map(
        local,
        mesh=mesh,
        in_specs=placed,
        out_specs=(
            P("section", "dp", "tensor", None),
            P("section", "dp", "tensor", None),
            P("section", "dp", None, "tensor"),
            P("section", "tensor", "dp"),
            P("section", "dp", "tensor"),
            P("section", "tensor", "dp"),
            P("section", None, None, None),
        ),
        check_vma=False,
    )
```

profile of v0, /device:TPU:1, one launch (start us, length us, event | category | flops | bytes accessed | tf_op | source)
XLA Modules:
  0.0 2894.0 jit_solution(17799221365053015108)
XLA Ops:
  14.5 991.3 %while.128 = (s32[]{:T(128)}, bf16[256,1024]{1,0:T(8,128)(2,1)S(1)}, f32[3,256,1024]{2,1,0:T(8,128)}, bf16[3,256,1024]{2,1,0:T(8,128)(2,1)}, pred[]{:T(512)}, /*...) while((s32[]{:T(128)}, bf16[256,1024]{1,0:T(8,128)(2,1)S(1)}, ...), condition=%wide.region_14.15_spmd, body=%wide.region_0.14_spmd.sunk | while | flops 7140972544 | bytes 157636400 | solution.py:342
  66.9 38.4 %all-gather.15.cloned.1.call-done = bf16[1024,1024]{1,0:T(8,128)(2,1)} async-done(((bf16[256,1024]{1,0:T(8,128)(2,1)}), bf16[1024,1024]{1,0:T(8,128)(2,1)}) %all-gather.15.cloned.1.call-update) | async-done | bytes 2097168 | tf_op jit(solution)/shard_map/while/body/eval_jaxpr/all_gather | solution.py:146
  110.1 22.4 while.132
  137.6 41.4 %reduce-scatter.10.cloned.1.call-done = bf16[256,1024]{1,0:T(8,128)(2,1)} async-done(((bf16[1024,1024]{1,0:T(8,128)(2,1)}), bf16[256,1024]{1,0:T(8,128)(2,1)}) %reduce-scatter.10.cloned.1.call-update) | async-done | bytes 524304 | tf_op jit(solution)/shard_map/while/body/eval_jaxpr/reduce_scatter | solution.py:150
  203.2 24.1 all-gather.21.cloned.1.call-done
  227.3 47.7 %all-gather.19.cloned.1.call-done = bf16[1024,1024]{1,0:T(8,128)(2,1)} async-done(((bf16[256,1024]{1,0:T(8,128)(2,1)}), bf16[1024,1024]{1,0:T(8,128)(2,1)}) %all-gather.19.cloned.1.call-update) | async-done | bytes 2097168 | tf_op jit(solution)/shard_map/while/body/eval_jaxpr/all_gather | solution.py:146
  283.8 42.6 %reduce-scatter.12.cloned.1.call-done = bf16[256,1024]{1,0:T(8,128)(2,1)} async-done(((bf16[1024,1024]{1,0:T(8,128)(2,1)}), bf16[256,1024]{1,0:T(8,128)(2,1)}) %reduce-scatter.12.cloned.1.call-update) | async-done | bytes 524304 | tf_op jit(solution)/shard_map/while/body/eval_jaxpr/reduce_scatter | solution.py:150
  397.7 37.8 %all-gather.15.cloned.1.call-done = bf16[1024,1024]{1,0:T(8,128)(2,1)} async-done(((bf16[256,1024]{1,0:T(8,128)(2,1)}), bf16[1024,1024]{1,0:T(8,128)(2,1)}) %all-gather.15.cloned.1.call-update) | async-done | bytes 2097168 | tf_op jit(solution)/shard_map/while/body/eval_jaxpr/all_gather | solution.py:146
  440.3 22.4 while.132
  467.9 41.2 %reduce-scatter.10.cloned.1.call-done = bf16[256,1024]{1,0:T(8,128)(2,1)} async-done(((bf16[1024,1024]{1,0:T(8,128)(2,1)}), bf16[256,1024]{1,0:T(8,128)(2,1)}) %reduce-scatter.10.cloned.1.call-update) | async-done | bytes 524304 | tf_op jit(solution)/shard_map/while/body/eval_jaxpr/reduce_scatter | solution.py:150
  533.6 24.1 all-gather.21.cloned.1.call-done
  557.7 47.8 %all-gather.19.cloned.1.call-done = bf16[1024,1024]{1,0:T(8,128)(2,1)} async-done(((bf16[256,1024]{1,0:T(8,128)(2,1)}), bf16[1024,1024]{1,0:T(8,128)(2,1)}) %all-gather.19.cloned.1.call-update) | async-done | bytes 2097168 | tf_op jit(solution)/shard_map/while/body/eval_jaxpr/all_gather | solution.py:146
  614.2 42.6 %reduce-scatter.12.cloned.1.call-done = bf16[256,1024]{1,0:T(8,128)(2,1)} async-done(((bf16[1024,1024]{1,0:T(8,128)(2,1)}), bf16[256,1024]{1,0:T(8,128)(2,1)}) %reduce-scatter.12.cloned.1.call-update) | async-done | bytes 524304 | tf_op jit(solution)/shard_map/while/body/eval_jaxpr/reduce_scatter | solution.py:150
  728.0 37.8 %all-gather.15.cloned.1.call-done = bf16[1024,1024]{1,0:T(8,128)(2,1)} async-done(((bf16[256,1024]{1,0:T(8,128)(2,1)}), bf16[1024,1024]{1,0:T(8,128)(2,1)}) %all-gather.15.cloned.1.call-update) | async-done | bytes 2097168 | tf_op jit(solution)/shard_map/while/body/eval_jaxpr/all_gather | solution.py:146
  770.6 22.4 while.132
  798.3 41.2 %reduce-scatter.10.cloned.1.call-done = bf16[256,1024]{1,0:T(8,128)(2,1)} async-done(((bf16[1024,1024]{1,0:T(8,128)(2,1)}), bf16[256,1024]{1,0:T(8,128)(2,1)}) %reduce-scatter.10.cloned.1.call-update) | async-done | bytes 524304 | tf_op jit(solution)/shard_map/while/body/eval_jaxpr/reduce_scatter | solution.py:150
  863.7 24.2 all-gather.21.cloned.1.call-done
  888.0 47.6 %all-gather.19.cloned.1.call-done = bf16[1024,1024]{1,0:T(8,128)(2,1)} async-done(((bf16[256,1024]{1,0:T(8,128)(2,1)}), bf16[1024,1024]{1,0:T(8,128)(2,1)}) %all-gather.19.cloned.1.call-update) | async-done | bytes 2097168 | tf_op jit(solution)/shard_map/while/body/eval_jaxpr/all_gather | solution.py:146
  944.4 42.6 %reduce-scatter.12.cloned.1.call-done = bf16[256,1024]{1,0:T(8,128)(2,1)} async-done(((bf16[1024,1024]{1,0:T(8,128)(2,1)}), bf16[256,1024]{1,0:T(8,128)(2,1)}) %reduce-scatter.12.cloned.1.call-update) | async-done | bytes 524304 | tf_op jit(solution)/shard_map/while/body/eval_jaxpr/reduce_scatter | solution.py:150
  1007.9 1786.4 %while.131 = (s32[]{:T(128)}, f32[256,1024]{1,0:T(8,128)}, f32[8,4096]{1,0:T(8,128)}, f32[256,3,256]{2,0,1:T(8,128)}, f32[256,256]{1,0:T(8,128)}, /*index=5*/f32...) while((s32[]{:T(128)}, f32[256,1024]{1,0:T(8,128)}, ...), condition=%wide.region_39.40_spmd.clone, body=%wide.region_15.39_spmd.clone.sunk | while | flops 19389042688 | bytes 496380096 | solution.py:392
  1051.8 37.9 %all-gather.23.cloned.1.call-done = bf16[1024,1024]{1,0:T(8,128)(2,1)} async-done(((bf16[256,1024]{1,0:T(8,128)(2,1)}), bf16[1024,1024]{1,0:T(8,128)(2,1)}) %all-gather.23.cloned.1.call-update) | async-done | bytes 2097168 | tf_op jit(solution)/shard_map/while/body/eval_jaxpr/all_gather | solution.py:146
  1119.2 41.8 %reduce-scatter.14.cloned.1.call-done = bf16[256,1024]{1,0:T(8,128)(2,1)} async-done(((bf16[1024,1024]{1,0:T(8,128)(2,1)}), bf16[256,1024]{1,0:T(8,128)(2,1)}) %reduce-scatter.14.cloned.1.call-update) | async-done | bytes 524304 | tf_op jit(solution)/shard_map/while/body/eval_jaxpr/reduce_scatter | solution.py:150
  1185.1 47.6 %all-gather.27.cloned.1.call-done = bf16[1024,1024]{1,0:T(8,128)(2,1)} async-done(((bf16[256,1024]{1,0:T(8,128)(2,1)}), bf16[1024,1024]{1,0:T(8,128)(2,1)}) %all-gather.27.cloned.1.call-update) | async-done | bytes 2097168 | tf_op jit(solution)/shard_map/while/body/eval_jaxpr/all_gather | solution.py:146
  1256.2 47.2 %all-gather.31.cloned.1.call-done = bf16[1024,1024]{1,0:T(8,128)(2,1)} async-done(((bf16[256,1024]{1,0:T(8,128)(2,1)}), bf16[1024,1024]{1,0:T(8,128)(2,1)}) %all-gather.31.cloned.1.call-update) | async-done | bytes 2097168 | tf_op jit(solution)/shard_map/while/body/eval_jaxpr/all_gather | solution.py:156
  1316.6 42.5 %reduce-scatter.16.cloned.1.call-done = bf16[256,1024]{1,0:T(8,128)(2,1)} async-done(((bf16[1024,1024]{1,0:T(8,128)(2,1)}), bf16[256,1024]{1,0:T(8,128)(2,1)}) %reduce-scatter.16.cloned.1.call-update) | async-done | bytes 524304 | tf_op jit(solution)/shard_map/while/body/eval_jaxpr/reduce_scatter | solution.py:160
  1378.9 32.0 %all-gather.35.cloned.1.call-done = bf16[1024,1024]{1,0:T(8,128)(2,1)} async-done(((bf16[256,1024]{1,0:T(8,128)(2,1)}), bf16[1024,1024]{1,0:T(8,128)(2,1)}) %all-gather.35.cloned.1.call-update) | async-done | bytes 2097168 | tf_op jit(solution)/shard_map/while/body/eval_jaxpr/all_gather | solution.py:156
  1417.4 56.9 %while.134 = (s32[]{:T(128)}, f32[1024,4,64]{0,2,1:T(8,128)S(1)}, f32[1024,4,64]{0,2,1:T(8,128)}, bf16[2,512,4,64]{1,0,3,2:T(2,128)(2,1)}, s32[2]{0:T(128)S(1)},...) while((s32[]{:T(128)}, f32[1024,4,64]{0,2,1:T(8,128)S(1)}, ...), condition=%wide.region_31.31_spmd.clone, body=%wide.region_29.30_spmd.clone.sunk | while | flops 1378876928 | bytes 81604968 | solution.py:141
  1502.8 29.9 %reduce-scatter.20.cloned.1.call-done = bf16[256,3,256]{2,0,1:T(8,128)(2,1)} async-done(((bf16[1024,3,256]{2,0,1:T(8,128)(2,1)}), bf16[256,3,256]{2,0,1:T(8,128)(2,1)}) %reduce-scatter.20.cloned.1.call-update) | async-done | bytes 393232 | tf_op jit(solution)/shard_map/while/body/eval_jaxpr/reduce_scatter | solution.py:293
  1534.7 44.6 %reduce-scatter.18.cloned.1.call-done = bf16[256,1024]{1,0:T(8,128)(2,1)} async-done(((bf16[1024,1024]{1,0:T(8,128)(2,1)}), bf16[256,1024]{1,0:T(8,128)(2,1)}) %reduce-scatter.18.cloned.1.call-update) | async-done | bytes 524304 | tf_op jit(solution)/shard_map/while/body/eval_jaxpr/reduce_scatter | solution.py:160
  1646.7 36.1 %all-gather.23.cloned.1.call-done = bf16[1024,1024]{1,0:T(8,128)(2,1)} async-done(((bf16[256,1024]{1,0:T(8,128)(2,1)}), bf16[1024,1024]{1,0:T(8,128)(2,1)}) %all-gather.23.cloned.1.call-update) | async-done | bytes 2097168 | tf_op jit(solution)/shard_map/while/body/eval_jaxpr/all_gather | solution.py:146
  1712.0 41.9 %reduce-scatter.14.cloned.1.call-done = bf16[256,1024]{1,0:T(8,128)(2,1)} async-done(((bf16[1024,1024]{1,0:T(8,128)(2,1)}), bf16[256,1024]{1,0:T(8,128)(2,1)}) %reduce-scatter.14.cloned.1.call-update) | async-done | bytes 524304 | tf_op jit(solution)/shard_map/while/body/eval_jaxpr/reduce_scatter | solution.py:150
  1778.0 47.8 %all-gather.27.cloned.1.call-done = bf16[1024,1024]{1,0:T(8,128)(2,1)} async-done(((bf16[256,1024]{1,0:T(8,128)(2,1)}), bf16[1024,1024]{1,0:T(8,128)(2,1)}) %all-gather.27.cloned.1.call-update) | async-done | bytes 2097168 | tf_op jit(solution)/shard_map/while/body/eval_jaxpr/all_gather | solution.py:146
  1849.4 47.2 %all-gather.31.cloned.1.call-done = bf16[1024,1024]{1,0:T(8,128)(2,1)} async-done(((bf16[256,1024]{1,0:T(8,128)(2,1)}), bf16[1024,1024]{1,0:T(8,128)(2,1)}) %all-gather.31.cloned.1.call-update) | async-done | bytes 2097168 | tf_op jit(solution)/shard_map/while/body/eval_jaxpr/all_gather | solution.py:156
  1909.8 42.5 %reduce-scatter.16.cloned.1.call-done = bf16[256,1024]{1,0:T(8,128)(2,1)} async-done(((bf16[1024,1024]{1,0:T(8,128)(2,1)}), bf16[256,1024]{1,0:T(8,128)(2,1)}) %reduce-scatter.16.cloned.1.call-update) | async-done | bytes 524304 | tf_op jit(solution)/shard_map/while/body/eval_jaxpr/reduce_scatter | solution.py:160
  1972.3 31.8 %all-gather.35.cloned.1.call-done = bf16[1024,1024]{1,0:T(8,128)(2,1)} async-done(((bf16[256,1024]{1,0:T(8,128)(2,1)}), bf16[1024,1024]{1,0:T(8,128)(2,1)}) %all-gather.35.cloned.1.call-update) | async-done | bytes 2097168 | tf_op jit(solution)/shard_map/while/body/eval_jaxpr/all_gather | solution.py:156
  2010.6 56.9 %while.134 = (s32[]{:T(128)}, f32[1024,4,64]{0,2,1:T(8,128)S(1)}, f32[1024,4,64]{0,2,1:T(8,128)}, bf16[2,512,4,64]{1,0,3,2:T(2,128)(2,1)}, s32[2]{0:T(128)S(1)},...) while((s32[]{:T(128)}, f32[1024,4,64]{0,2,1:T(8,128)S(1)}, ...), condition=%wide.region_31.31_spmd.clone, body=%wide.region_29.30_spmd.clone.sunk | while | flops 1378876928 | bytes 81604968 | solution.py:141
  2095.7 29.8 %reduce-scatter.20.cloned.1.call-done = bf16[256,3,256]{2,0,1:T(8,128)(2,1)} async-done(((bf16[1024,3,256]{2,0,1:T(8,128)(2,1)}), bf16[256,3,256]{2,0,1:T(8,128)(2,1)}) %reduce-scatter.20.cloned.1.call-update) | async-done | bytes 393232 | tf_op jit(solution)/shard_map/while/body/eval_jaxpr/reduce_scatter | solution.py:293
  2127.7 44.3 %reduce-scatter.18.cloned.1.call-done = bf16[256,1024]{1,0:T(8,128)(2,1)} async-done(((bf16[1024,1024]{1,0:T(8,128)(2,1)}), bf16[256,1024]{1,0:T(8,128)(2,1)}) %reduce-scatter.18.cloned.1.call-update) | async-done | bytes 524304 | tf_op jit(solution)/shard_map/while/body/eval_jaxpr/reduce_scatter | solution.py:160
  2239.5 35.9 %all-gather.23.cloned.1.call-done = bf16[1024,1024]{1,0:T(8,128)(2,1)} async-done(((bf16[256,1024]{1,0:T(8,128)(2,1)}), bf16[1024,1024]{1,0:T(8,128)(2,1)}) %all-gather.23.cloned.1.call-update) | async-done | bytes 2097168 | tf_op jit(solution)/shard_map/while/body/eval_jaxpr/all_gather | solution.py:146
  2304.6 41.9 %reduce-scatter.14.cloned.1.call-done = bf16[256,1024]{1,0:T(8,128)(2,1)} async-done(((bf16[1024,1024]{1,0:T(8,128)(2,1)}), bf16[256,1024]{1,0:T(8,128)(2,1)}) %reduce-scatter.14.cloned.1.call-update) | async-done | bytes 524304 | tf_op jit(solution)/shard_map/while/body/eval_jaxpr/reduce_scatter | solution.py:150
  2370.5 47.8 %all-gather.27.cloned.1.call-done = bf16[1024,1024]{1,0:T(8,128)(2,1)} async-done(((bf16[256,1024]{1,0:T(8,128)(2,1)}), bf16[1024,1024]{1,0:T(8,128)(2,1)}) %all-gather.27.cloned.1.call-update) | async-done | bytes 2097168 | tf_op jit(solution)/shard_map/while/body/eval_jaxpr/all_gather | solution.py:146
  2442.0 47.2 %all-gather.31.cloned.1.call-done = bf16[1024,1024]{1,0:T(8,128)(2,1)} async-done(((bf16[256,1024]{1,0:T(8,128)(2,1)}), bf16[1024,1024]{1,0:T(8,128)(2,1)}) %all-gather.31.cloned.1.call-update) | async-done | bytes 2097168 | tf_op jit(solution)/shard_map/while/body/eval_jaxpr/all_gather | solution.py:156
  2502.4 42.5 %reduce-scatter.16.cloned.1.call-done = bf16[256,1024]{1,0:T(8,128)(2,1)} async-done(((bf16[1024,1024]{1,0:T(8,128)(2,1)}), bf16[256,1024]{1,0:T(8,128)(2,1)}) %reduce-scatter.16.cloned.1.call-update) | async-done | bytes 524304 | tf_op jit(solution)/shard_map/while/body/eval_jaxpr/reduce_scatter | solution.py:160
  2564.7 31.9 %all-gather.35.cloned.1.call-done = bf16[1024,1024]{1,0:T(8,128)(2,1)} async-done(((bf16[256,1024]{1,0:T(8,128)(2,1)}), bf16[1024,1024]{1,0:T(8,128)(2,1)}) %all-gather.35.cloned.1.call-update) | async-done | bytes 2097168 | tf_op jit(solution)/shard_map/while/body/eval_jaxpr/all_gather | solution.py:156
  2603.1 57.1 %while.134 = (s32[]{:T(128)}, f32[1024,4,64]{0,2,1:T(8,128)S(1)}, f32[1024,4,64]{0,2,1:T(8,128)}, bf16[2,512,4,64]{1,0,3,2:T(2,128)(2,1)}, s32[2]{0:T(128)S(1)},...) while((s32[]{:T(128)}, f32[1024,4,64]{0,2,1:T(8,128)S(1)}, ...), condition=%wide.region_31.31_spmd.clone, body=%wide.region_29.30_spmd.clone.sunk | while | flops 1378876928 | bytes 81604968 | solution.py:141
  2688.6 29.9 %reduce-scatter.20.cloned.1.call-done = bf16[256,3,256]{2,0,1:T(8,128)(2,1)} async-done(((bf16[1024,3,256]{2,0,1:T(8,128)(2,1)}), bf16[256,3,256]{2,0,1:T(8,128)(2,1)}) %reduce-scatter.20.cloned.1.call-update) | async-done | bytes 393232 | tf_op jit(solution)/shard_map/while/body/eval_jaxpr/reduce_scatter | solution.py:293
  2720.7 44.2 %reduce-scatter.18.cloned.1.call-done = bf16[256,1024]{1,0:T(8,128)(2,1)} async-done(((bf16[1024,1024]{1,0:T(8,128)(2,1)}), bf16[256,1024]{1,0:T(8,128)(2,1)}) %reduce-scatter.18.cloned.1.call-update) | async-done | bytes 524304 | tf_op jit(solution)/shard_map/while/body/eval_jaxpr/reduce_scatter | solution.py:160
  2801.4 83.6 %all-reduce.2.cloned.1.call-done = f32[1,8,4,1024]{3,2,1,0:T(4,128)} async-done(((f32[1,8,4,1024]{3,2,1,0:T(4,128)}), f32[1,8,4,1024]{3,2,1,0:T(4,128)}) %all-reduce.2.cloned.1.call-update) | async-done | bytes 131088 | tf_op jit(solution)/shard_map/psum | solution.py:394
  (968 shorter events, 1251.6 us)
Async XLA Ops:
  15.2 90.1 %all-gather.15.cloned.1.call-start = ((), (), s32[]{:S(2)}) async-start(), calls=%async_computation.11 | async-start | bytes 2621440 | tf_op jit(solution)/shard_map/while/body/eval_jaxpr/all_gather | solution.py:146
  57.2 121.8 %reduce-scatter.10.cloned.1.call-start = ((), (), s32[]{:S(2)}) async-start(), calls=%async_computation.13 | async-start | bytes 2621440 | tf_op jit(solution)/shard_map/while/body/eval_jaxpr/reduce_scatter | solution.py:150
  137.0 90.3 %all-gather.21.cloned.1.call-start = ((), (), s32[]{:S(2)}) async-start(), calls=%async_computation.15 | async-start | bytes 2621440 | tf_op jit(solution)/shard_map/while/body/eval_jaxpr/all_gather | solution.py:285
  137.6 137.4 %all-gather.19.cloned.1.call-start = ((), (), s32[]{:S(2)}) async-start(), calls=%async_computation.14 | async-start | bytes 2621440 | tf_op jit(solution)/shard_map/while/body/eval_jaxpr/all_gather | solution.py:146
  197.0 129.3 %reduce-scatter.12.cloned.1.call-start = ((), (), s32[]{:S(2)}) async-start(), calls=%async_computation.16 | async-start | bytes 2621440 | tf_op jit(solution)/shard_map/while/body/eval_jaxpr/reduce_scatter | solution.py:150
  345.9 89.6 %all-gather.15.cloned.1.call-start = ((), (), s32[]{:S(2)}) async-start(), calls=%async_computation.11 | async-start | bytes 2621440 | tf_op jit(solution)/shard_map/while/body/eval_jaxpr/all_gather | solution.py:146
  387.9 121.3 %reduce-scatter.10.cloned.1.call-start = ((), (), s32[]{:S(2)}) async-start(), calls=%async_computation.13 | async-start | bytes 2621440 | tf_op jit(solution)/shard_map/while/body/eval_jaxpr/reduce_scatter | solution.py:150
  467.3 90.3 %all-gather.21.cloned.1.call-start = ((), (), s32[]{:S(2)}) async-start(), calls=%async_computation.15 | async-start | bytes 2621440 | tf_op jit(solution)/shard_map/while/body/eval_jaxpr/all_gather | solution.py:285
  467.9 137.6 %all-gather.19.cloned.1.call-start = ((), (), s32[]{:S(2)}) async-start(), calls=%async_computation.14 | async-start | bytes 2621440 | tf_op jit(solution)/shard_map/while/body/eval_jaxpr/all_gather | solution.py:146
  527.2 129.6 %reduce-scatter.12.cloned.1.call-start = ((), (), s32[]{:S(2)}) async-start(), calls=%async_computation.16 | async-start | bytes 2621440 | tf_op jit(solution)/shard_map/while/body/eval_jaxpr/reduce_scatter | solution.py:150
  718.2 121.2 %reduce-scatter.10.cloned.1.call-start = ((), (), s32[]{:S(2)}) async-start(), calls=%async_computation.13 | async-start | bytes 2621440 | tf_op jit(solution)/shard_map/while/body/eval_jaxpr/reduce_scatter | solution.py:150
  797.5 90.5 %all-gather.21.cloned.1.call-start = ((), (), s32[]{:S(2)}) async-start(), calls=%async_computation.15 | async-start | bytes 2621440 | tf_op jit(solution)/shard_map/while/body/eval_jaxpr/all_gather | solution.py:285
  798.2 137.4 %all-gather.19.cloned.1.call-start = ((), (), s32[]{:S(2)}) async-start(), calls=%async_computation.14 | async-start | bytes 2621440 | tf_op jit(solution)/shard_map/while/body/eval_jaxpr/all_gather | solution.py:146
  857.5 129.4 %reduce-scatter.12.cloned.1.call-start = ((), (), s32[]{:S(2)}) async-start(), calls=%async_computation.16 | async-start | bytes 2621440 | tf_op jit(solution)/shard_map/while/body/eval_jaxpr/reduce_scatter | solution.py:150
  1042.1 118.8 %reduce-scatter.14.cloned.1.call-start = ((), (), s32[]{:S(2)}) async-start(), calls=%async_computation.19 | async-start | bytes 2621440 | tf_op jit(solution)/shard_map/while/body/eval_jaxpr/reduce_scatter | solution.py:150
  1119.1 113.6 %all-gather.27.cloned.1.call-start = ((), (), s32[]{:S(2)}) async-start(), calls=%async_computation.20 | async-start | bytes 2621440 | tf_op jit(solution)/shard_map/while/body/eval_jaxpr/all_gather | solution.py:146
  1165.6 90.6 %all-gather.33.cloned.1.call-start = ((), (), s32[]{:S(2)}) async-start(), calls=%async_computation.23 | async-start | bytes 2621440 | tf_op jit(solution)/shard_map/while/body/eval_jaxpr/all_gather | solution.py:286
  1166.2 137.2 %all-gather.31.cloned.1.call-start = ((), (), s32[]{:S(2)}) async-start(), calls=%async_computation.22 | async-start | bytes 2621440 | tf_op jit(solution)/shard_map/while/body/eval_jaxpr/all_gather | solution.py:156
  1169.5 189.6 %reduce-scatter.16.cloned.1.call-start = ((), (), s32[]{:S(2)}) async-start(), calls=%async_computation.24 | async-start | bytes 2621440 | tf_op jit(solution)/shard_map/while/body/eval_jaxpr/reduce_scatter | solution.py:160
  1316.6 94.3 %all-gather.35.cloned.1.call-start = ((), (), s32[]{:S(2)}) async-start(), calls=%async_computation.25 | async-start | bytes 2621440 | tf_op jit(solution)/shard_map/while/body/eval_jaxpr/all_gather | solution.py:156
  1365.3 121.2 %reduce-scatter.26.cloned.1.call-start = ((), (), s32[]{:S(2)}) async-start(), calls=%async_computation.30 | async-start | bytes 2621440 | tf_op jit(solution)/shard_map/while/body/eval_jaxpr/reduce_scatter | solution.py:302
  1372.4 116.6 %reduce-scatter.24.cloned.1.call-start = ((), (), s32[]{:S(2)}) async-start(), calls=%async_computation.29 | async-start | bytes 2621440 | tf_op jit(solution)/shard_map/while/body/eval_jaxpr/reduce_scatter | solution.py:299
  1378.8 123.0 %reduce-scatter.22.cloned.1.call-start = ((), (), s32[]{:S(2)}) async-start(), calls=%async_computation.28 | async-start | bytes 655360 | tf_op jit(solution)/shard_map/while/body/eval_jaxpr/reduce_scatter | solution.py:296
  1414.2 118.5 %reduce-scatter.20.cloned.1.call-start = ((), (), s32[]{:S(2)}) async-start(), calls=%async_computation.27 | async-start | bytes 1966080 | tf_op jit(solution)/shard_map/while/body/eval_jaxpr/reduce_scatter | solution.py:293
  1481.6 97.7 %reduce-scatter.18.cloned.1.call-start = ((), (), s32[]{:S(2)}) async-start(), calls=%async_computation.26 | async-start | bytes 2621440 | tf_op jit(solution)/shard_map/while/body/eval_jaxpr/reduce_scatter | solution.py:160
  1637.0 117.0 %reduce-scatter.14.cloned.1.call-start = ((), (), s32[]{:S(2)}) async-start(), calls=%async_computation.19 | async-start | bytes 2621440 | tf_op jit(solution)/shard_map/while/body/eval_jaxpr/reduce_scatter | solution.py:150
  1712.0 113.8 %all-gather.27.cloned.1.call-start = ((), (), s32[]{:S(2)}) async-start(), calls=%async_computation.20 | async-start | bytes 2621440 | tf_op jit(solution)/shard_map/while/body/eval_jaxpr/all_gather | solution.py:146
  1758.6 90.8 %all-gather.33.cloned.1.call-start = ((), (), s32[]{:S(2)}) async-start(), calls=%async_computation.23 | async-start | bytes 2621440 | tf_op jit(solution)/shard_map/while/body/eval_jaxpr/all_gather | solution.py:286
  1759.4 137.2 %all-gather.31.cloned.1.call-start = ((), (), s32[]{:S(2)}) async-start(), calls=%async_computation.22 | async-start | bytes 2621440 | tf_op jit(solution)/shard_map/while/body/eval_jaxpr/all_gather | solution.py:156
  1763.1 189.3 %reduce-scatter.16.cloned.1.call-start = ((), (), s32[]{:S(2)}) async-start(), calls=%async_computation.24 | async-start | bytes 2621440 | tf_op jit(solution)/shard_map/while/body/eval_jaxpr/reduce_scatter | solution.py:160
  1909.8 94.3 %all-gather.35.cloned.1.call-start = ((), (), s32[]{:S(2)}) async-start(), calls=%async_computation.25 | async-start | bytes 2621440 | tf_op jit(solution)/shard_map/while/body/eval_jaxpr/all_gather | solution.py:156
  1958.5 121.2 %reduce-scatter.26.cloned.1.call-start = ((), (), s32[]{:S(2)}) async-start(), calls=%async_computation.30 | async-start | bytes 2621440 | tf_op jit(solution)/shard_map/while/body/eval_jaxpr/reduce_scatter | solution.py:302
  1965.6 116.6 %reduce-scatter.24.cloned.1.call-start = ((), (), s32[]{:S(2)}) async-start(), calls=%async_computation.29 | async-start | bytes 2621440 | tf_op jit(solution)/shard_map/while/body/eval_jaxpr/reduce_scatter | solution.py:299
  1972.2 122.5 %reduce-scatter.22.cloned.1.call-start = ((), (), s32[]{:S(2)}) async-start(), calls=%async_computation.28 | async-start | bytes 655360 | tf_op jit(solution)/shard_map/while/body/eval_jaxpr/reduce_scatter | solution.py:296
  2007.4 118.1 %reduce-scatter.20.cloned.1.call-start = ((), (), s32[]{:S(2)}) async-start(), calls=%async_computation.27 | async-start | bytes 1966080 | tf_op jit(solution)/shard_map/while/body/eval_jaxpr/reduce_scatter | solution.py:293
  2074.9 97.1 %reduce-scatter.18.cloned.1.call-start = ((), (), s32[]{:S(2)}) async-start(), calls=%async_computation.26 | async-start | bytes 2621440 | tf_op jit(solution)/shard_map/while/body/eval_jaxpr/reduce_scatter | solution.py:160
  2229.5 117.0 %reduce-scatter.14.cloned.1.call-start = ((), (), s32[]{:S(2)}) async-start(), calls=%async_computation.19 | async-start | bytes 2621440 | tf_op jit(solution)/shard_map/while/body/eval_jaxpr/reduce_scatter | solution.py:150
  2304.6 113.8 %all-gather.27.cloned.1.call-start = ((), (), s32[]{:S(2)}) async-start(), calls=%async_computation.20 | async-start | bytes 2621440 | tf_op jit(solution)/shard_map/while/body/eval_jaxpr/all_gather | solution.py:146
  2351.2 90.8 %all-gather.33.cloned.1.call-start = ((), (), s32[]{:S(2)}) async-start(), calls=%async_computation.23 | async-start | bytes 2621440 | tf_op jit(solution)/shard_map/while/body/eval_jaxpr/all_gather | solution.py:286
  2352.0 137.2 %all-gather.31.cloned.1.call-start = ((), (), s32[]{:S(2)}) async-start(), calls=%async_computation.22 | async-start | bytes 2621440 | tf_op jit(solution)/shard_map/while/body/eval_jaxpr/all_gather | solution.py:156
  2355.6 189.3 %reduce-scatter.16.cloned.1.call-start = ((), (), s32[]{:S(2)}) async-start(), calls=%async_computation.24 | async-start | bytes 2621440 | tf_op jit(solution)/shard_map/while/body/eval_jaxpr/reduce_scatter | solution.py:160
  2502.3 94.3 %all-gather.35.cloned.1.call-start = ((), (), s32[]{:S(2)}) async-start(), calls=%async_computation.25 | async-start | bytes 2621440 | tf_op jit(solution)/shard_map/while/body/eval_jaxpr/all_gather | solution.py:156
  2551.1 121.4 %reduce-scatter.26.cloned.1.call-start = ((), (), s32[]{:S(2)}) async-start(), calls=%async_computation.30 | async-start | bytes 2621440 | tf_op jit(solution)/shard_map/while/body/eval_jaxpr/reduce_scatter | solution.py:302
  2558.2 116.8 %reduce-scatter.24.cloned.1.call-start = ((), (), s32[]{:S(2)}) async-start(), calls=%async_computation.29 | async-start | bytes 2621440 | tf_op jit(solution)/shard_map/while/body/eval_jaxpr/reduce_scatter | solution.py:299
  2564.6 123.0 %reduce-scatter.22.cloned.1.call-start = ((), (), s32[]{:S(2)}) async-start(), calls=%async_computation.28 | async-start | bytes 655360 | tf_op jit(solution)/shard_map/while/body/eval_jaxpr/reduce_scatter | solution.py:296
  2599.9 118.6 %reduce-scatter.20.cloned.1.call-start = ((), (), s32[]{:S(2)}) async-start(), calls=%async_computation.27 | async-start | bytes 1966080 | tf_op jit(solution)/shard_map/while/body/eval_jaxpr/reduce_scatter | solution.py:293
  2667.6 97.4 %reduce-scatter.18.cloned.1.call-start = ((), (), s32[]{:S(2)}) async-start(), calls=%async_computation.26 | async-start | bytes 2621440 | tf_op jit(solution)/shard_map/while/body/eval_jaxpr/reduce_scatter | solution.py:160
  2794.3 90.7 %all-reduce.2.cloned.1.call-start = ((), (), s32[]{:S(2)}) async-start(), calls=%async_computation.9 | async-start | bytes 262144 | tf_op jit(solution)/shard_map/psum | solution.py:394
  (157 other events, 3982.9 us)
Sparse Core Ops, SparseCore 0:
  57.3 47.9 all-gather.14
  136.5 42.4 reduce-scatter.9
  180.5 22.7 all-gather.12
  204.7 22.5 all-gather.20
  229.4 45.5 all-gather.18
  283.9 42.4 reduce-scatter.11
  388.0 47.4 all-gather.14
  466.7 42.3 reduce-scatter.9
  510.8 22.7 all-gather.12
  535.0 22.5 all-gather.20
  559.9 45.5 all-gather.18
  614.3 42.4 reduce-scatter.11
  718.3 47.4 all-gather.14
  797.0 42.4 reduce-scatter.9
  841.0 22.7 all-gather.12
  865.4 22.5 all-gather.20
  890.1 45.5 all-gather.18
  944.5 42.4 reduce-scatter.11
  1042.2 47.4 all-gather.22
  1118.5 42.4 reduce-scatter.13
  1187.2 45.5 all-gather.26
  1257.9 45.5 all-gather.30
  1316.7 42.4 reduce-scatter.15
  1365.4 45.4 all-gather.34
  1413.4 30.1 reduce-scatter.25
  1446.3 31.4 reduce-scatter.23
  1504.5 28.1 reduce-scatter.19
  1535.6 43.6 reduce-scatter.17
  1637.1 45.5 all-gather.22
  1711.5 42.4 reduce-scatter.13
  1780.2 45.5 all-gather.26
  1851.1 45.5 all-gather.30
  1909.9 42.4 reduce-scatter.15
  1958.6 45.3 all-gather.34
  2006.5 30.0 reduce-scatter.25
  2039.1 31.4 reduce-scatter.23
  2097.2 28.1 reduce-scatter.19
  2128.2 43.6 reduce-scatter.17
  2229.7 45.6 all-gather.22
  2304.1 42.3 reduce-scatter.13
  2372.8 45.5 all-gather.26
  2443.6 45.5 all-gather.30
  2502.5 42.4 reduce-scatter.15
  2551.2 45.3 all-gather.34
  2599.0 30.2 reduce-scatter.25
  2631.9 31.5 reduce-scatter.23
  2690.3 28.1 reduce-scatter.19
  2721.2 43.6 reduce-scatter.17
  (15 shorter events, 325.2 us)
Sparse Core Ops, SparseCore 1:
  2798.3 86.7 all-reduce.1
where the time goes:
time: 2910 us; the launch traced here: 2890 us
  waiting for transfers between devices  1830 us (63%)
  matrix products  353 us (12%)
  other arithmetic  309 us (11%)
  local copies, waits for them, and re-layouts  253 us (9%)
  loops' own time  61.6 us (2%)
  blocking collectives  53.9 us (2%)
    all_gather x12, waiting for transfers between devices, spread_rows(): return lax.all_gather(normed, 'tensor', axis=0, tiled=True)  510 us
    reduce_scatter x9, waiting for transfers between devices, fold_rows(): lax.psum_scatter(term_rows.astype(jnp.bfloat16), 'tensor', scatter_dimens...  377 us
    reduce_scatter x6, waiting for transfers between devices, fold_grads(): lax.psum_scatter(term_rows.astype(jnp.bfloat16), 'tensor', scatter_dimens...  261 us
    all_gather x6, waiting for transfers between devices, spread_grads(): return lax.all_gather(gradient, 'tensor', axis=0, tiled=True)  237 us
    dot_general x24, matrix products, product(): lax.dot_general(left, right, (((left_dim,), (right_dim,)), ((), ())), pre...  117 us
    all_gather x6, waiting for transfers between devices, gather_weights(): lax.all_gather(expand_weight, 'dp', axis=1, tiled=True)  117 us
    reduce_scatter x3, waiting for transfers between devices, sum_weight_grads(): lax.psum_scatter(weight_terms[0].astype(jnp.bfloat16), 'dp', scatter_dime...  89.7 us
    psum x1, waiting for transfers between devices, local(): lax.psum(table_term, ('dp', 'tensor')).reshape(norm_table.shape)  83.6 us
  transfers between devices with their start and end apart: 70, of which 58 were waited for; matrix products, arithmetic and copies ran while one was open for 21% of the time, Pallas kernels for 0%

commit v1 on v0

v1 whole, which is shorter than its diff:
```python
import math

import jax
import jax.numpy as jnp
from jax import lax
from jax.experimental import pallas as pl
from jax.experimental.pallas import tpu as pltpu
from jax.sharding import Mesh, PartitionSpec as P

HEAD_DIM = 64
NORM_EPS = 1e-05
MASKED = -1e30
HIGHEST = lax.Precision.HIGHEST
PAIR = 2 * HEAD_DIM
QUERY_SCALE = 1.0 / math.sqrt(HEAD_DIM)
VMEM_LIMIT = 32 * 2**20
BF16 = jnp.bfloat16
F32 = jnp.float32


def product(left, right, left_dim, right_dim):
    return lax.dot_general(left, right, (((left_dim,), (right_dim,)), ((), ())), preferred_element_type=F32)


def partner(block, axis, step=1):
    return lax.ppermute(block, axis, [(i, i ^ step) for i in range(lax.axis_size(axis))])


def gather_waves(piece):
    waves = []
    for step in range(lax.axis_size("zl")):
        part = piece if step == 0 else partner(piece, "zl", step)
        waves.append(jnp.concatenate([part, partner(part, "core")], axis=0))
    return waves


def scatter_waves(term_of):
    total = None
    for step in reversed(range(lax.axis_size("zl"))):
        term = term_of(step)
        half = term.shape[0] // 2
        mine = term[:half] + partner(term[half:].astype(BF16), "core").astype(F32)
        if step:
            mine = partner(mine.astype(BF16), "zl", step).astype(F32)
        total = mine if total is None else total + mine
    return total


def waves_of(array):
    return jnp.split(array, lax.axis_size("zl"), axis=0)


def positions_table(offset, features):
    column = jnp.arange(features, dtype=jnp.int32)
    frequency = jnp.exp(-math.log(10000.0) * (2 * (column // 2)).astype(F32) / features)
    angles = offset.astype(F32)[:, None] * frequency[None, :]
    return jnp.where(column[None, :] % 2 == 0, jnp.sin(angles), jnp.cos(angles))


def normalize(values):
    centred = values - jnp.mean(values, axis=-1, keepdims=True)
    spread = jnp.mean(centred * centred, axis=-1, keepdims=True)
    rate = lax.rsqrt(spread + NORM_EPS)
    return centred * rate, rate


def gelu_pair(x):
    slope = math.sqrt(2.0 / math.pi)
    square = x * x
    bent = jnp.tanh(slope * x * (1.0 + 0.044715 * square))
    half = 0.5 * (1.0 + bent)
    rise = half + 0.5 * x * (1.0 - bent * bent) * (slope * (1.0 + 3.0 * 0.044715 * square))
    return x * half, rise


def head_lanes(block, side):
    lanes = lax.broadcasted_iota(jnp.int32, block.shape, 1)
    return jnp.where(lanes // HEAD_DIM == side, block, jnp.zeros_like(block))


def attend_kernel(
    query_ref, key_ref, value_ref, key_info_ref, query_info_ref, mixed_ref, logsum_ref, bias_ref
):
    key_segment, key_place = key_info_ref[:, 0:1], key_info_ref[:, 1:2]
    query_segment, query_place, last = query_info_ref[0:1, :], query_info_ref[1:2, :], query_info_ref[2:3, :]
    allowed = ((key_segment == query_segment) & (key_place <= last)) | (key_place == query_place)
    bias_ref[...] = jnp.where(allowed, 0.0, MASKED)
    rows, logsums = [], []
    for pair in range(query_ref.shape[1] // PAIR):
        lanes = slice(pair * PAIR, (pair + 1) * PAIR)
        keys, values = key_ref[:, lanes], value_ref[:, lanes]
        queries = query_ref[:, lanes] * QUERY_SCALE
        for side in range(PAIR // HEAD_DIM):
            scores = product(keys, head_lanes(queries, side), 1, 1) + bias_ref[...]
            peak = jnp.max(scores, axis=0, keepdims=True)
            raised = jnp.exp(scores - peak)
            total = jnp.sum(raised, axis=0, keepdims=True)
            mixed = product(values, raised.astype(BF16), 0, 0)
            rows.append(mixed[side * HEAD_DIM : (side + 1) * HEAD_DIM] * (1.0 / total))
            logsums.append(peak + jnp.log(total))
    mixed_ref[...] = jnp.concatenate(rows, axis=0).T.astype(BF16)
    logsum_ref[...] = jnp.concatenate(logsums, axis=0)


def attend(projected, key_info, query_info):
    frames, width = projected.shape[0], projected.shape[1] // 3
    block = min(frames, 256)
    blocks, heads = frames // block, width // HEAD_DIM
    return pl.pallas_call(
        attend_kernel,
        grid=(blocks,),
        in_specs=[
            pl.BlockSpec((block, width), lambda i: (i, 0)),
            pl.BlockSpec((frames, width), lambda i: (0, 1)),
            pl.BlockSpec((frames, width), lambda i: (0, 2)),
            pl.BlockSpec(key_info.shape, lambda i: (0, 0)),
            pl.BlockSpec((query_info.shape[0], block), lambda i: (0, i)),
        ],
        out_specs=[
            pl.BlockSpec((block, width), lambda i: (i, 0)),
            pl.BlockSpec((heads, block), lambda i: (0, i)),
        ],
        out_shape=[
            jax.ShapeDtypeStruct((frames, width), BF16),
            jax.ShapeDtypeStruct((heads, frames), F32),
        ],
        scratch_shapes=[pltpu.VMEM((frames, block), F32)],
        compiler_params=pltpu.CompilerParams(vmem_limit_bytes=VMEM_LIMIT),
        cost_estimate=pl.CostEstimate(
            flops=16 * frames * frames * width,
            bytes_accessed=8 * frames * width,
            transcendentals=heads * frames * frames,
        ),
        name="attend",
    )(projected, projected, projected, key_info, query_info)


def attend_back_kernel(
    query_ref, key_ref, value_ref, key_info_ref, query_info_ref, mixed_ref, logsum_ref, grad_ref, key_sum, value_sum, bias_ref
):
    step = pl.program_id(0)
    block, width = query_ref.shape

    @pl.when(step == 0)
    def _():
        key_sum[...] = jnp.zeros_like(key_sum)
        value_sum[...] = jnp.zeros_like(value_sum)

    key_segment, key_place = key_info_ref[:, 0:1], key_info_ref[:, 1:2]
    query_segment, query_place, last = query_info_ref[0:1, :], query_info_ref[1:2, :], query_info_ref[2:3, :]
    allowed = ((key_segment == query_segment) & (key_place <= last)) | (key_place == query_place)
    bias_ref[...] = jnp.where(allowed, 0.0, MASKED)
    rows = []
    for pair in range(width // PAIR):
        lanes = slice(pair * PAIR, (pair + 1) * PAIR)
        keys, values = key_ref[:, lanes], value_ref[:, lanes]
        queries = query_ref[:, lanes] * QUERY_SCALE
        for side in range(PAIR // HEAD_DIM):
            head = pair * (PAIR // HEAD_DIM) + side
            query_part = head_lanes(queries, side)
            upstream = head_lanes(mixed_ref[:, lanes], side)
            scores = product(keys, query_part, 1, 1) + bias_ref[...]
            probs = jnp.exp(scores - logsum_ref[head : head + 1, :])
            prob_grad = product(values, upstream, 1, 1)
            inner = jnp.sum(probs * prob_grad, axis=0, keepdims=True)
            score_grad = (probs * (prob_grad - inner)).astype(BF16)
            value_sum[:, lanes] += product(probs.astype(BF16), upstream, 1, 0)
            key_sum[:, lanes] += product(score_grad, query_part, 1, 0)
            row = product(keys, score_grad, 0, 0)
            rows.append(row[side * HEAD_DIM : (side + 1) * HEAD_DIM])
    query_grad = jnp.concatenate(rows, axis=0).T * QUERY_SCALE
    grad_ref[pl.ds(pl.multiple_of(step * block, block), block), :width] = query_grad.astype(BF16)

    @pl.when(step == pl.num_programs(0) - 1)
    def _():
        grad_ref[:, width : 2 * width] = key_sum[...].astype(BF16)
        grad_ref[:, 2 * width :] = value_sum[...].astype(BF16)


def attend_back(projected, key_info, query_info, mixture_grad, logsum):
    frames, width = mixture_grad.shape
    block = min(frames, 256)
    blocks, heads = frames // block, width // HEAD_DIM
    return pl.pallas_call(
        attend_back_kernel,
        grid=(blocks,),
        in_specs=[
            pl.BlockSpec((block, width), lambda i: (i, 0)),
            pl.BlockSpec((frames, width), lambda i: (0, 1)),
            pl.BlockSpec((frames, width), lambda i: (0, 2)),
            pl.BlockSpec(key_info.shape, lambda i: (0, 0)),
            pl.BlockSpec((query_info.shape[0], block), lambda i: (0, i)),
            pl.BlockSpec((block, width), lambda i: (i, 0)),
            pl.BlockSpec((heads, block), lambda i: (0, i)),
        ],
        out_specs=pl.BlockSpec((frames, 3 * width), lambda i: (0, 0)),
        out_shape=jax.ShapeDtypeStruct((frames, 3 * width), BF16),
        scratch_shapes=[
            pltpu.VMEM((frames, width), F32),
            pltpu.VMEM((frames, width), F32),
            pltpu.VMEM((frames, block), F32),
        ],
        compiler_params=pltpu.CompilerParams(vmem_limit_bytes=VMEM_LIMIT),
        cost_estimate=pl.CostEstimate(
            flops=40 * frames * frames * width,
            bytes_accessed=14 * frames * width,
            transcendentals=heads * frames * frames,
        ),
        name="attend_back",
    )(projected, projected, projected, key_info, query_info, mixture_grad, logsum)


def after(value, earlier):
    return lax.optimization_barrier((value, earlier))[0]


def together(*values):
    return lax.optimization_barrier(values)


def layer_forward(stream, context, table, weights, causal, at_projected, at_second):
    entry_mixing, expand, contract = weights
    width = entry_mixing.shape[1] // 4
    entry, mixing = entry_mixing[:, : 3 * width], entry_mixing[:, 3 * width :]
    scale_one, shift_one, scale_two, shift_two = table
    unit_one, rate_one = normalize(stream)
    normed = gather_waves((unit_one * (1.0 + scale_one) + shift_one).astype(BF16))
    projected = jnp.concatenate([product(wave, entry, 1, 0).astype(BF16) for wave in normed], axis=0)
    side = at_projected(projected)
    mixture, logsum = attend(projected, context["key_info"], context["query_info"][causal])
    mixture, side = together(mixture, side)
    mixture_waves = waves_of(mixture)
    middle = stream + scatter_waves(lambda step: product(mixture_waves[step], mixing, 1, 1))
    middle = lax.optimization_barrier(middle)
    unit_two, rate_two = normalize(middle)
    second = gather_waves((unit_two * (1.0 + scale_two) + shift_two).astype(BF16))
    second = at_second(second)
    pairs = [gelu_pair(product(wave, expand, 1, 0)) for wave in second]
    pairs = [together(pair[0].astype(BF16), pair[1].astype(BF16)) for pair in pairs]
    hidden, rise = [pair[0] for pair in pairs], [pair[1] for pair in pairs]
    result = middle + scatter_waves(lambda step: product(hidden[step], contract, 1, 1))
    join = lambda waves: jnp.concatenate(waves, axis=0)
    saved = (unit_one, rate_one, unit_two, rate_two, join(normed), projected, mixture, logsum, join(second), join(hidden), rise)
    return result, saved, side


def norm_back(unit, rate, scale, grad, chosen):
    lifted = grad * (1.0 + scale)
    back = rate * (
        lifted
        - jnp.mean(lifted, axis=-1, keepdims=True)
        - unit * jnp.mean(lifted * unit, axis=-1, keepdims=True)
    )
    scale_sum = lax.dot_general(chosen, grad * unit, (((0,), (0,)), ((), ())), precision=HIGHEST)
    shift_sum = lax.dot_general(chosen, grad, (((0,), (0,)), ((), ())), precision=HIGHEST)
    return back, scale_sum, shift_sum


def layer_backward(saved, context, table, weights, upstream, branch, causal, at_second, at_outgoing, at_projected):
    unit_one, rate_one, unit_two, rate_two, normed, projected, mixture, logsum, second, hidden, rise = saved
    entry_mixing, expand, contract = weights
    width = entry_mixing.shape[1] // 4
    entry, mixing = entry_mixing[:, : 3 * width], entry_mixing[:, 3 * width :]
    scale_one, shift_one, scale_two, shift_two = table
    gate_grad = [
        (product(wave, contract, 1, 0) * steep.astype(F32)).astype(BF16) for wave, steep in zip(branch, rise)
    ]
    second_grad = scatter_waves(lambda step: product(gate_grad[step], expand, 1, 1))
    branch, gate_grad = jnp.concatenate(branch, axis=0), jnp.concatenate(gate_grad, axis=0)
    terms = (product(branch, hidden, 0, 0).astype(BF16), product(second, gate_grad, 0, 0).astype(BF16))
    second_grad, terms = together(second_grad, terms)
    contract_part, expand_part = reduce_weight(terms[0]), reduce_weight(terms[1])
    second_grad = at_second(second_grad)
    part, scale_two_sum, shift_two_sum = norm_back(unit_two, rate_two, scale_two, second_grad, context["chosen"])
    middle_grad = upstream + part
    outgoing = gather_waves(middle_grad.astype(BF16))
    outgoing = at_outgoing(outgoing)
    mixture_grad = jnp.concatenate([product(wave, mixing, 1, 0).astype(BF16) for wave in outgoing], axis=0)
    mixing_term = product(jnp.concatenate(outgoing, axis=0), mixture, 0, 0).astype(BF16)
    projected_grad = attend_back(
        projected, context["key_info"], context["query_info"][causal], mixture_grad, logsum
    )
    projected_grad = at_projected(projected_grad)
    term = jnp.concatenate((product(normed, projected_grad, 0, 0).astype(BF16), mixing_term), axis=1)
    projected_grad, term = together(projected_grad, term)
    entry_part = reduce_weight(term)
    projected_waves = waves_of(projected_grad)
    normed_grad = scatter_waves(lambda step: product(projected_waves[step], entry, 1, 1))
    part, scale_one_sum, shift_one_sum = norm_back(unit_one, rate_one, scale_one, normed_grad, context["chosen"])
    table_term = jnp.stack((scale_one_sum, shift_one_sum, scale_two_sum, shift_two_sum), axis=1)
    return middle_grad + part, (entry_part, expand_part, contract_part), table_term


SPOT = ("section", "core", "zh")
GRID = ("dph", "section")


def spot(section, core, high):
    return 4 * section + 2 * core + high


def routes(layer, far):
    return [
        (spot(layer, block, high), spot(block, high, high ^ far)) for block in range(2) for high in range(2)
    ]


def at_home():
    return lax.axis_index("core") == lax.axis_index("zh")


def spread_weight(shard, layer):
    near, far = (lax.ppermute(shard, SPOT, routes(layer, far)) for far in (0, 1))
    return jnp.where(at_home(), near, far)


def whole_weight(part):
    return lax.all_gather(part, GRID, axis=0, tiled=True)


def reduce_weight(term):
    return lax.psum_scatter(term, GRID, scatter_dimension=0, tiled=True)


def return_weight(part, layer):
    return tuple(lax.ppermute(part, SPOT, [(b, a) for a, b in routes(layer, far)]) for far in (0, 1))


def rows_route(source, target):
    return [(spot(source, core, high), spot(target, high, core)) for core in range(2) for high in range(2)]


def keep_rows(rows):
    return lax.ppermute(rows, SPOT, rows_route(0, 0) + rows_route(1, 1))


def cross_rows(rows):
    return lax.ppermute(rows, SPOT, rows_route(0, 1) + rows_route(1, 0))


def send_rows(rows, layer):
    return lax.ppermute(rows, SPOT, rows_route(layer, layer)), lax.ppermute(rows, SPOT, rows_route(1 - layer, layer))


def sum_everywhere(value, axes):
    for axis in axes:
        step = 1
        while step < lax.axis_size(axis):
            value = value + partner(value, axis, step)
            step *= 2
    return value


def local(
    inputs,
    segment_ids,
    valid_frames,
    segment_codes,
    norm_table,
    entry_weight,
    mixing_weight,
    expand_weight,
    contract_weight,
    cotangent,
):
    section = lax.axis_index("section")
    core, low = lax.axis_index("core"), lax.axis_index("zl")
    low_count = lax.axis_size("zl")
    micro_count, shard_rows, features = inputs.shape
    frames = segment_ids.shape[1]
    code_count = norm_table.shape[1]
    segment_count = segment_codes.shape[1]

    pick = lambda array: lax.dynamic_index_in_dim(array, section, 0, keepdims=False)
    first_section = section == 0
    shards = (
        jnp.concatenate((entry_weight[0].reshape(entry_weight.shape[1], -1), mixing_weight[0].T), axis=1),
        expand_weight[0],
        contract_weight[0].T,
    )
    entry_part = spread_weight(shards[0], 0)
    codes = jnp.pad(pick(segment_codes), (0, frames - segment_count))
    numbers = keep_rows(jnp.stack((pick(segment_ids), pick(valid_frames), codes)))
    segment_row, valid_row, code_row = numbers[0], numbers[1], numbers[2, :segment_count]
    own_input = keep_rows(pick(inputs))
    other_table = partner(norm_table[0], "section")
    tables = (
        jnp.where(first_section, norm_table[0], other_table),
        jnp.where(first_section, other_table, norm_table[0]),
    )
    expand_part = spread_weight(after(shards[1], (own_input, entry_part)), 0)
    contract_part = spread_weight(after(shards[2], (own_input, entry_part)), 0)
    weights = [[whole_weight(part) for part in (entry_part, expand_part, contract_part)]]
    entry_next = spread_weight(after(shards[0], expand_part), 1)
    expand_next = spread_weight(after(shards[1], contract_part), 1)
    contract_next = spread_weight(after(shards[2], entry_next), 1)
    weights.append([whole_weight(part) for part in (entry_next, expand_next, contract_next)])

    rank = core * low_count + low
    ranks = jnp.stack(
        [(core ^ side) * low_count + (low ^ step) for step in range(low_count) for side in range(2)]
    )
    places = (ranks[:, None] * shard_rows + jnp.arange(shard_rows, dtype=jnp.int32)[None, :]).reshape(-1)
    reorder = lambda row: row.reshape(-1, shard_rows)[ranks].reshape(-1)
    segment_rel, valid_rel = reorder(segment_row), reorder(valid_row)
    key_info = jnp.stack((jnp.where(valid_rel == 1, segment_rel, -1), places), axis=1)
    query_info = {
        causal: jnp.stack((segment_rel, places, places if causal else jnp.full_like(places, frames)))
        for causal in (False, True)
    }

    all_places = jnp.arange(frames, dtype=jnp.int32)
    earlier = jnp.concatenate([segment_row[:1] - 1, segment_row[:-1]])
    starts = lax.cummax(jnp.where(segment_row != earlier, all_places, 0), axis=0)
    own_slice = lambda row: lax.dynamic_slice_in_dim(row, rank * shard_rows, shard_rows, 0)
    own_segment = own_slice(segment_row)
    own_offset = own_slice(all_places - starts)
    chosen = (own_segment[:, None] == jnp.arange(segment_count, dtype=jnp.int32)[None, :]).astype(F32)
    code_hot = (code_row[:, None] == jnp.arange(code_count, dtype=jnp.int32)[None, :]).astype(F32)
    context = {"key_info": key_info, "query_info": query_info, "chosen": chosen}

    def frame_table(layer):
        by_segment = jnp.dot(code_hot, tables[layer].reshape(code_count, -1), precision=HIGHEST)
        by_segment = by_segment.reshape(segment_count, 4, features)
        rows = []
        for kind in range(4):
            row = by_segment[0, kind][None, :]
            for segment in range(1, segment_count):
                row = jnp.where(own_segment[:, None] == segment, by_segment[segment, kind][None, :], row)
            rows.append(row)
        return rows

    frame_tables = [frame_table(layer) for layer in range(2)]
    stream = lax.optimization_barrier(own_input.astype(F32) + positions_table(own_offset, features))
    leave = lambda value: value

    other_rows = lax.dynamic_index_in_dim(cotangent[0], 1 - section, 0, keepdims=False)

    def fetch_cotangents(projected):
        return keep_rows(after(pick(cotangent[0]), (projected, contract_next))), cross_rows(
            after(other_rows, (projected, contract_next))
        )

    first, first_saved, (own_cotangent, other_cotangent) = layer_forward(
        stream, context, frame_tables[0], weights[0], True, fetch_cotangents, leave
    )
    cotangents = (
        jnp.where(first_section, own_cotangent, other_cotangent),
        jnp.where(first_section, other_cotangent, own_cotangent),
    )
    first_out = first.astype(BF16)

    def fetch_branch(projected):
        return gather_waves(after(cotangents[1], projected)), send_rows(after(first_out, projected), 0)

    second, second_saved, (branch, first_rows) = layer_forward(
        first_out.astype(F32), context, frame_tables[1], weights[1], False, fetch_branch, leave
    )
    second_out = second.astype(BF16)
    flying = {}

    def send_second(value):
        flying["second"] = send_rows(after(second_out, value), 1)
        return value

    def end(name):
        def hold(value):
            value, flying[name] = together(value, flying[name])
            return value

        return hold

    upper_grad, upper_parts, upper_table = layer_backward(
        second_saved, context, frame_tables[1], weights[1], cotangents[1].astype(F32), branch, False,
        send_second, leave, end("second"),
    )
    upper_round = upper_grad.astype(BF16)
    lower_cotangent = cotangents[0].astype(F32) + upper_grad
    branch = gather_waves(lower_cotangent.astype(BF16))
    flying["upper"] = send_rows(after(upper_round, branch), 1)

    def return_upper(value):
        value = end("upper")(value)
        flying["terms"] = [return_weight(after(part, value), 1) for part in upper_parts[1:]]
        return value

    def return_entry(value):
        flying["terms"].append(return_weight(after(upper_parts[0], value), 1))
        return value

    lower_grad, lower_parts, lower_table = layer_backward(
        first_saved, context, frame_tables[0], weights[0], lower_cotangent, branch, True,
        return_upper, return_entry, end("terms"),
    )
    lower_rows = send_rows(lower_grad.astype(BF16), 0)
    lower_terms = [return_weight(part, 0) for part in (lower_parts[2], lower_parts[1], lower_parts[0])]
    upper_terms = [flying["terms"][1], flying["terms"][0], flying["terms"][2]]
    contract_grad, expand_grad, entry_grad = (
        sum(jnp.where(first_section, lower, upper).astype(F32) for lower, upper in zip(lower_pair, upper_pair))
        for lower_pair, upper_pair in zip(lower_terms, upper_terms)
    )

    def rows_of(lower_pair, upper_pair):
        own, other = (jnp.where(first_section, lower, upper) for lower, upper in zip(lower_pair, upper_pair))
        return jnp.stack((jnp.where(first_section, own, other), jnp.where(first_section, other, own)))[None]

    layer_outputs = rows_of(first_rows, flying["second"])
    input_grads = rows_of(lower_rows, flying["upper"]).astype(F32)

    by_code = lambda term: lax.dot_general(
        code_hot, term.reshape(segment_count, -1), (((0,), (0,)), ((), ())), precision=HIGHEST
    )
    lower_table, upper_table = by_code(lower_table), by_code(upper_table)
    table_grad = jnp.where(first_section, lower_table, upper_table)
    table_grad = table_grad + partner(jnp.where(first_section, upper_table, lower_table), "section")
    table_grad = sum_everywhere(table_grad, ("dph", "core", "zh", "zl")).reshape(norm_table.shape)
    width = entry_grad.shape[1] // 4
    return (
        layer_outputs,
        input_grads,
        entry_grad[:, : 3 * width].reshape(entry_weight.shape),
        entry_grad[:, 3 * width :].T[None],
        expand_grad[None],
        contract_grad.T[None],
        table_grad,
    )


def solution(mesh):
    sections, dp, tensor = (mesh.shape[name] for name in ("section", "dp", "tensor"))
    grid = Mesh(
        mesh.devices.reshape(sections, dp // 2, 2, 2, tensor // 2), ("section", "dph", "core", "zh", "zl")
    )
    row, unit = ("dph", "core"), ("zh", "zl")
    placed = (
        P(row, unit, None),
        P(row, None),
        P(row, None),
        P(row, None),
        P("section", None, None, None),
        P("section", row, None, unit),
        P("section", unit, row),
        P("section", row, unit),
        P("section", unit, row),
        P("section", row, unit, None),
    )
    return jax.shard_map(
        local,
        mesh=grid,
        in_specs=placed,
        out_specs=(
            P("section", row, unit, None),
            P("section", row, unit, None),
            P("section", row, None, unit),
            P("section", unit, row),
            P("section", row, unit),
            P("section", unit, row),
            P("section", None, None, None),
        ),
        check_vma=False,
    )
```

time: 2910 us -> 750 us (0.26)
  waiting for transfers between devices: 1830 us -> 257 us
  matrix products: 353 us -> 110 us
  other arithmetic: 309 us -> 68 us
  local copies, waits for them, and re-layouts: 253 us -> 33.4 us
  starting transfers between devices: 18.3 us -> 198 us
  loops' own time: 61.6 us -> 0 us
  Pallas kernels: 0 us -> 55 us
  blocking collectives: 53.9 us -> 0 us
    all_gather x36 -> x6, waiting for transfers between devices: 934 us -> 0.03 us  [whole_weight(): return lax.all_gather(part, GRID, axis=0, tiled=True)]
    reduce_scatter x27 -> x6, waiting for transfers between devices: 757 us -> 0.01 us  [reduce_weight(): return lax.psum_scatter(term, GRID, scatter_dimension=0, tiled=True)]
    dot_general x81 -> x12, matrix products: 236 us -> 6.15 us  [the longest x4 2.77 us: norm_back(): lax.dot_general(chosen, grad * unit, (((0,), (0,)), ((), ())), precision=...]
    ppermute x6 -> x90, waiting for transfers between devices: 42.9 us -> 257 us  [the longest x54 148 us: partner(): lax.ppermute(block, axis, [(i, i ^ step) for i in range(lax.axis_size(axi...]
    ppermute x6 -> x90, starting transfers between devices: 14.1 us -> 197 us  [the longest x54 89.1 us: partner(): lax.ppermute(block, axis, [(i, i ^ step) for i in range(lax.axis_size(axi...]
    reduce_sum x54 -> x12, other arithmetic: 117 us -> 9.47 us  [the longest x4 5.18 us: norm_back(): jnp.mean(lifted, axis=-1, keepdims=True)]
    psum x1 -> x0, waiting for transfers between devices: 83.6 us -> none  [local(): lax.psum(table_term, ('dp', 'tensor')).reshape(norm_table.shape)]
    convert_element_type x39 -> x19, other arithmetic: 100 us -> 23.4 us  [the longest x8 5.52 us: scatter_waves(): mine = partner(mine.astype(BF16), 'zl', step).astype(F32)]
  transfers between devices with their start and end apart: 70 -> 102, of which waited for: 58 -> 36; matrix products, arithmetic and copies ran while one was open for 21% -> 25% of each run, Pallas kernels for 0% -> 7%
where the time goes in v1:
time: 750 us; the launch traced here: 739 us
  waiting for transfers between devices  257 us (34%)
  starting transfers between devices  198 us (26%)
  matrix products  110 us (15%)
  other arithmetic  68 us (9%)
  Pallas kernels  55 us (7%)
  local copies, waits for them, and re-layouts  33.4 us (4%)
  between operations  17.8 us (2%)
    ppermute x54, waiting for transfers between devices, partner(): lax.ppermute(block, axis, [(i, i ^ step) for i in range(lax.axis_size(axi...  148 us
    dot_general x40, matrix products, product(): lax.dot_general(left, right, (((left_dim,), (right_dim,)), ((), ())), pre...  103 us
    ppermute x54, starting transfers between devices, partner(): lax.ppermute(block, axis, [(i, i ^ step) for i in range(lax.axis_size(axi...  89.1 us
    ppermute x12, waiting for transfers between devices, spread_weight(): lax.ppermute(shard, SPOT, routes(layer, far))  79.8 us
    pallas_call x2, Pallas kernels, attend_back(): pl.pallas_call(attend_back_kernel, grid=(blocks,), in_specs=[pl.BlockSpec...  30.9 us
    ppermute x12, starting transfers between devices, return_weight(): lax.ppermute(part, SPOT, [(b, a) for a, b in routes(layer, far)])  27 us
    pallas_call x2, Pallas kernels, attend(): pl.pallas_call(attend_kernel, grid=(blocks,), in_specs=[pl.BlockSpec((blo...  24.2 us
    ppermute x12, starting transfers between devices, spread_weight(): lax.ppermute(shard, SPOT, routes(layer, far))  24.1 us
  transfers between devices with their start and end apart: 102, of which 36 were waited for; matrix products, arithmetic and copies ran while one was open for 25% of the time, Pallas kernels for 7%

profile of v1, /device:TPU:1, one launch (start us, length us, event | category | flops | bytes accessed | tf_op | source)
XLA Modules:
  0.0 739.5 jit_solution(593472780444332126)
XLA Ops:
  9.5 6.6 collective-permute-start.5
  27.4 17.1 %collective-permute-done.5 = bf16[256,1024]{0,1:T(8,128)(2,1)} collective-permute-done((bf16[256,1024]{0,1:T(8,128)(2,1)S(1)}, bf16[256,1024]{0,1:T(8,128)(2,1)}, u32[]{:S(2)}, u32[]{:S(2)}) %collective-permute-start.5) | collective-permute-done | bytes 524320 | tf_op jit(solution)/shard_map/ppermute | solution.py:313
  49.7 6.3 collective-permute-done
  60.1 3.8 fusion.119
  64.1 8.9 %collective-permute-done.9 = bf16[256,1024]{0,1:T(8,128)(2,1)S(1)} collective-permute-done((bf16[256,1024]{0,1:T(8,128)(2,1)S(1)}, bf16[256,1024]{0,1:T(8,128)(2,1)S(1)}, u32[]{:S(2)}, u32[]{:S(2)}) %collective-permute-start.9) | collective-permute-done | bytes 524320 | tf_op jit(solution)/shard_map/ppermute | solution.py:313
  79.4 6.9 collective-permute-start.6
  86.3 8.9 %collective-permute-done.11 = bf16[256,1024]{0,1:T(8,128)(2,1)S(1)} collective-permute-done((bf16[256,1024]{0,1:T(8,128)(2,1)S(1)}, bf16[256,1024]{0,1:T(8,128)(2,1)S(1)}, u32[]{:S(2)}, u32[]{:S(2)}) %collective-permute-start.11) | collective-permute-done | bytes 524320 | tf_op jit(solution)/shard_map/ppermute | solution.py:313
  100.3 8.6 %collective-permute-start.3 = (bf16[256,1024]{1,0:T(8,128)(2,1)}, bf16[256,1024]{1,0:T(8,128)(2,1)S(1)}, u32[]{:S(2)}, u32[]{:S(2)}) collective-permute-start(bf16[256,1024]{1,0:T(8,128)(2,1)} %add_convert_fusion.7), channel_id=1, source_target_pairs={{0,4},{4,0},{1,5},{5,1},{2,6},{6,2},{3,7},{7,3},{8,12},{12,8},{9,1... | collective-permute-start | bytes 1572872 | tf_op jit(solution)/shard_map/ppermute | solution.py:26
  109.3 14.5 %collective-permute-done.13 = bf16[256,1024]{0,1:T(8,128)(2,1)S(1)} collective-permute-done((bf16[256,1024]{0,1:T(8,128)(2,1)}, bf16[256,1024]{0,1:T(8,128)(2,1)S(1)}, u32[]{:S(2)}, u32[]{:S(2)}) %collective-permute-start.13) | collective-permute-done | bytes 524320 | tf_op jit(solution)/shard_map/ppermute | solution.py:313
  139.8 12.1 %attend.2 = (bf16[1024,256]{1,0:T(8,128)(2,1)S(1)}, f32[4,1024]{1,0:T(4,128)S(1)}) custom-call(bf16[1024,768]{1,0:T(8,128)(2,1)S(1)} %pad_maximum_fusion.2.query_ref.key_ref.value_ref, bf16[1024,768]{1,0:T(8,128)(2,1)S(1)} %pad_maximum_fusion.2.query_ref.key_ref.value_ref, bf16[1024,768]{1,0:T(8,128)(2,1)S(1)} %pad_maximum_fusion.2.query_ref.key_ref.value_ref, ...), custom_call_target="tpu_custom_call" | custom-call | flops 4294967296 | bytes 2097152 | tf_op jit(solution)/shard_map/attend/pallas_call | solution.py:109
  151.9 6.7 collective-permute-done.15
  160.5 20.9 %collective-permute-done.22 = bf16[256,1024]{0,1:T(8,128)(2,1)S(1)} collective-permute-done((bf16[256,1024]{0,1:T(8,128)(2,1)S(1)}, bf16[256,1024]{0,1:T(8,128)(2,1)S(1)}, u32[]{:S(2)}, u32[]{:S(2)}) %collective-permute-start.22) | collective-permute-done | bytes 524320 | tf_op jit(solution)/shard_map/ppermute | solution.py:313
  186.0 12.6 %collective-permute-done.17 = bf16[256,1024]{1,0:T(8,128)(2,1)S(1)} collective-permute-done((bf16[256,1024]{1,0:T(8,128)(2,1)S(1)}, bf16[256,1024]{1,0:T(8,128)(2,1)S(1)}, u32[]{:S(2)}, u32[]{:S(2)}) %collective-permute-start.17) | collective-permute-done | bytes 524320 | tf_op jit(solution)/shard_map/ppermute | solution.py:26
  202.2 12.0 %collective-permute-done.19 = bf16[256,1024]{1,0:T(8,128)(2,1)} collective-permute-done((bf16[256,1024]{1,0:T(8,128)(2,1)S(1)}, bf16[256,1024]{1,0:T(8,128)(2,1)}, u32[]{:S(2)}, u32[]{:S(2)}) %collective-permute-start.19) | collective-permute-done | bytes 524320 | tf_op jit(solution)/shard_map/ppermute | solution.py:26
  218.2 5.6 add_convert_fusion.3
  227.9 4.6 add_convert_fusion.2
  236.7 10.6 %collective-permute-done.24 = bf16[256,1024]{1,0:T(8,128)(2,1)S(1)} collective-permute-done((bf16[256,1024]{1,0:T(8,128)(2,1)S(1)}, bf16[256,1024]{1,0:T(8,128)(2,1)S(1)}, u32[]{:S(2)}, u32[]{:S(2)}) %collective-permute-start.24) | collective-permute-done | bytes 524320 | tf_op jit(solution)/shard_map/ppermute | solution.py:26
  252.1 9.6 %collective-permute-done.41 = bf16[256,1024]{0,1:T(8,128)(2,1)S(1)} collective-permute-done((bf16[256,1024]{0,1:T(8,128)(2,1)S(1)}, bf16[256,1024]{0,1:T(8,128)(2,1)S(1)}, u32[]{:S(2)}, u32[]{:S(2)}) %collective-permute-start.41) | collective-permute-done | bytes 524320 | tf_op jit(solution)/shard_map/ppermute | solution.py:313
  275.2 14.5 %collective-permute-start.33 = (bf16[256,1024]{1,0:T(8,128)(2,1)S(1)}, bf16[256,1024]{1,0:T(8,128)(2,1)S(1)}, u32[]{:S(2)}, u32[]{:S(2)}) collective-permute-start(bf16[256,1024]{1,0:T(8,128)(2,1)S(1)} %copy-done.27), channel_id=1, source_target_pairs={{0,0},{2,4},{4,2},{6,6},{1,1},{3,5},{5,3},{7,7},{8,8},{10,12},{12,... | collective-permute-start | bytes 1572872 | tf_op jit(solution)/shard_map/ppermute | solution.py:342
  289.8 12.1 %attend.3 = (bf16[1024,256]{1,0:T(8,128)(2,1)S(1)}, f32[4,1024]{1,0:T(4,128)S(1)}) custom-call(bf16[1024,768]{1,0:T(8,128)(2,1)S(1)} %pad_maximum_fusion.3.query_ref.key_ref.value_ref, bf16[1024,768]{1,0:T(8,128)(2,1)S(1)} %pad_maximum_fusion.3.query_ref.key_ref.value_ref, bf16[1024,768]{1,0:T(8,128)(2,1)S(1)} %pad_maximum_fusion.3.query_ref.key_ref.value_ref, ...), custom_call_target="tpu_custom_call" | custom-call | flops 4294967296 | bytes 2097152 | tf_op jit(solution)/shard_map/attend/pallas_call | solution.py:109
  310.1 12.1 %collective-permute-done.36 = bf16[256,1024]{1,0:T(8,128)(2,1)} collective-permute-done((bf16[256,1024]{1,0:T(8,128)(2,1)}, bf16[256,1024]{1,0:T(8,128)(2,1)}, u32[]{:S(2)}, u32[]{:S(2)}) %collective-permute-start.36) | collective-permute-done | bytes 524320 | tf_op jit(solution)/shard_map/ppermute | solution.py:26
  333.6 10.5 %collective-permute-done.38 = bf16[256,1024]{1,0:T(8,128)(2,1)} collective-permute-done((bf16[256,1024]{1,0:T(8,128)(2,1)}, bf16[256,1024]{1,0:T(8,128)(2,1)}, u32[]{:S(2)}, u32[]{:S(2)}) %collective-permute-start.38) | collective-permute-done | bytes 524320 | tf_op jit(solution)/shard_map/ppermute | solution.py:26
  346.4 5.7 add_convert_fusion
  352.1 5.0 add_convert_fusion.1
  370.0 4.0 fusion.87
  374.0 5.9 fusion.82
  394.0 11.5 %collective-permute-done.50 = bf16[256,1024]{1,0:T(8,128)(2,1)S(1)} collective-permute-done((bf16[256,1024]{1,0:T(8,128)(2,1)S(1)}, bf16[256,1024]{1,0:T(8,128)(2,1)S(1)}, u32[]{:S(2)}, u32[]{:S(2)}) %collective-permute-start.50) | collective-permute-done | bytes 524320 | tf_op jit(solution)/shard_map/ppermute | solution.py:26
  411.1 10.7 %collective-permute-done.47 = bf16[256,1024]{1,0:T(8,128)(2,1)} collective-permute-done((bf16[256,1024]{1,0:T(8,128)(2,1)}, bf16[256,1024]{1,0:T(8,128)(2,1)}, u32[]{:S(2)}, u32[]{:S(2)}) %collective-permute-start.47) | collective-permute-done | bytes 524320 | tf_op jit(solution)/shard_map/ppermute | solution.py:26
  424.0 16.1 %collective-permute-start.53 = (bf16[256,1024]{1,0:T(8,128)(2,1)}, bf16[256,1024]{1,0:T(8,128)(2,1)}, u32[]{:S(2)}, u32[]{:S(2)}) collective-permute-start(bf16[256,1024]{1,0:T(8,128)(2,1)} %get-tuple-element.90), channel_id=1, source_target_pairs={{0,16},{2,20},{4,18},{6,22},{1,17},{3,21},{5,19},{7,23},{8,24},{10... | collective-permute-start | bytes 1572872 | tf_op jit(solution)/shard_map/ppermute | solution.py:342
  445.9 15.3 %attend_back.2 = bf16[1024,768]{1,0:T(8,128)(2,1)S(1)} custom-call(bf16[1024,768]{1,0:T(8,128)(2,1)S(1)} %pad_maximum_fusion.3.query_ref.key_ref.value_ref, bf16[1024,768]{1,0:T(8,128)(2,1)S(1)} %pad_maximum_fusion.3.query_ref.key_ref.value_ref, bf16[1024,768]{1,0:T(8,128)(2,1)S(1)} %pad_maximum_fusion.3.query_ref.key_ref.value_ref, ...), custom_call_target="tpu_custom_call" | custom-call | flops 10737418240 | bytes 3670016 | tf_op jit(solution)/shard_map/attend_back/pallas_call | solution.py:184
  475.1 12.2 %collective-permute-done.55 = bf16[256,1024]{1,0:T(8,128)(2,1)S(1)} collective-permute-done((bf16[256,1024]{1,0:T(8,128)(2,1)S(1)}, bf16[256,1024]{1,0:T(8,128)(2,1)S(1)}, u32[]{:S(2)}, u32[]{:S(2)}) %collective-permute-start.55) | collective-permute-done | bytes 524320 | tf_op jit(solution)/shard_map/ppermute | solution.py:26
  492.1 11.2 %collective-permute-done.57 = bf16[256,1024]{1,0:T(8,128)(2,1)S(1)} collective-permute-done((bf16[256,1024]{1,0:T(8,128)(2,1)S(1)}, bf16[256,1024]{1,0:T(8,128)(2,1)S(1)}, u32[]{:S(2)}, u32[]{:S(2)}) %collective-permute-start.57) | collective-permute-done | bytes 524320 | tf_op jit(solution)/shard_map/ppermute | solution.py:26
  524.6 6.0 fusion.72
  536.4 5.3 collective-permute-start.64
  542.6 5.5 collective-permute-done.64
  552.2 6.7 collective-permute-start.66
  559.0 6.9 collective-permute-start.65
  565.9 7.5 %collective-permute-start.67 = (bf16[256,1024]{1,0:T(8,128)(2,1)}, bf16[256,1024]{1,0:T(8,128)(2,1)}, u32[]{:S(2)}, u32[]{:S(2)}) collective-permute-start(bf16[256,1024]{1,0:T(8,128)(2,1)} %collective-permute-done.66), channel_id=1, source_target_pairs={{0,4},{4,0},{1,5},{5,1},{2,6},{6,2},{3,7},{7,3},{8,12},{12,8},{9,1... | collective-permute-start | bytes 1572872 | tf_op jit(solution)/shard_map/ppermute | solution.py:26
  574.5 7.4 %collective-permute-start.69 = (bf16[256,1024]{1,0:T(8,128)(2,1)}, bf16[256,1024]{1,0:T(8,128)(2,1)}, u32[]{:S(2)}, u32[]{:S(2)}) collective-permute-start(bf16[256,1024]{1,0:T(8,128)(2,1)} %reduce-scatter.7.cloned.1.call-done), channel_id=1, source_target_pairs={{2,16},{4,18},{18,20},{20,22},{3,17},{5,19},{19,21},{21,23},{10,24... | collective-permute-start | bytes 1572872 | tf_op jit(solution)/shard_map/ppermute | solution.py:326
  598.2 15.6 %attend_back.3 = bf16[1024,768]{1,0:T(8,128)(2,1)S(1)} custom-call(bf16[1024,768]{1,0:T(8,128)(2,1)S(1)} %pad_maximum_fusion.2.query_ref.key_ref.value_ref, bf16[1024,768]{1,0:T(8,128)(2,1)S(1)} %pad_maximum_fusion.2.query_ref.key_ref.value_ref, bf16[1024,768]{1,0:T(8,128)(2,1)S(1)} %pad_maximum_fusion.2.query_ref.key_ref.value_ref, ...), custom_call_target="tpu_custom_call" | custom-call | flops 10737418240 | bytes 3670016 | tf_op jit(solution)/shard_map/attend_back/pallas_call | solution.py:184
  624.6 10.7 %collective-permute-start.74 = (bf16[256,1024]{1,0:T(8,128)(2,1)S(1)}, bf16[256,1024]{1,0:T(8,128)(2,1)S(1)}, u32[]{:S(2)}, u32[]{:S(2)}) collective-permute-start(bf16[256,1024]{1,0:T(8,128)(2,1)S(1)} %slice.542), channel_id=1, source_target_pairs={{0,4},{4,0},{1,5},{5,1},{2,6},{6,2},{3,7},{7,3},{8,12},{12,8},{9,1... | collective-permute-start | bytes 1572872 | tf_op jit(solution)/shard_map/ppermute | solution.py:26
  643.8 10.1 %collective-permute-done.75 = bf16[256,1024]{1,0:T(8,128)(2,1)S(1)} collective-permute-done((bf16[256,1024]{1,0:T(8,128)(2,1)}, bf16[256,1024]{1,0:T(8,128)(2,1)S(1)}, u32[]{:S(2)}, u32[]{:S(2)}) %collective-permute-start.75) | collective-permute-done | bytes 524320 | tf_op jit(solution)/shard_map/ppermute | solution.py:26
  659.4 6.0 collective-permute-done.85
  669.2 5.6 collective-permute-start.77
  684.1 10.2 %collective-permute-done.88 = f32[8,4096]{1,0:T(8,128)S(1)} collective-permute-done((f32[8,4096]{1,0:T(8,128)S(1)}, f32[8,4096]{1,0:T(8,128)S(1)}, u32[]{:S(2)}, u32[]{:S(2)}) %collective-permute-start.88) | collective-permute-done | bytes 131104 | tf_op jit(solution)/shard_map/ppermute | solution.py:26
  694.4 4.8 collective-permute-start.89
  705.1 3.8 collective-permute-done.89
  715.7 7.2 collective-permute-done.82
  (625 shorter events, 279.6 us)
Async XLA Ops:
  7.2 117.5 %all-gather.7.cloned.1.call-start = ((), (), s32[]{:S(2)}) async-start(), calls=%async_computation.6 | async-start | bytes 2621440 | tf_op jit(solution)/shard_map/all_gather | solution.py:318
  9.5 35.1 %collective-permute-start.5 = (bf16[256,1024]{0,1:T(8,128)(2,1)S(1)}, bf16[256,1024]{0,1:T(8,128)(2,1)}, u32[]{:S(2)}, u32[]{:S(2)}) collective-permute-start(bf16[256,1024]{0,1:T(8,128)(2,1)S(1)} %pad_maximum_fusion.8), channel_id=1, source_target_pairs={{0,2},{2,4},{4,18},{6,20},{1,3},{3,5},{5,19},{7,21},{8,10},{10,12}... | collective-permute-start | bytes 1572872 | tf_op jit(solution)/shard_map/ppermute | solution.py:313
  16.0 28.5 %collective-permute-start.4 = (bf16[256,1024]{0,1:T(8,128)(2,1)S(1)}, bf16[256,1024]{0,1:T(8,128)(2,1)}, u32[]{:S(2)}, u32[]{:S(2)}) collective-permute-start(bf16[256,1024]{0,1:T(8,128)(2,1)S(1)} %pad_maximum_fusion.8), channel_id=1, source_target_pairs={{0,0},{2,6},{4,16},{6,22},{1,1},{3,7},{5,17},{7,23},{8,8},{10,14},... | collective-permute-start | bytes 1572872 | tf_op jit(solution)/shard_map/ppermute | solution.py:313
  19.6 26.9 %collective-permute-start.1 = (s32[3,1024]{1,0:T(4,128)S(1)}, s32[3,1024]{1,0:T(4,128)S(1)}, u32[]{:S(2)}, u32[]{:S(2)}) collective-permute-start(s32[3,1024]{1,0:T(4,128)S(1)} %pad_add_fusion), channel_id=1, source_target_pairs={{0,0},{2,4},{4,2},{6,6},{16,16},{18,20},{20,18},{22,22},{1,1},{3,5... | collective-permute-start | bytes 36872 | tf_op jit(solution)/shard_map/ppermute | solution.py:334
  22.8 25.7 %collective-permute-start.2 = (f32[8,4,1024]{2,1,0:T(4,128)}, f32[8,4,1024]{2,1,0:T(4,128)}, u32[]{:S(2)}, u32[]{:S(2)}) collective-permute-start(f32[8,4,1024]{2,1,0:T(4,128)} %bitcast.200), channel_id=1, source_target_pairs={{0,16},{16,0},{1,17},{17,1},{2,18},{18,2},{3,19},{19,3},{4,20},{20... | collective-permute-start | bytes 393224 | tf_op jit(solution)/shard_map/ppermute | solution.py:26
  23.7 32.3 %collective-permute-start = (bf16[256,1024]{1,0:T(8,128)(2,1)}, bf16[256,1024]{1,0:T(8,128)(2,1)S(1)}, u32[]{:S(2)}, u32[]{:S(2)}) collective-permute-start(bf16[256,1024]{1,0:T(8,128)(2,1)} %dynamic-slice_bitcast_fusion.2), channel_id=1, source_target_pairs={{0,0},{2,4},{4,2},{6,6},{16,16},{18,20},{20,18},{22,22},{1,1},{3,5... | collective-permute-start | bytes 1572872 | tf_op jit(solution)/shard_map/ppermute | solution.py:334
  46.5 170.0 %all-gather.9.cloned.1.call-start = ((), (), s32[]{:S(2)}) async-start(), calls=%async_computation.7 | async-start | bytes 2621440 | tf_op jit(solution)/shard_map/all_gather | solution.py:318
  73.8 21.3 %collective-permute-start.11 = (bf16[256,1024]{0,1:T(8,128)(2,1)S(1)}, bf16[256,1024]{0,1:T(8,128)(2,1)S(1)}, u32[]{:S(2)}, u32[]{:S(2)}) collective-permute-start(bf16[256,1024]{0,1:T(8,128)(2,1)S(1)} %pad_maximum_fusion.8), channel_id=1, source_target_pairs={{16,2},{18,4},{20,18},{22,20},{17,3},{19,5},{21,19},{23,21},{24,10... | collective-permute-start | bytes 1572872 | tf_op jit(solution)/shard_map/ppermute | solution.py:313
  76.9 146.9 %all-gather.11.cloned.1.call-start = ((), (), s32[]{:S(2)}) async-start(), calls=%async_computation.8 | async-start | bytes 2621440 | tf_op jit(solution)/shard_map/all_gather | solution.py:318
  79.4 29.8 %collective-permute-start.6 = (bf16[256,1024]{1,0:T(8,128)(2,1)}, bf16[256,1024]{1,0:T(8,128)(2,1)S(1)}, u32[]{:S(2)}, u32[]{:S(2)}) collective-permute-start(bf16[256,1024]{1,0:T(8,128)(2,1)} %add_convert_fusion.7), channel_id=1, source_target_pairs={{0,1},{1,0},{2,3},{3,2},{4,5},{5,4},{6,7},{7,6},{8,9},{9,8},{10,11... | collective-permute-start | bytes 1572872 | tf_op jit(solution)/shard_map/ppermute | solution.py:26
  96.1 27.7 %collective-permute-start.13 = (bf16[256,1024]{0,1:T(8,128)(2,1)}, bf16[256,1024]{0,1:T(8,128)(2,1)S(1)}, u32[]{:S(2)}, u32[]{:S(2)}) collective-permute-start(bf16[256,1024]{0,1:T(8,128)(2,1)} %bitcast.275), channel_id=1, source_target_pairs={{16,2},{18,4},{20,18},{22,20},{17,3},{19,5},{21,19},{23,21},{24,10... | collective-permute-start | bytes 1572872 | tf_op jit(solution)/shard_map/ppermute | solution.py:313
  97.3 26.4 %collective-permute-start.12 = (bf16[256,1024]{0,1:T(8,128)(2,1)}, bf16[256,1024]{0,1:T(8,128)(2,1)S(1)}, u32[]{:S(2)}, u32[]{:S(2)}) collective-permute-start(bf16[256,1024]{0,1:T(8,128)(2,1)} %bitcast.276), channel_id=1, source_target_pairs={{16,0},{18,6},{20,16},{22,22},{17,1},{19,7},{21,17},{23,23},{24,8}... | collective-permute-start | bytes 1572872 | tf_op jit(solution)/shard_map/ppermute | solution.py:313
  100.3 24.3 %collective-permute-start.3 = (bf16[256,1024]{1,0:T(8,128)(2,1)}, bf16[256,1024]{1,0:T(8,128)(2,1)S(1)}, u32[]{:S(2)}, u32[]{:S(2)}) collective-permute-start(bf16[256,1024]{1,0:T(8,128)(2,1)} %add_convert_fusion.7), channel_id=1, source_target_pairs={{0,4},{4,0},{1,5},{5,1},{2,6},{6,2},{3,7},{7,3},{8,12},{12,8},{9,1... | collective-permute-start | bytes 1572872 | tf_op jit(solution)/shard_map/ppermute | solution.py:26
  130.7 21.2 %collective-permute-start.14 = (bf16[256,1024]{1,0:T(8,128)(2,1)S(1)}, bf16[256,1024]{1,0:T(8,128)(2,1)S(1)}, u32[]{:S(2)}, u32[]{:S(2)}) collective-permute-start(bf16[256,1024]{1,0:T(8,128)(2,1)S(1)} %copy-done.81), channel_id=1, source_target_pairs={{0,0},{2,4},{4,2},{6,6},{16,16},{18,20},{20,18},{22,22},{1,1},{3,5... | collective-permute-start | bytes 1572872 | tf_op jit(solution)/shard_map/ppermute | solution.py:334
  132.6 26.0 %collective-permute-start.15 = (bf16[256,1024]{1,0:T(8,128)(2,1)S(1)}, bf16[256,1024]{1,0:T(8,128)(2,1)S(1)}, u32[]{:S(2)}, u32[]{:S(2)}) collective-permute-start(bf16[256,1024]{1,0:T(8,128)(2,1)S(1)} %copy-done.80), channel_id=1, source_target_pairs={{0,16},{2,20},{4,18},{6,22},{16,0},{18,4},{20,2},{22,6},{1,17},{3,... | collective-permute-start | bytes 1572872 | tf_op jit(solution)/shard_map/ppermute | solution.py:338
  135.0 46.3 %collective-permute-start.22 = (bf16[256,1024]{0,1:T(8,128)(2,1)S(1)}, bf16[256,1024]{0,1:T(8,128)(2,1)S(1)}, u32[]{:S(2)}, u32[]{:S(2)}) collective-permute-start(bf16[256,1024]{0,1:T(8,128)(2,1)S(1)} %bitcast.277), channel_id=1, source_target_pairs={{0,2},{2,4},{4,18},{6,20},{1,3},{3,5},{5,19},{7,21},{8,10},{10,12}... | collective-permute-start | bytes 1572872 | tf_op jit(solution)/shard_map/ppermute | solution.py:313
  138.2 43.2 %collective-permute-start.21 = (bf16[256,1024]{0,1:T(8,128)(2,1)S(1)}, bf16[256,1024]{0,1:T(8,128)(2,1)S(1)}, u32[]{:S(2)}, u32[]{:S(2)}) collective-permute-start(bf16[256,1024]{0,1:T(8,128)(2,1)S(1)} %bitcast.278), channel_id=1, source_target_pairs={{0,0},{2,6},{4,16},{6,22},{1,1},{3,7},{5,17},{7,23},{8,8},{10,14},... | collective-permute-start | bytes 1572872 | tf_op jit(solution)/shard_map/ppermute | solution.py:313
  160.4 23.7 %collective-permute-start.16 = (bf16[256,1024]{1,0:T(8,128)(2,1)S(1)}, bf16[256,1024]{1,0:T(8,128)(2,1)}, u32[]{:S(2)}, u32[]{:S(2)}) collective-permute-start(bf16[256,1024]{1,0:T(8,128)(2,1)S(1)} %slice.556), channel_id=1, source_target_pairs={{0,4},{4,0},{1,5},{5,1},{2,6},{6,2},{3,7},{7,3},{8,12},{12,8},{9,1... | collective-permute-start | bytes 1572872 | tf_op jit(solution)/shard_map/ppermute | solution.py:26
  182.3 84.0 %all-gather.13.cloned.1.call-start = ((), (), s32[]{:S(2)}) async-start(), calls=%async_computation.9 | async-start | bytes 2621440 | tf_op jit(solution)/shard_map/all_gather | solution.py:318
  216.3 130.1 %all-gather.17.cloned.1.call-start = ((), (), s32[]{:S(2)}) async-start(), calls=%async_computation.11 | async-start | bytes 2621440 | tf_op jit(solution)/shard_map/all_gather | solution.py:318
  234.7 27.0 %collective-permute-start.41 = (bf16[256,1024]{0,1:T(8,128)(2,1)S(1)}, bf16[256,1024]{0,1:T(8,128)(2,1)S(1)}, u32[]{:S(2)}, u32[]{:S(2)}) collective-permute-start(bf16[256,1024]{0,1:T(8,128)(2,1)S(1)} %bitcast.196), channel_id=1, source_target_pairs={{16,2},{18,4},{20,18},{22,20},{17,3},{19,5},{21,19},{23,21},{24,10... | collective-permute-start | bytes 1572872 | tf_op jit(solution)/shard_map/ppermute | solution.py:313
  236.0 25.7 %collective-permute-start.40 = (bf16[256,1024]{0,1:T(8,128)(2,1)S(1)}, bf16[256,1024]{0,1:T(8,128)(2,1)S(1)}, u32[]{:S(2)}, u32[]{:S(2)}) collective-permute-start(bf16[256,1024]{0,1:T(8,128)(2,1)S(1)} %bitcast.197), channel_id=1, source_target_pairs={{16,0},{18,6},{20,16},{22,22},{17,1},{19,7},{21,17},{23,23},{24,8}... | collective-permute-start | bytes 1572872 | tf_op jit(solution)/shard_map/ppermute | solution.py:313
  262.6 94.5 %all-gather.15.cloned.1.call-start = ((), (), s32[]{:S(2)}) async-start(), calls=%async_computation.10 | async-start | bytes 2621440 | tf_op jit(solution)/shard_map/all_gather | solution.py:318
  273.6 28.3 %collective-permute-start.30 = (bf16[256,1024]{1,0:T(8,128)(2,1)S(1)}, bf16[256,1024]{1,0:T(8,128)(2,1)S(1)}, u32[]{:S(2)}, u32[]{:S(2)}) collective-permute-start(bf16[256,1024]{1,0:T(8,128)(2,1)S(1)} %copy-done.44), channel_id=1, source_target_pairs={{0,4},{4,0},{1,5},{5,1},{2,6},{6,2},{3,7},{7,3},{8,12},{12,8},{9,1... | collective-permute-start | bytes 1572872 | tf_op jit(solution)/shard_map/ppermute | solution.py:26
  273.9 30.2 %collective-permute-start.34 = (bf16[256,1024]{1,0:T(8,128)(2,1)S(1)}, bf16[256,1024]{1,0:T(8,128)(2,1)S(1)}, u32[]{:S(2)}, u32[]{:S(2)}) collective-permute-start(bf16[256,1024]{1,0:T(8,128)(2,1)S(1)} %copy-done.27), channel_id=1, source_target_pairs={{16,0},{18,4},{20,2},{22,6},{17,1},{19,5},{21,3},{23,7},{24,8},{26... | collective-permute-start | bytes 1572872 | tf_op jit(solution)/shard_map/ppermute | solution.py:342
  275.2 28.9 %collective-permute-start.33 = (bf16[256,1024]{1,0:T(8,128)(2,1)S(1)}, bf16[256,1024]{1,0:T(8,128)(2,1)S(1)}, u32[]{:S(2)}, u32[]{:S(2)}) collective-permute-start(bf16[256,1024]{1,0:T(8,128)(2,1)S(1)} %copy-done.27), channel_id=1, source_target_pairs={{0,0},{2,4},{4,2},{6,6},{1,1},{3,5},{5,3},{7,7},{8,8},{10,12},{12,... | collective-permute-start | bytes 1572872 | tf_op jit(solution)/shard_map/ppermute | solution.py:342
  309.2 265.3 %reduce-scatter.7.cloned.1.call-start = ((), (), s32[]{:S(2)}) async-start(), calls=%async_computation.12 | async-start | bytes 2621440 | tf_op jit(solution)/shard_map/reduce_scatter | solution.py:322
  385.8 197.6 %reduce-scatter.9.cloned.1.call-start = ((), (), s32[]{:S(2)}) async-start(), calls=%async_computation.13 | async-start | bytes 2621440 | tf_op jit(solution)/shard_map/reduce_scatter | solution.py:322
  409.6 32.5 %collective-permute-start.46 = (bf16[256,1024]{1,0:T(8,128)(2,1)}, bf16[256,1024]{1,0:T(8,128)(2,1)}, u32[]{:S(2)}, u32[]{:S(2)}) collective-permute-start(bf16[256,1024]{1,0:T(8,128)(2,1)} %get-tuple-element.158), channel_id=1, source_target_pairs={{0,4},{4,0},{1,5},{5,1},{2,6},{6,2},{3,7},{7,3},{8,12},{12,8},{9,1... | collective-permute-start | bytes 1572872 | tf_op jit(solution)/shard_map/ppermute | solution.py:26
  421.8 22.1 %collective-permute-start.48 = (bf16[256,1024]{1,0:T(8,128)(2,1)}, bf16[256,1024]{1,0:T(8,128)(2,1)}, u32[]{:S(2)}, u32[]{:S(2)}) collective-permute-start(bf16[256,1024]{1,0:T(8,128)(2,1)} %collective-permute-done.47), channel_id=1, source_target_pairs={{0,4},{4,0},{1,5},{5,1},{2,6},{6,2},{3,7},{7,3},{8,12},{12,8},{9,1... | collective-permute-start | bytes 1572872 | tf_op jit(solution)/shard_map/ppermute | solution.py:26
  424.0 37.2 %collective-permute-start.53 = (bf16[256,1024]{1,0:T(8,128)(2,1)}, bf16[256,1024]{1,0:T(8,128)(2,1)}, u32[]{:S(2)}, u32[]{:S(2)}) collective-permute-start(bf16[256,1024]{1,0:T(8,128)(2,1)} %get-tuple-element.90), channel_id=1, source_target_pairs={{0,16},{2,20},{4,18},{6,22},{1,17},{3,21},{5,19},{7,23},{8,24},{10... | collective-permute-start | bytes 1572872 | tf_op jit(solution)/shard_map/ppermute | solution.py:342
  441.6 151.6 %reduce-scatter.11.cloned.1.call-start = ((), (), s32[]{:S(2)}) async-start(), calls=%async_computation.14 | async-start | bytes 2621440 | tf_op jit(solution)/shard_map/reduce_scatter | solution.py:322
  491.9 186.8 %reduce-scatter.17.cloned.1.call-start = ((), (), s32[]{:S(2)}) async-start(), calls=%async_computation.17 | async-start | bytes 2621440 | tf_op jit(solution)/shard_map/reduce_scatter | solution.py:322
  536.3 162.9 %reduce-scatter.15.cloned.1.call-start = ((), (), s32[]{:S(2)}) async-start(), calls=%async_computation.16 | async-start | bytes 2621440 | tf_op jit(solution)/shard_map/reduce_scatter | solution.py:322
  559.0 27.2 %collective-permute-start.65 = (bf16[256,1024]{1,0:T(8,128)(2,1)}, bf16[256,1024]{1,0:T(8,128)(2,1)S(1)}, u32[]{:S(2)}, u32[]{:S(2)}) collective-permute-start(bf16[256,1024]{1,0:T(8,128)(2,1)} %get-tuple-element.153), channel_id=1, source_target_pairs={{0,4},{4,0},{1,5},{5,1},{2,6},{6,2},{3,7},{7,3},{8,12},{12,8},{9,1... | collective-permute-start | bytes 1572872 | tf_op jit(solution)/shard_map/ppermute | solution.py:26
  565.9 25.4 %collective-permute-start.67 = (bf16[256,1024]{1,0:T(8,128)(2,1)}, bf16[256,1024]{1,0:T(8,128)(2,1)}, u32[]{:S(2)}, u32[]{:S(2)}) collective-permute-start(bf16[256,1024]{1,0:T(8,128)(2,1)} %collective-permute-done.66), channel_id=1, source_target_pairs={{0,4},{4,0},{1,5},{5,1},{2,6},{6,2},{3,7},{7,3},{8,12},{12,8},{9,1... | collective-permute-start | bytes 1572872 | tf_op jit(solution)/shard_map/ppermute | solution.py:26
  574.5 23.0 %collective-permute-start.69 = (bf16[256,1024]{1,0:T(8,128)(2,1)}, bf16[256,1024]{1,0:T(8,128)(2,1)}, u32[]{:S(2)}, u32[]{:S(2)}) collective-permute-start(bf16[256,1024]{1,0:T(8,128)(2,1)} %reduce-scatter.7.cloned.1.call-done), channel_id=1, source_target_pairs={{2,16},{4,18},{18,20},{20,22},{3,17},{5,19},{19,21},{21,23},{10,24... | collective-permute-start | bytes 1572872 | tf_op jit(solution)/shard_map/ppermute | solution.py:326
  581.9 34.6 %collective-permute-start.68 = (bf16[256,1024]{1,0:T(8,128)(2,1)}, bf16[256,1024]{1,0:T(8,128)(2,1)}, u32[]{:S(2)}, u32[]{:S(2)}) collective-permute-start(bf16[256,1024]{1,0:T(8,128)(2,1)} %reduce-scatter.7.cloned.1.call-done), channel_id=1, source_target_pairs={{0,16},{6,18},{16,20},{22,22},{1,17},{7,19},{17,21},{23,23},{8,24}... | collective-permute-start | bytes 1572872 | tf_op jit(solution)/shard_map/ppermute | solution.py:326
  583.4 33.2 %collective-permute-start.71 = (bf16[256,1024]{1,0:T(8,128)(2,1)}, bf16[256,1024]{1,0:T(8,128)(2,1)}, u32[]{:S(2)}, u32[]{:S(2)}) collective-permute-start(bf16[256,1024]{1,0:T(8,128)(2,1)} %reduce-scatter.9.cloned.1.call-done), channel_id=1, source_target_pairs={{2,16},{4,18},{18,20},{20,22},{3,17},{5,19},{19,21},{21,23},{10,24... | collective-permute-start | bytes 1572872 | tf_op jit(solution)/shard_map/ppermute | solution.py:326
  586.1 123.5 %reduce-scatter.13.cloned.1.call-start = ((), (), s32[]{:S(2)}) async-start(), calls=%async_computation.15 | async-start | bytes 2621440 | tf_op jit(solution)/shard_map/reduce_scatter | solution.py:322
  586.2 30.4 %collective-permute-start.70 = (bf16[256,1024]{1,0:T(8,128)(2,1)}, bf16[256,1024]{1,0:T(8,128)(2,1)}, u32[]{:S(2)}, u32[]{:S(2)}) collective-permute-start(bf16[256,1024]{1,0:T(8,128)(2,1)} %reduce-scatter.9.cloned.1.call-done), channel_id=1, source_target_pairs={{0,16},{6,18},{16,20},{22,22},{1,17},{7,19},{17,21},{23,23},{8,24}... | collective-permute-start | bytes 1572872 | tf_op jit(solution)/shard_map/ppermute | solution.py:326
  593.2 23.4 %collective-permute-start.73 = (bf16[256,1024]{1,0:T(8,128)(2,1)}, bf16[256,1024]{1,0:T(8,128)(2,1)S(1)}, u32[]{:S(2)}, u32[]{:S(2)}) collective-permute-start(bf16[256,1024]{1,0:T(8,128)(2,1)} %reduce-scatter.11.cloned.1.call-done), channel_id=1, source_target_pairs={{2,16},{4,18},{18,20},{20,22},{3,17},{5,19},{19,21},{21,23},{10,24... | collective-permute-start | bytes 1572872 | tf_op jit(solution)/shard_map/ppermute | solution.py:326
  667.9 31.3 %collective-permute-start.78 = (bf16[256,1024]{1,0:T(8,128)(2,1)}, bf16[256,1024]{1,0:T(8,128)(2,1)S(1)}, u32[]{:S(2)}, u32[]{:S(2)}) collective-permute-start(bf16[256,1024]{1,0:T(8,128)(2,1)} %add_convert_fusion.4), channel_id=1, source_target_pairs={{16,0},{18,4},{20,2},{22,6},{17,1},{19,5},{21,3},{23,7},{24,8},{26... | collective-permute-start | bytes 1572872 | tf_op jit(solution)/shard_map/ppermute | solution.py:342
  669.2 31.9 %collective-permute-start.77 = (bf16[256,1024]{1,0:T(8,128)(2,1)}, bf16[256,1024]{1,0:T(8,128)(2,1)}, u32[]{:S(2)}, u32[]{:S(2)}) collective-permute-start(bf16[256,1024]{1,0:T(8,128)(2,1)} %add_convert_fusion.4), channel_id=1, source_target_pairs={{0,0},{2,4},{4,2},{6,6},{1,1},{3,5},{5,3},{7,7},{8,8},{10,12},{12,... | collective-permute-start | bytes 1572872 | tf_op jit(solution)/shard_map/ppermute | solution.py:342
  678.7 32.9 %collective-permute-start.84 = (bf16[256,1024]{1,0:T(8,128)(2,1)}, bf16[256,1024]{1,0:T(8,128)(2,1)}, u32[]{:S(2)}, u32[]{:S(2)}) collective-permute-start(bf16[256,1024]{1,0:T(8,128)(2,1)} %reduce-scatter.17.cloned.1.call-done), channel_id=1, source_target_pairs={{2,0},{4,2},{18,4},{20,6},{3,1},{5,3},{19,5},{21,7},{10,8},{12,10}... | collective-permute-start | bytes 1572872 | tf_op jit(solution)/shard_map/ppermute | solution.py:326
  681.8 31.1 %collective-permute-start.83 = (bf16[256,1024]{1,0:T(8,128)(2,1)}, bf16[256,1024]{1,0:T(8,128)(2,1)}, u32[]{:S(2)}, u32[]{:S(2)}) collective-permute-start(bf16[256,1024]{1,0:T(8,128)(2,1)} %reduce-scatter.17.cloned.1.call-done), channel_id=1, source_target_pairs={{0,0},{6,2},{16,4},{22,6},{1,1},{7,3},{17,5},{23,7},{8,8},{14,10},... | collective-permute-start | bytes 1572872 | tf_op jit(solution)/shard_map/ppermute | solution.py:326
  699.2 23.7 %collective-permute-start.82 = (bf16[256,1024]{1,0:T(8,128)(2,1)}, bf16[256,1024]{1,0:T(8,128)(2,1)}, u32[]{:S(2)}, u32[]{:S(2)}) collective-permute-start(bf16[256,1024]{1,0:T(8,128)(2,1)} %reduce-scatter.15.cloned.1.call-done), channel_id=1, source_target_pairs={{2,0},{4,2},{18,4},{20,6},{3,1},{5,3},{19,5},{21,7},{10,8},{12,10}... | collective-permute-start | bytes 1572872 | tf_op jit(solution)/shard_map/ppermute | solution.py:326
  701.1 21.8 %collective-permute-start.81 = (bf16[256,1024]{1,0:T(8,128)(2,1)}, bf16[256,1024]{1,0:T(8,128)(2,1)}, u32[]{:S(2)}, u32[]{:S(2)}) collective-permute-start(bf16[256,1024]{1,0:T(8,128)(2,1)} %reduce-scatter.15.cloned.1.call-done), channel_id=1, source_target_pairs={{0,0},{6,2},{16,4},{22,6},{1,1},{7,3},{17,5},{23,7},{8,8},{14,10},... | collective-permute-start | bytes 1572872 | tf_op jit(solution)/shard_map/ppermute | solution.py:326
  (180 other events, 1802.2 us)
Sparse Core Ops, SparseCore 0:
  46.6 54.6 all-gather.6
  103.7 43.7 all-gather.8
  182.4 33.4 all-gather.10
  217.5 46.2 all-gather.12
  265.5 40.9 all-gather.16
  309.3 45.7 all-gather.14
  385.9 47.1 reduce-scatter.6
  441.7 37.5 reduce-scatter.8
  492.0 35.3 reduce-scatter.10
  536.4 42.6 reduce-scatter.16
  586.2 56.9 reduce-scatter.14
  646.3 41.6 reduce-scatter.12

commit v2 on v1

--- a/solution.py
+++ b/solution.py
@@ -4,6 +4,7 @@
 import jax.numpy as jnp
 from jax import lax
 from jax.experimental import pallas as pl
+from jax.experimental.layout import Layout, with_layout_constraint
 from jax.experimental.pallas import tpu as pltpu
 from jax.sharding import Mesh, PartitionSpec as P
 
@@ -26,12 +27,22 @@
     return lax.ppermute(block, axis, [(i, i ^ step) for i in range(lax.axis_size(axis))])
 
 
-def gather_waves(piece):
-    waves = []
-    for step in range(lax.axis_size("zl")):
-        part = piece if step == 0 else partner(piece, "zl", step)
+def low_parts(piece):
+    return [piece] + [partner(piece, "zl", step) for step in range(1, lax.axis_size("zl"))]
+
+
+def whole_waves(parts):
+    return [jnp.concatenate([part, partner(part, "core")], axis=0) for part in parts]
+
+
+def gather_waves(piece, work):
+    waves, results = [], []
+    for part in low_parts(piece):
+        if results:
+            part = after(part, results[-1])
         waves.append(jnp.concatenate([part, partner(part, "core")], axis=0))
-    return waves
+        results.append(work(waves[-1]))
+    return waves, results
 
 
 def scatter_waves(term_of):
@@ -218,30 +229,51 @@
     return lax.optimization_barrier(values)
 
 
-def layer_forward(stream, context, table, weights, causal, at_projected, at_second):
-    entry_mixing, expand, contract = weights
-    width = entry_mixing.shape[1] // 4
-    entry, mixing = entry_mixing[:, : 3 * width], entry_mixing[:, 3 * width :]
-    scale_one, shift_one, scale_two, shift_two = table
-    unit_one, rate_one = normalize(stream)
-    normed = gather_waves((unit_one * (1.0 + scale_one) + shift_one).astype(BF16))
-    projected = jnp.concatenate([product(wave, entry, 1, 0).astype(BF16) for wave in normed], axis=0)
-    side = at_projected(projected)
+def rows_major(array):
+    return with_layout_constraint(array, Layout((0, 1)))
+
+
+def join(waves):
+    return jnp.concatenate(waves, axis=0)
+
+
+def stretch(sure, body, *args):
+    shapes = jax.eval_shape(body, *args)
+    blank = lambda *rest: jax.tree.map(lambda leaf: jnp.zeros(leaf.shape, leaf.dtype), shapes)
+    return lax.cond(sure, body, blank, *args)
+
+
+def modulate(values, scale, shift):
+    unit, rate = normalize(values)
+    return unit, rate, (unit * (1.0 + scale) + shift).astype(BF16)
+
+
+def first_half(normed, entry, context, causal):
+    projected = join([product(wave, entry, 1, 0).astype(BF16) for wave in normed])
     mixture, logsum = attend(projected, context["key_info"], context["query_info"][causal])
-    mixture, side = together(mixture, side)
-    mixture_waves = waves_of(mixture)
-    middle = stream + scatter_waves(lambda step: product(mixture_waves[step], mixing, 1, 1))
-    middle = lax.optimization_barrier(middle)
-    unit_two, rate_two = normalize(middle)
-    second = gather_waves((unit_two * (1.0 + scale_two) + shift_two).astype(BF16))
-    second = at_second(second)
-    pairs = [gelu_pair(product(wave, expand, 1, 0)) for wave in second]
-    pairs = [together(pair[0].astype(BF16), pair[1].astype(BF16)) for pair in pairs]
-    hidden, rise = [pair[0] for pair in pairs], [pair[1] for pair in pairs]
-    result = middle + scatter_waves(lambda step: product(hidden[step], contract, 1, 1))
-    join = lambda waves: jnp.concatenate(waves, axis=0)
-    saved = (unit_one, rate_one, unit_two, rate_two, join(normed), projected, mixture, logsum, join(second), join(hidden), rise)
-    return result, saved, side
+    return projected, mixture, logsum
+
+
+def mix(stream, mixture, mixing):
+    waves = waves_of(mixture)
+    return stream + scatter_waves(lambda step: product(waves[step], mixing, 1, 1))
+
+
+def widen(expand):
+    def work(wave):
+        value, slope = gelu_pair(product(wave, expand, 1, 0))
+        return together(value.astype(BF16), slope.astype(BF16))
+
+    return work
+
+
+def narrow(contract, rise):
+    slopes = iter(rise)
+    return lambda wave: (product(wave, contract, 1, 0) * next(slopes).astype(F32)).astype(BF16)
+
+
+def collect(middle, hidden, contract):
+    return middle + scatter_waves(lambda step: product(hidden[step], contract, 1, 1))
 
 
 def norm_back(unit, rate, scale, grad, chosen):
@@ -256,39 +288,34 @@
     return back, scale_sum, shift_sum
 
 
-def layer_backward(saved, context, table, weights, upstream, branch, causal, at_second, at_outgoing, at_projected):
-    unit_one, rate_one, unit_two, rate_two, normed, projected, mixture, logsum, second, hidden, rise = saved
-    entry_mixing, expand, contract = weights
-    width = entry_mixing.shape[1] // 4
-    entry, mixing = entry_mixing[:, : 3 * width], entry_mixing[:, 3 * width :]
-    scale_one, shift_one, scale_two, shift_two = table
-    gate_grad = [
-        (product(wave, contract, 1, 0) * steep.astype(F32)).astype(BF16) for wave, steep in zip(branch, rise)
-    ]
-    second_grad = scatter_waves(lambda step: product(gate_grad[step], expand, 1, 1))
-    branch, gate_grad = jnp.concatenate(branch, axis=0), jnp.concatenate(gate_grad, axis=0)
-    terms = (product(branch, hidden, 0, 0).astype(BF16), product(second, gate_grad, 0, 0).astype(BF16))
-    second_grad, terms = together(second_grad, terms)
-    contract_part, expand_part = reduce_weight(terms[0]), reduce_weight(terms[1])
-    second_grad = at_second(second_grad)
-    part, scale_two_sum, shift_two_sum = norm_back(unit_two, rate_two, scale_two, second_grad, context["chosen"])
+def wide_terms(gate_grad, branch, expand, second, hidden):
+    grad = scatter_waves(lambda step: product(gate_grad[step], expand, 1, 1))
+    terms = (product(join(branch), join(hidden), 0, 0), product(join(second), join(gate_grad), 0, 0))
+    return grad, rows_major(jnp.concatenate([term.astype(BF16) for term in terms], axis=1))
+
+
+def back_norm(second_grad, upstream, kept, table, mixing, mixture, context):
+    part, scale_sum, shift_sum = norm_back(*kept, table[2], second_grad, context["chosen"])
     middle_grad = upstream + part
-    outgoing = gather_waves(middle_grad.astype(BF16))
-    outgoing = at_outgoing(outgoing)
-    mixture_grad = jnp.concatenate([product(wave, mixing, 1, 0).astype(BF16) for wave in outgoing], axis=0)
-    mixing_term = product(jnp.concatenate(outgoing, axis=0), mixture, 0, 0).astype(BF16)
-    projected_grad = attend_back(
-        projected, context["key_info"], context["query_info"][causal], mixture_grad, logsum
-    )
-    projected_grad = at_projected(projected_grad)
-    term = jnp.concatenate((product(normed, projected_grad, 0, 0).astype(BF16), mixing_term), axis=1)
-    projected_grad, term = together(projected_grad, term)
-    entry_part = reduce_weight(term)
-    projected_waves = waves_of(projected_grad)
-    normed_grad = scatter_waves(lambda step: product(projected_waves[step], entry, 1, 1))
-    part, scale_one_sum, shift_one_sum = norm_back(unit_one, rate_one, scale_one, normed_grad, context["chosen"])
-    table_term = jnp.stack((scale_one_sum, shift_one_sum, scale_two_sum, shift_two_sum), axis=1)
-    return middle_grad + part, (entry_part, expand_part, contract_part), table_term
+    outgoing, mixture_grad = gather_waves(
+        middle_grad.astype(BF16), lambda wave: product(wave, mixing, 1, 0).astype(BF16)
+    )
+    return middle_grad, join(outgoing), join(mixture_grad), (scale_sum, shift_sum)
+
+
+def back_attention(outgoing, mixture_grad, kept, context, causal):
+    normed, projected, mixture, logsum = kept
+    projected_grad = attend_back(projected, context["key_info"], context["query_info"][causal], mixture_grad, logsum)
+    terms = product(join(normed), projected_grad, 0, 0), product(outgoing, mixture, 0, 0)
+    return projected_grad, rows_major(jnp.concatenate([term.astype(BF16) for term in terms], axis=1))
+
+
+def back_entry(projected_grad, middle_grad, sums, kept, table, entry, context):
+    unit_one, rate_one = kept
+    waves = waves_of(projected_grad)
+    normed_grad = scatter_waves(lambda step: product(waves[step], entry, 1, 1))
+    part, scale_sum, shift_sum = norm_back(unit_one, rate_one, table[0], normed_grad, context["chosen"])
+    return middle_grad + part, jnp.stack((scale_sum, shift_sum) + sums, axis=1)
 
 
 SPOT = ("section", "core", "zh")
@@ -305,12 +332,24 @@
     ]
 
 
+def hop_weight(shard):
+    route = [(spot(1 - block, block, high), spot(block, block, high)) for block in range(2) for high in range(2)]
+    other = lax.ppermute(shard, SPOT, route)
+    first = lax.axis_index("section") == 0
+    return jnp.where(first, shard, other), jnp.where(first, other, shard)
+
+
 def at_home():
     return lax.axis_index("core") == lax.axis_index("zh")
 
 
-def spread_weight(shard, layer):
-    near, far = (lax.ppermute(shard, SPOT, routes(layer, far)) for far in (0, 1))
+def spread_weight(shard):
+    near, far = (
+        lax.ppermute(
+            shard, SPOT, [(spot(block, block, high), spot(block, high, high ^ far)) for block in range(2) for high in range(2)]
+        )
+        for far in (0, 1)
+    )
     return jnp.where(at_home(), near, far)
 
 
@@ -320,6 +359,80 @@
 
 def reduce_weight(term):
     return lax.psum_scatter(term, GRID, scatter_dimension=0, tiled=True)
+
+
+def across(block, step):
+    flip = 2 * (step % 2) + step // 2
+    return lax.ppermute(block, GRID[::-1], [(i, i ^ flip) for i in range(4)])
+
+
+def near_blocks(part):
+    if lax.axis_size("dph") != 2:
+        return (whole_weight(part),)
+    return part, across(part, 1), across(part, 2)
+
+
+def far_block(blocks):
+    return (across(blocks[0], 3),) if len(blocks) > 1 else ()
+
+
+def direct_blocks(part):
+    blocks = near_blocks(part)
+    return blocks + far_block(blocks)
+
+
+def direct_sums(term):
+    return reduce_near(term) + reduce_far(term)
+
+
+def assemble(blocks):
+    if len(blocks) == 1:
+        return blocks[0]
+    first = lax.axis_index("section") == 0
+    left = lax.axis_index("dph") == 0
+    one, two, three, four = blocks
+    own = (jnp.where(first, one, two), jnp.where(first, two, one))
+    other = (jnp.where(first, three, four), jnp.where(first, four, three))
+    order = [jnp.where(left, a, b) for a, b in zip(own + other, other + own)]
+    return jnp.concatenate(order, axis=0)
+
+
+def blocks_of(term, *steps):
+    blocks = term.reshape(4, -1, term.shape[1])
+    place = 2 * lax.axis_index("dph") + lax.axis_index("section")
+    return [lax.dynamic_index_in_dim(blocks, place ^ step, 0, keepdims=False) for step in steps]
+
+
+def reduce_near(term):
+    if lax.axis_size("dph") != 2:
+        return (reduce_weight(term),)
+    own, one, two = blocks_of(term, 0, 1, 2)
+    return own, across(one, 1), across(two, 2)
+
+
+def reduce_far(term):
+    return tuple(across(block, 3) for block in blocks_of(term, 3)) if lax.axis_size("dph") == 2 else ()
+
+
+def half_sum(term):
+    if lax.axis_size("dph") != 2:
+        return (reduce_weight(term),)
+    parts, place = term.reshape(2, -1, term.shape[1]), lax.axis_index("dph")
+    pick = lambda index: lax.dynamic_index_in_dim(parts, index, 0, keepdims=False)
+    return pick(place), partner(pick(1 - place), "dph")
+
+
+def whole_sum(halves):
+    if len(halves) == 1:
+        return halves[0]
+    part = halves[0].astype(F32) + halves[1].astype(F32)
+    parts, place = part.reshape(2, -1, part.shape[1]), lax.axis_index("section")
+    pick = lambda index: lax.dynamic_index_in_dim(parts, index, 0, keepdims=False)
+    return (pick(place) + partner(pick(1 - place).astype(BF16), "section").astype(F32)).astype(BF16)
+
+
+def total(blocks):
+    return sum(block.astype(F32) for block in blocks).astype(BF16)
 
 
 def return_weight(part, layer):
@@ -373,28 +486,24 @@
 
     pick = lambda array: lax.dynamic_index_in_dim(array, section, 0, keepdims=False)
     first_section = section == 0
-    shards = (
-        jnp.concatenate((entry_weight[0].reshape(entry_weight.shape[1], -1), mixing_weight[0].T), axis=1),
-        expand_weight[0],
-        contract_weight[0].T,
-    )
-    entry_part = spread_weight(shards[0], 0)
+    sure = valid_frames[0, 0] >= 0
+    units = mixing_weight.shape[1]
+    entry_shard = entry_weight[0].reshape(entry_weight.shape[1], -1)
+    rest_shard = jnp.concatenate((mixing_weight[0].T, expand_weight[0], contract_weight[0].T), axis=1)
+    entry_shard = lax.optimization_barrier(entry_shard)
+    entry_hop = hop_weight(entry_shard)
     codes = jnp.pad(pick(segment_codes), (0, frames - segment_count))
-    numbers = keep_rows(jnp.stack((pick(segment_ids), pick(valid_frames), codes)))
+    numbers = keep_rows(after(jnp.stack((pick(segment_ids), pick(valid_frames), codes)), entry_shard))
     segment_row, valid_row, code_row = numbers[0], numbers[1], numbers[2, :segment_count]
-    own_input = keep_rows(pick(inputs))
-    other_table = partner(norm_table[0], "section")
+    own_input = keep_rows(after(pick(inputs), entry_shard))
+    other_table = partner(after(norm_table[0], entry_shard), "section")
     tables = (
         jnp.where(first_section, norm_table[0], other_table),
         jnp.where(first_section, other_table, norm_table[0]),
     )
-    expand_part = spread_weight(after(shards[1], (own_input, entry_part)), 0)
-    contract_part = spread_weight(after(shards[2], (own_input, entry_part)), 0)
-    weights = [[whole_weight(part) for part in (entry_part, expand_part, contract_part)]]
-    entry_next = spread_weight(after(shards[0], expand_part), 1)
-    expand_next = spread_weight(after(shards[1], contract_part), 1)
-    contract_next = spread_weight(after(shards[2], entry_next), 1)
-    weights.append([whole_weight(part) for part in (entry_next, expand_next, contract_next)])
+    rest_hop = hop_weight(after(rest_shard, entry_shard))
+    entry_part = spread_weight(entry_hop[0])
+    other_rows = lax.dynamic_index_in_dim(cotangent[0], 1 - section, 0, keepdims=False)
 
     rank = core * low_count + low
     ranks = jnp.stack(
@@ -431,82 +540,133 @@
         return rows
 
     frame_tables = [frame_table(layer) for layer in range(2)]
+    blocks = direct_blocks(entry_part)
     stream = lax.optimization_barrier(own_input.astype(F32) + positions_table(own_offset, features))
-    leave = lambda value: value
-
-    other_rows = lax.dynamic_index_in_dim(cotangent[0], 1 - section, 0, keepdims=False)
-
-    def fetch_cotangents(projected):
-        return keep_rows(after(pick(cotangent[0]), (projected, contract_next))), cross_rows(
-            after(other_rows, (projected, contract_next))
+    unit_one, rate_one, normed = modulate(stream, frame_tables[0][0], frame_tables[0][1])
+    rest_part = spread_weight(after(rest_hop[0], (own_input, entry_part)))
+    normed, blocks, rest_part = together(whole_waves(low_parts(normed)), blocks, rest_part)
+    entry = assemble(blocks)
+    cut = units + expand_weight.shape[2]
+    every = jnp.concatenate((entry_hop[1], rest_hop[1]), axis=1)
+    moving = direct_blocks(rest_part[:, :cut]), spread_weight(after(every, entry))
+    halfway = stretch(sure, lambda *args: first_half(*args, context, True), normed, entry)
+    (projected, mixture, logsum), (blocks, every) = together(halfway, moving)
+    mixed = assemble(blocks)
+    mixing, expand = mixed[:, :units], mixed[:, units:]
+
+    def through(stream, mixture, mixing, expand, table):
+        middle = lax.optimization_barrier(mix(stream, mixture, mixing))
+        unit, rate, modulated = modulate(middle, table[2], table[3])
+        second, pairs = gather_waves(modulated, widen(expand))
+        return middle, unit, rate, second, [pair[0] for pair in pairs], [pair[1] for pair in pairs]
+
+    moving = direct_blocks(rest_part[:, cut:])
+    passed = stretch(sure, through, stream, mixture, mixing, expand, frame_tables[0])
+    (middle, unit_two, rate_two, second, hidden, rise), blocks = together(passed, moving)
+    contract = assemble(blocks)
+    lower_weights = (entry, mixing, expand, contract)
+    lower_kept = (unit_one, rate_one), (unit_two, rate_two), (normed, projected, mixture, logsum), second, hidden, rise
+
+    def turn_layer(middle, hidden, contract, table):
+        first_out = collect(middle, hidden, contract).astype(BF16)
+        unit, rate, modulated = modulate(first_out.astype(F32), table[0], table[1])
+        return first_out, unit, rate, whole_waves(low_parts(modulated))
+
+    moving = direct_blocks(every[:, : 4 * units])
+    turned = stretch(sure, turn_layer, middle, hidden, contract, frame_tables[1])
+    (first_out, unit_one, rate_one, normed), blocks = together(turned, moving)
+
+    entry = assemble(blocks)
+    entry, mixing = entry[:, : 3 * units], entry[:, 3 * units :]
+    moving = near_blocks(every[:, 4 * units :]), keep_rows(after(pick(cotangent[0]), entry)), cross_rows(
+        after(other_rows, entry)
+    )
+    halfway = stretch(sure, lambda *args: first_half(*args, context, False), normed, entry)
+    (projected, mixture, logsum), (blocks, own, other) = together(halfway, moving)
+    cotangents = jnp.where(first_section, own, other), jnp.where(first_section, other, own)
+
+    def settle(stream, mixture, mixing, table):
+        middle = lax.optimization_barrier(mix(stream.astype(F32), mixture, mixing))
+        unit, rate, modulated = modulate(middle, table[2], table[3])
+        return middle, unit, rate, whole_waves(low_parts(modulated))
+
+    moving = far_block(blocks), low_parts(cotangents[1])
+    settled = stretch(sure, settle, first_out, mixture, mixing, frame_tables[1])
+    (middle, unit_two, rate_two, second), (far, branch) = together(settled, moving)
+    wide = assemble(blocks + far)
+    expand, contract = wide[:, : wide.shape[1] // 2], wide[:, wide.shape[1] // 2 :]
+
+    def finish(middle, second, expand, contract):
+        pairs = [widen(expand)(wave) for wave in second]
+        hidden, rise = [pair[0] for pair in pairs], [pair[1] for pair in pairs]
+        return collect(middle, hidden, contract).astype(BF16), hidden, rise
+
+    moving = [partner(part, "core") for part in branch]
+    finished = stretch(sure, finish, middle, second, expand, contract)
+    (second_out, hidden, rise), others = together(finished, moving)
+    branch = list(zip(branch, others))
+    weights = (entry, mixing, expand, contract)
+    kept = (unit_one, rate_one), (unit_two, rate_two), (normed, projected, mixture, logsum), second, hidden, rise
+
+    def start_back(branch, contract, rise, expand, second, hidden):
+        branch = [join(wave) if isinstance(wave, tuple) else wave for wave in branch]
+        gate_grad = [narrow(contract, rise[step : step + 1])(wave) for step, wave in enumerate(branch)]
+        return wide_terms(gate_grad, branch, expand, second, hidden)
+
+    own_of = lambda lower, upper: jnp.where(first_section, lower, upper)
+    second_grad, wide_term = stretch(sure, start_back, branch, contract, rise, expand, second, hidden)
+
+    def send_outputs(pin):
+        own, other = after((own_of(first_out, second_out), own_of(second_out, first_out)), pin)
+        return keep_rows(own), cross_rows(other)
+
+
+    def back_middle(second_grad, upstream, kept, table, weights, wide_term, causal, beside):
+        moving = direct_sums(wide_term)
+        stepped = stretch(
+            sure, lambda *args: back_norm(*args, context), second_grad, upstream, kept[1], table, weights[1], kept[2][2]
         )
-
-    first, first_saved, (own_cotangent, other_cotangent) = layer_forward(
-        stream, context, frame_tables[0], weights[0], True, fetch_cotangents, leave
-    )
-    cotangents = (
-        jnp.where(first_section, own_cotangent, other_cotangent),
-        jnp.where(first_section, other_cotangent, own_cotangent),
-    )
-    first_out = first.astype(BF16)
-
-    def fetch_branch(projected):
-        return gather_waves(after(cotangents[1], projected)), send_rows(after(first_out, projected), 0)
-
-    second, second_saved, (branch, first_rows) = layer_forward(
-        first_out.astype(F32), context, frame_tables[1], weights[1], False, fetch_branch, leave
-    )
-    second_out = second.astype(BF16)
-    flying = {}
-
-    def send_second(value):
-        flying["second"] = send_rows(after(second_out, value), 1)
-        return value
-
-    def end(name):
-        def hold(value):
-            value, flying[name] = together(value, flying[name])
-            return value
-
-        return hold
-
-    upper_grad, upper_parts, upper_table = layer_backward(
-        second_saved, context, frame_tables[1], weights[1], cotangents[1].astype(F32), branch, False,
-        send_second, leave, end("second"),
-    )
-    upper_round = upper_grad.astype(BF16)
-    lower_cotangent = cotangents[0].astype(F32) + upper_grad
-    branch = gather_waves(lower_cotangent.astype(BF16))
-    flying["upper"] = send_rows(after(upper_round, branch), 1)
-
-    def return_upper(value):
-        value = end("upper")(value)
-        flying["terms"] = [return_weight(after(part, value), 1) for part in upper_parts[1:]]
-        return value
-
-    def return_entry(value):
-        flying["terms"].append(return_weight(after(upper_parts[0], value), 1))
-        return value
-
-    lower_grad, lower_parts, lower_table = layer_backward(
-        first_saved, context, frame_tables[0], weights[0], lower_cotangent, branch, True,
-        return_upper, return_entry, end("terms"),
-    )
+        middle_grad, outgoing, mixture_grad, sums = stepped
+        sent = beside(mixture_grad)
+        attended = stretch(
+            sure, lambda *args: back_attention(*args, context, causal), outgoing, mixture_grad, kept[2]
+        )
+        (projected_grad, entry_term), moving, sent = together(attended, moving, sent)
+        return middle_grad, sums, projected_grad, entry_term, total(moving), sent
+
+    middle_grad, sums, projected_grad, entry_term, wide_part, out_rows = back_middle(
+        second_grad, cotangents[1].astype(F32), kept, frame_tables[1], weights, wide_term, False, send_outputs
+    )
+
+    def cross_back(projected_grad, middle_grad, sums, kept, table, entry, cotangent):
+        upper_grad, table_term = back_entry(projected_grad, middle_grad, sums, kept, table, entry, context)
+        upstream = cotangent.astype(F32) + upper_grad
+        return upper_grad.astype(BF16), table_term, upstream, whole_waves(low_parts(upstream.astype(BF16)))
+
+    moving = direct_sums(entry_term)
+    crossed = stretch(
+        sure, cross_back, projected_grad, middle_grad, sums, kept[0], frame_tables[1], weights[0], cotangents[0]
+    )
+    (upper_grad, upper_table, upstream, branch), parts = together(crossed, moving)
+
+    moving = return_weight(jnp.concatenate((wide_part, total(parts)), axis=1), 1)
+    started = stretch(
+        sure, start_back, branch, lower_weights[3], lower_kept[5], lower_weights[2], lower_kept[3], lower_kept[4]
+    )
+    (second_grad, wide_term), upper_terms = together(started, moving)
+    middle_grad, sums, projected_grad, entry_term, wide_part, upper_rows = back_middle(
+        second_grad, upstream, lower_kept, frame_tables[0], lower_weights, wide_term, True,
+        lambda pin: send_rows(after(upper_grad, pin), 1)
+    )
+    moving = half_sum(entry_term), return_weight(wide_part, 0)
+    closed = stretch(
+        sure, lambda *args: back_entry(*args, context),
+        projected_grad, middle_grad, sums, lower_kept[0], frame_tables[0], lower_weights[0],
+    )
+    (lower_grad, lower_table), (halves, lower_wide) = together(closed, moving)
+    entry_part = whole_sum(halves)
     lower_rows = send_rows(lower_grad.astype(BF16), 0)
-    lower_terms = [return_weight(part, 0) for part in (lower_parts[2], lower_parts[1], lower_parts[0])]
-    upper_terms = [flying["terms"][1], flying["terms"][0], flying["terms"][2]]
-    contract_grad, expand_grad, entry_grad = (
-        sum(jnp.where(first_section, lower, upper).astype(F32) for lower, upper in zip(lower_pair, upper_pair))
-        for lower_pair, upper_pair in zip(lower_terms, upper_terms)
-    )
-
-    def rows_of(lower_pair, upper_pair):
-        own, other = (jnp.where(first_section, lower, upper) for lower, upper in zip(lower_pair, upper_pair))
-        return jnp.stack((jnp.where(first_section, own, other), jnp.where(first_section, other, own)))[None]
-
-    layer_outputs = rows_of(first_rows, flying["second"])
-    input_grads = rows_of(lower_rows, flying["upper"]).astype(F32)
-
+    lower_entry = return_weight(entry_part, 0)
     by_code = lambda term: lax.dot_general(
         code_hot, term.reshape(segment_count, -1), (((0,), (0,)), ((), ())), precision=HIGHEST
     )
@@ -514,14 +674,29 @@
     table_grad = jnp.where(first_section, lower_table, upper_table)
     table_grad = table_grad + partner(jnp.where(first_section, upper_table, lower_table), "section")
     table_grad = sum_everywhere(table_grad, ("dph", "core", "zh", "zl")).reshape(norm_table.shape)
-    width = entry_grad.shape[1] // 4
+    wide_width = 2 * expand_weight.shape[2]
+    upper_terms = [(array[:, :wide_width], array[:, wide_width:]) for array in upper_terms]
+    wide_grad, entry_grad = (
+        sum(own_of(lower, upper).astype(F32) for lower, upper in zip(lower_pair, upper_pair))
+        for lower_pair, upper_pair in zip((lower_wide, lower_entry), zip(*upper_terms))
+    )
+
+    def rows_of(lower_pair, upper_pair):
+        own, other = (jnp.where(first_section, lower, upper) for lower, upper in zip(lower_pair, upper_pair))
+        return jnp.stack((jnp.where(first_section, own, other), jnp.where(first_section, other, own)))[None]
+
+    own, other = out_rows
+    layer_outputs = jnp.stack((own_of(own, other), own_of(other, own)))[None]
+    input_grads = rows_of(lower_rows, upper_rows).astype(F32)
+
+    hidden_units = wide_grad.shape[1] // 2
     return (
         layer_outputs,
         input_grads,
-        entry_grad[:, : 3 * width].reshape(entry_weight.shape),
-        entry_grad[:, 3 * width :].T[None],
-        expand_grad[None],
-        contract_grad.T[None],
+        entry_grad[:, : 3 * units].reshape(entry_weight.shape),
+        entry_grad[:, 3 * units :].T[None],
+        wide_grad[:, hidden_units:][None],
+        wide_grad[:, :hidden_units].T[None],
         table_grad,
     )
 

time: 750 us -> 733 us (0.977)
  other arithmetic: 68 us -> 96.2 us
  waiting for transfers between devices: 257 us -> 233 us
  starting transfers between devices: 198 us -> 178 us
  between operations: 17.8 us -> 3.69 us
  matrix products: 110 us -> 96.4 us
  local copies, waits for them, and re-layouts: 33.4 us -> 45.6 us
  Pallas kernels: 55 us -> 63.1 us
    ppermute x12 -> x32, waiting for transfers between devices: 79.8 us -> 17 us  [the longest x6 15.7 us: spread_weight(): lax.ppermute(shard, SPOT, [(spot(block, block, high), spot(block, high, h...]
    ppermute x54 -> x56, waiting for transfers between devices: 148 us -> 206 us  [partner(): lax.ppermute(block, axis, [(i, i ^ step) for i in range(lax.axis_size(axi...]
    ppermute x12 -> x32, starting transfers between devices: 24.1 us -> 55.1 us  [the longest x24 37.8 us: across(): return lax.ppermute(block, GRID[::-1], [(i, i ^ flip) for i in range(4)])]
    ppermute x54 -> x56, starting transfers between devices: 89.1 us -> 67.9 us  [partner(): lax.ppermute(block, axis, [(i, i ^ step) for i in range(lax.axis_size(axi...]
    concatenate x7 -> x26, other arithmetic: 4.51 us -> 22.4 us  [the longest x8 6.73 us: whole_waves(): jnp.concatenate([part, partner(part, 'core')], axis=0)]
    ppermute x4 -> x2, starting transfers between devices: 22.4 us -> 4.86 us  [send_rows(): lax.ppermute(rows, SPOT, rows_route(layer, layer))]
    select_n x1 -> x9, other arithmetic: 0.85 us -> 15.7 us  [the longest x5 7.62 us: assemble(): order = [jnp.where(left, a, b) for a, b in zip(own + other, other + own)]]
    dot_general x40, matrix products: 103 us -> 88.7 us  [product(): lax.dot_general(left, right, (((left_dim,), (right_dim,)), ((), ())), pre...]
  transfers between devices with their start and end apart: 102 -> 104, of which waited for: 36 -> 38; matrix products, arithmetic and copies ran while one was open for 25% -> 28% of each run, Pallas kernels for 7% -> 9%
where the time goes in v2:
time: 733 us; the launch traced here: 720 us
  waiting for transfers between devices  233 us (32%)
  starting transfers between devices  178 us (24%)
  matrix products  96.4 us (13%)
  other arithmetic  96.2 us (13%)
  Pallas kernels  63.1 us (9%)
  local copies, waits for them, and re-layouts  45.6 us (6%)
    ppermute x56, waiting for transfers between devices, partner(): lax.ppermute(block, axis, [(i, i ^ step) for i in range(lax.axis_size(axi...  206 us
    dot_general x40, matrix products, product(): lax.dot_general(left, right, (((left_dim,), (right_dim,)), ((), ())), pre...  88.7 us
    ppermute x56, starting transfers between devices, partner(): lax.ppermute(block, axis, [(i, i ^ step) for i in range(lax.axis_size(axi...  67.9 us
    ppermute x24, starting transfers between devices, across(): return lax.ppermute(block, GRID[::-1], [(i, i ^ flip) for i in range(4)])  37.8 us
    pallas_call x2, Pallas kernels, attend_back(): pl.pallas_call(attend_back_kernel, grid=(blocks,), in_specs=[pl.BlockSpec...  35.6 us
    pallas_call x2, Pallas kernels, attend(): pl.pallas_call(attend_kernel, grid=(blocks,), in_specs=[pl.BlockSpec((blo...  27.6 us
    ppermute x4, starting transfers between devices, keep_rows(): return lax.ppermute(rows, SPOT, rows_route(0, 0) + rows_route(1, 1))  18.4 us
    ppermute x6, starting transfers between devices, return_weight(): lax.ppermute(part, SPOT, [(b, a) for a, b in routes(layer, far)])  17.2 us
  transfers between devices with their start and end apart: 104, of which 38 were waited for; matrix products, arithmetic and copies ran while one was open for 28% of the time, Pallas kernels for 9%

profile of v2, /device:TPU:1, one launch (start us, length us, event | category | flops | bytes accessed | tf_op | source)
XLA Modules:
  0.0 719.8 jit_solution(11784490946030841389)
XLA Ops:
  2.0 4.7 collective-permute-start.48
  29.5 5.0 fusion.146
  50.7 12.5 %collective-permute-start.45 = (bf16[256,1024]{1,0:T(8,128)(2,1)S(1)}, bf16[256,1024]{1,0:T(8,128)(2,1)}, u32[]{:S(2)}, u32[]{:S(2)}) collective-permute-start(bf16[256,1024]{1,0:T(8,128)(2,1)S(1)} %get-tuple-element.1025), channel_id=1, source_target_pairs={{0,4},{4,0},{1,5},{5,1},{2,6},{6,2},{3,7},{7,3},{8,12},{12,8},{9,1... | collective-permute-start | bytes 1572872 | tf_op jit(solution)/shard_map/ppermute | solution.py:27
  72.5 8.5 %collective-permute-done.56 = bf16[256,2304]{1,0:T(8,128)(2,1)} collective-permute-done((bf16[256,2304]{1,0:T(8,128)(2,1)}, bf16[256,2304]{1,0:T(8,128)(2,1)}, u32[]{:S(2)}, u32[]{:S(2)}) %collective-permute-start.56) | collective-permute-done | bytes 1179680 | tf_op jit(solution)/shard_map/ppermute | solution.py:348
  93.9 8.4 %collective-permute-start.57 = (bf16[256,1280]{1,0:T(8,128)(2,1)S(1)}, bf16[256,1280]{1,0:T(8,128)(2,1)}, u32[]{:S(2)}, u32[]{:S(2)}) collective-permute-start(bf16[256,1280]{1,0:T(8,128)(2,1)S(1)} %slice.322), channel_id=1, source_target_pairs={{0,16},{8,24},{16,0},{24,8},{1,17},{9,25},{17,1},{25,9},{2,18},{10... | collective-permute-start | bytes 1966088 | tf_op jit(solution)/shard_map/ppermute | solution.py:366
  104.5 17.6 %conditional.14 = (bf16[1024,768]{1,0:T(8,128)(2,1)}, bf16[1024,256]{1,0:T(8,128)(2,1)S(1)}, f32[4,1024]{1,0:T(4,128)}) conditional(s32[]{:T(128)} %bitcast.33, () %tuple.155, (bf16[512,1024]{1,0:T(8,128)(2,1)S(1)}, bf16[1024,768]{0,1:T(8,128)(2,1)S(1)}, bf16[512,1024]{1,0:T(8,128)(2,1)S(1)}, s32[1024,2]{0,1:T(2,128)S(1)}, ...), branch_computations={%region_4.5_spmd, %region_5.6_spmd} | conditional | flops 5909512192 | bytes 12075032 | solution.py:243
  108.4 13.6 %attend.2 = (bf16[1024,256]{1,0:T(8,128)(2,1)S(1)}, f32[4,1024]{1,0:T(4,128)}) custom-call(bf16[1024,768]{1,0:T(8,128)(2,1)} %pad_maximum_fusion.query_ref.key_ref.value_ref, bf16[1024,768]{1,0:T(8,128)(2,1)} %pad_maximum_fusion.query_ref.key_ref.value_ref, bf16[1024,768]{1,0:T(8,128)(2,1)} %pad_maximum_fusion.query_ref.key_ref.value_ref, ...), custom_call_target="tpu_custom_call" | custom-call | flops 4294967296 | bytes 2097152 | tf_op jit(solution)/shard_map/cond/branch_1_fun/attend/pallas_call | solution.py:120
  123.4 4.7 collective-permute-done.61
  131.0 8.2 %collective-permute-start.64 = (bf16[256,1024]{1,0:T(8,128)(2,1)}, bf16[256,1024]{1,0:T(8,128)(2,1)}, u32[]{:S(2)}, u32[]{:S(2)}) collective-permute-start(bf16[256,1024]{1,0:T(8,128)(2,1)} %slice.329), channel_id=1, source_target_pairs={{0,24},{8,16},{16,8},{24,0},{1,25},{9,17},{17,9},{25,1},{2,26},{10... | collective-permute-start | bytes 1572872 | tf_op jit(solution)/shard_map/ppermute | solution.py:366
  144.4 42.4 %conditional.15 = (f32[256,1024]{1,0:T(8,128)S(1)}, f32[256,1024]{1,0:T(8,128)}, f32[256,1]{0,1:T(1,128)S(1)}, bf16[512,1024]{1,0:T(8,128)(2,1)}, bf16[512,1024]...) conditional(s32[]{:T(128)} %bitcast.33, () %tuple.154, ...), branch_computations={%region_6.7_spmd, %region_7.10_spmd} | conditional | flops 2711879936 | bytes 69928704 | solution.py:243
  149.0 11.9 %collective-permute-done.1 = bf16[256,1024]{1,0:T(8,128)(2,1)S(1)} collective-permute-done((bf16[256,1024]{1,0:T(8,128)(2,1)S(1)}, bf16[256,1024]{1,0:T(8,128)(2,1)S(1)}, u32[]{:S(2)}, u32[]{:S(2)}) %collective-permute-start.1) | collective-permute-done | bytes 524320 | tf_op jit(solution)/shard_map/cond/branch_1_fun/ppermute | solution.py:27
  167.7 4.9 add_convert_fusion.1
  172.6 6.0 collective-permute-done.4
  181.8 5.0 add_convert_fusion
  195.3 42.3 %conditional.16 = (bf16[256,1024]{1,0:T(8,128)(2,1)}, f32[256,1024]{1,0:T(8,128)S(1)}, f32[256,1]{0,1:T(1,128)S(1)}, bf16[512,1024]{1,0:T(8,128)(2,1)S(1)}, bf16[512,1024]{1,0:T(8,128)(2,1)S(1)}) conditional(s32[]{:T(128)} %bitcast.33, () %tuple.153, (bf16[512,1024]{1,0:T(8,128)(2,1)}, bf16[1024,1024]{1,0:T(8,128)(2,1)}, ...), branch_computations={%region_10.11_spmd, %region_11.14_spmd} | conditional | flops 2158231808 | bytes 39519824 | solution.py:243
  205.7 11.3 %collective-permute-done.7 = bf16[256,1024]{1,0:T(8,128)(2,1)S(1)} collective-permute-done((bf16[256,1024]{1,0:T(8,128)(2,1)S(1)}, bf16[256,1024]{1,0:T(8,128)(2,1)S(1)}, u32[]{:S(2)}, u32[]{:S(2)}) %collective-permute-start.7) | collective-permute-done | bytes 524320 | tf_op jit(solution)/shard_map/cond/branch_1_fun/ppermute | solution.py:27
  224.2 9.0 %collective-permute-done.10 = bf16[256,1024]{1,0:T(8,128)(2,1)S(1)} collective-permute-done((bf16[256,1024]{1,0:T(8,128)(2,1)S(1)}, bf16[256,1024]{1,0:T(8,128)(2,1)S(1)}, u32[]{:S(2)}, u32[]{:S(2)}) %collective-permute-start.10) | collective-permute-done | bytes 524320 | tf_op jit(solution)/shard_map/cond/branch_1_fun/ppermute | solution.py:27
  244.9 6.1 collective-permute-start.70
  251.1 17.4 %conditional.17 = (bf16[1024,768]{1,0:T(8,128)(2,1)}, bf16[1024,256]{1,0:T(8,128)(2,1)}, f32[4,1024]{1,0:T(4,128)S(1)}) conditional(s32[]{:T(128)} %bitcast.33, () %tuple.152, (bf16[512,1024]{1,0:T(8,128)(2,1)S(1)}, bf16[1024,768]{1,0:T(8,128)(2,1)S(1)}, bf16[512,1024]{1,0:T(8,128)(2,1)S(1)}, s32[1024,2]{0,1:T(2,128)S(1)}, ...), branch_computations={%region_14.15_spmd, %region_15.16_spmd} | conditional | flops 5909512192 | bytes 12075032 | solution.py:243
  254.6 13.9 %attend.3 = (bf16[1024,256]{1,0:T(8,128)(2,1)}, f32[4,1024]{1,0:T(4,128)S(1)}) custom-call(bf16[1024,768]{1,0:T(8,128)(2,1)} %pad_maximum_fusion.4.query_ref.key_ref.value_ref, bf16[1024,768]{1,0:T(8,128)(2,1)} %pad_maximum_fusion.4.query_ref.key_ref.value_ref, bf16[1024,768]{1,0:T(8,128)(2,1)} %pad_maximum_fusion.4.query_ref.key_ref.value_ref, ...), custom_call_target="tpu_custom_call" | custom-call | flops 4294967296 | bytes 2097152 | tf_op jit(solution)/shard_map/cond/branch_1_fun/attend/pallas_call | solution.py:120
  269.3 5.7 collective-permute-done.71
  280.2 43.7 %conditional.18 = (f32[256,1024]{1,0:T(8,128)S(1)}, f32[256,1024]{1,0:T(8,128)S(1)}, f32[256,1]{0,1:T(1,128)S(1)}, bf16[512,1024]{1,0:T(8,128)(2,1)}, bf16[512,1024]{1,0:T(8,128)(2,1)}) conditional(s32[]{:T(128)} %bitcast.33, () %tuple.174, (bf16[256,1024]{1,0:T(8,128)(2,1)}, bf16[1024,256]{1,0:T(8,128)(2,1)}, bf16[1024,256]{1,0:T(8,128)(2,1)S(1)}, ...), branch_computations={%region_16.17_spmd, %region_17.20_spmd} | conditional | flops 546832640 | bytes 45287052 | solution.py:243
  288.1 15.5 %collective-permute-done.13 = bf16[256,1024]{1,0:T(8,128)(2,1)S(1)} collective-permute-done((bf16[256,1024]{1,0:T(8,128)(2,1)S(1)}, bf16[256,1024]{1,0:T(8,128)(2,1)S(1)}, u32[]{:S(2)}, u32[]{:S(2)}) %collective-permute-start.13) | collective-permute-done | bytes 524320 | tf_op jit(solution)/shard_map/cond/branch_1_fun/ppermute | solution.py:27
  308.7 10.1 %collective-permute-done.16 = bf16[256,1024]{1,0:T(8,128)(2,1)S(1)} collective-permute-done((bf16[256,1024]{1,0:T(8,128)(2,1)S(1)}, bf16[256,1024]{1,0:T(8,128)(2,1)S(1)}, u32[]{:S(2)}, u32[]{:S(2)}) %collective-permute-start.16) | collective-permute-done | bytes 524320 | tf_op jit(solution)/shard_map/cond/branch_1_fun/ppermute | solution.py:27
  330.0 24.3 %conditional.19 = (bf16[256,1024]{1,0:T(8,128)(2,1)S(1)}, bf16[512,1024]{1,0:T(8,128)(2,1)S(1)}, bf16[512,1024]{1,0:T(8,128)(2,1)}, bf16[512,1024]{1,0:T(8,128)(2,1)S(1)}, bf16[512,1024]{1,0:T(8,128)(2,1)S(1)}) conditional(s32[]{:T(128)} %bitcast.33, () %tuple.178, (bf16[512,1024]{1,0:T(8,128)(2,1)}, bf16[1024,1024]{1,0:T(8,128)(2,1)S(1)}, ...), branch_computations={%region_20.21_spmd, %region_21.22_spmd} | conditional | flops 4317249536 | bytes 47710452 | solution.py:243
  342.3 11.6 %collective-permute-done.19 = bf16[256,1024]{1,0:T(8,128)(2,1)S(1)} collective-permute-done((bf16[256,1024]{1,0:T(8,128)(2,1)S(1)}, bf16[256,1024]{1,0:T(8,128)(2,1)S(1)}, u32[]{:S(2)}, u32[]{:S(2)}) %collective-permute-start.19) | collective-permute-done | bytes 524320 | tf_op jit(solution)/shard_map/cond/branch_1_fun/ppermute | solution.py:27
  355.1 28.0 %conditional.20 = (f32[256,1024]{1,0:T(8,128)S(1)}, bf16[4,256,2048]{2,1,0:T(8,128)(2,1)S(1)}) conditional(s32[]{:T(128)} %bitcast.33, () %tuple.177, (bf16[256,1024]{1,0:T(8,128)(2,1)}, bf16[256,1024]{1,0:T(8,128)(2,1)}, bf16[1024,1024]{1,0:T(8,128)(2,1)}, bf16[512,1024]{1,0:T(8,128)(2,1)S(1)}, bf16[1024,1024]{1,0:T(8,128)(2,1)}, ...), branch_computations={%region_22.23_spmd, %region_23.24_spmd} | conditional | flops 8630566912 | bytes 84934936 | solution.py:243
  374.2 8.7 %collective-permute-done.22 = bf16[256,1024]{1,0:T(8,128)(2,1)S(1)} collective-permute-done((bf16[256,1024]{1,0:T(8,128)(2,1)S(1)}, bf16[256,1024]{1,0:T(8,128)(2,1)S(1)}, u32[]{:S(2)}, u32[]{:S(2)}) %collective-permute-start.22) | collective-permute-done | bytes 524320 | tf_op jit(solution)/shard_map/cond/branch_1_fun/ppermute | solution.py:27
  388.7 19.5 %conditional.21 = (f32[256,1024]{1,0:T(8,128)S(1)}, bf16[1024,1024]{1,0:T(8,128)(2,1)S(1)}, bf16[1024,256]{1,0:T(8,128)(2,1)S(1)}, f32[4,1024]{1,0:T(4,128)S(1)}, f32[4,1024]{1,0:T(4,128)S(1)}) conditional(s32[]{:T(128)} %bitcast.33, () %tuple.173, (f32[256,1]{0,1:T(1,128)S(1)}, f32[256,1024]{1,0:T(8,128)S(1)}, f32[256,1024]{1,0:T(8,128)S(1)}, ...), branch_computations={%region_24.25_spmd, %region_25.28_spmd} | conditional | flops 579600384 | bytes 27313312 | solution.py:243
  393.6 11.6 %collective-permute-done.25 = bf16[256,1024]{1,0:T(8,128)(2,1)S(1)} collective-permute-done((bf16[256,1024]{1,0:T(8,128)(2,1)S(1)}, bf16[256,1024]{1,0:T(8,128)(2,1)S(1)}, u32[]{:S(2)}, u32[]{:S(2)}) %collective-permute-start.25) | collective-permute-done | bytes 524320 | tf_op jit(solution)/shard_map/cond/branch_1_fun/ppermute | solution.py:27
  410.9 5.8 collective-permute-start.79
  416.8 27.0 %conditional.22 = (bf16[1024,768]{1,0:T(8,128)(2,1)}, bf16[1024,1024]{1,0:T(8,128)(2,1)}) conditional(s32[]{:T(128)} %bitcast.33, () %tuple.151, (bf16[1024,768]{1,0:T(8,128)(2,1)}, s32[1024,2]{0,1:T(2,128)S(1)}, s32[3,1024]{1,0:T(4,128)S(1)}, bf16[1024,256]{1,0:T(8,128)(2,1)S(1)}, f32[4,1024]{1,0:T(4,128)S(1)}, ...), branch_computations={%region_28.29_spmd, %region_29.30_spmd} | conditional | flops 12894339072 | bytes 39338112 | solution.py:243
  419.1 17.8 %attend_back.2 = bf16[1024,768]{1,0:T(8,128)(2,1)} custom-call(bf16[1024,768]{1,0:T(8,128)(2,1)} %get-tuple-element.374.query_ref.key_ref.value_ref, bf16[1024,768]{1,0:T(8,128)(2,1)} %get-tuple-element.374.query_ref.key_ref.value_ref, bf16[1024,768]{1,0:T(8,128)(2,1)} %get-tuple-element.374.query_ref.key_ref.value_ref, s32[1024,2]{1,0:T(8,128)S(1)} %copy.121.key_info_ref, ...), custom_call_target="tpu_custom_call" | custom-call | flops 10737418240 | bytes 3670016 | tf_op jit(solution)/shard_map/cond/branch_1_fun/attend_back/pallas_call | solution.py:195
  449.5 39.8 %conditional.23 = (bf16[256,1024]{1,0:T(8,128)(2,1)S(1)}, f32[4,4,1024]{2,0,1:T(4,128)S(1)}, f32[256,1024]{1,0:T(8,128)S(1)}, bf16[512,1024]{1,0:T(8,128)(2,1)S(1)}, bf16[512,1024]{1,0:T(8,128)(2,1)S(1)}) conditional(s32[]{:T(128)} %bitcast.33, () %tuple.190, (f32[256,1]{0,1:T(1,128)S(1)}, bf16[1024,768]{1,0:T(8,128)(2,1)}, ...), branch_computations={%region_30.31_spmd, %region_31.34_spmd} | conditional | flops 1646575616 | bytes 52086068 | solution.py:243
  460.8 11.4 %collective-permute-done.28 = bf16[256,1024]{1,0:T(8,128)(2,1)S(1)} collective-permute-done((bf16[256,1024]{1,0:T(8,128)(2,1)S(1)}, bf16[256,1024]{1,0:T(8,128)(2,1)S(1)}, u32[]{:S(2)}, u32[]{:S(2)}) %collective-permute-start.28) | collective-permute-done | bytes 524320 | tf_op jit(solution)/shard_map/cond/branch_1_fun/ppermute | solution.py:27
  474.8 10.7 %collective-permute-done.31 = bf16[256,1024]{1,0:T(8,128)(2,1)S(1)} collective-permute-done((bf16[256,1024]{1,0:T(8,128)(2,1)S(1)}, bf16[256,1024]{1,0:T(8,128)(2,1)S(1)}, u32[]{:S(2)}, u32[]{:S(2)}) %collective-permute-start.31) | collective-permute-done | bytes 524320 | tf_op jit(solution)/shard_map/cond/branch_1_fun/ppermute | solution.py:27
  497.4 5.3 collective-permute-start.85
  502.7 44.3 %conditional.24 = (f32[256,1024]{1,0:T(8,128)S(1)}, bf16[1024,2048]{1,0:T(8,128)(2,1)S(1)}) conditional(s32[]{:T(128)} %bitcast.33, () %tuple.189, (bf16[512,1024]{1,0:T(8,128)(2,1)S(1)}, bf16[1024,1024]{1,0:T(8,128)(2,1)}, bf16[512,1024]{1,0:T(8,128)(2,1)}, bf16[1024,1024]{1,0:T(8,128)(2,1)S(1)}, bf16[512,1024]{1,0:T(8,128)(2,1)S(1)}, ...), branch_computations={%region_34.35_spmd, %region_35.36_spmd} | conditional | flops 8622178304 | bytes 55574664 | solution.py:243
  522.5 24.4 %collective-permute-done.34 = bf16[256,1024]{1,0:T(8,128)(2,1)S(1)} collective-permute-done((bf16[256,1024]{1,0:T(8,128)(2,1)S(1)}, bf16[256,1024]{1,0:T(8,128)(2,1)S(1)}, u32[]{:S(2)}, u32[]{:S(2)}) %collective-permute-start.34) | collective-permute-done | bytes 524320 | tf_op jit(solution)/shard_map/cond/branch_1_fun/ppermute | solution.py:27
  553.0 24.9 %conditional.25 = (f32[256,1024]{1,0:T(8,128)}, bf16[1024,1024]{1,0:T(8,128)(2,1)}, bf16[1024,256]{1,0:T(8,128)(2,1)}, f32[4,1024]{1,0:T(4,128)S(1)}, f32[4,1024]{1,0:T(4,128)S(1)}) conditional(s32[]{:T(128)} %bitcast.33, () %tuple.188, (f32[256,1]{0,1:T(1,128)S(1)}, f32[256,1024]{1,0:T(8,128)S(1)}, f32[256,1024]{1,0:T(8,128)S(1)}, ...), branch_computations={%region_36.37_spmd, %region_37.40_spmd} | conditional | flops 579600384 | bytes 27313312 | solution.py:243
  560.2 11.7 %collective-permute-done.37 = bf16[256,1024]{1,0:T(8,128)(2,1)S(1)} collective-permute-done((bf16[256,1024]{1,0:T(8,128)(2,1)S(1)}, bf16[256,1024]{1,0:T(8,128)(2,1)S(1)}, u32[]{:S(2)}, u32[]{:S(2)}) %collective-permute-start.37) | collective-permute-done | bytes 524320 | tf_op jit(solution)/shard_map/cond/branch_1_fun/ppermute | solution.py:27
  579.3 12.8 %collective-permute-start.90 = (bf16[256,1024]{1,0:T(8,128)(2,1)}, bf16[256,1024]{1,0:T(8,128)(2,1)}, u32[]{:S(2)}, u32[]{:S(2)}) collective-permute-start(bf16[256,1024]{1,0:T(8,128)(2,1)} %copy-done.75), channel_id=1, source_target_pairs={{0,16},{2,20},{4,18},{6,22},{1,17},{3,21},{5,19},{7,23},{8,24},{10... | collective-permute-start | bytes 1572872 | tf_op jit(solution)/shard_map/ppermute | solution.py:455
  592.2 24.0 %conditional.26 = (bf16[1024,768]{1,0:T(8,128)(2,1)}, bf16[1024,1024]{1,0:T(8,128)(2,1)S(1)}) conditional(s32[]{:T(128)} %bitcast.33, () %tuple.187, (bf16[1024,768]{1,0:T(8,128)(2,1)}, s32[1024,2]{0,1:T(2,128)S(1)}, s32[3,1024]{1,0:T(4,128)S(1)}, bf16[1024,256]{1,0:T(8,128)(2,1)}, f32[4,1024]{1,0:T(4,128)S(1)}, ...), branch_computations={%region_40.41_spmd, %region_41.42_spmd} | conditional | flops 12894339072 | bytes 24657992 | solution.py:243
  592.4 17.8 %attend_back.3 = bf16[1024,768]{1,0:T(8,128)(2,1)} custom-call(bf16[1024,768]{1,0:T(8,128)(2,1)} %get-tuple-element.413.query_ref.key_ref.value_ref, bf16[1024,768]{1,0:T(8,128)(2,1)} %get-tuple-element.413.query_ref.key_ref.value_ref, bf16[1024,768]{1,0:T(8,128)(2,1)} %get-tuple-element.413.query_ref.key_ref.value_ref, s32[1024,2]{1,0:T(8,128)S(1)} %copy.122.key_info_ref, ...), custom_call_target="tpu_custom_call" | custom-call | flops 10737418240 | bytes 3670016 | tf_op jit(solution)/shard_map/cond/branch_1_fun/attend_back/pallas_call | solution.py:195
  621.4 4.5 collective-permute-start.93
  629.5 34.4 %conditional.27 = (bf16[256,1024]{1,0:T(8,128)(2,1)}, f32[4,4,1024]{2,0,1:T(4,128)S(1)}) conditional(s32[]{:T(128)} %bitcast.33, () %tuple.186, (f32[256]{0:T(256)S(1)}, bf16[1024,768]{1,0:T(8,128)(2,1)}, bf16[1024,768]{0,1:T(8,128)(2,1)S(1)}, f32[256,1024]{1,0:T(8,128)S(1)}, f32[256,1024]{1,0:T(8,128)S(1)}, /*index=5*/f32[256,1024]{1,0:T(8,128)}, ...), branch_computations={%region_42.43_spmd, %region_43.46_spmd} | conditional | flops 1641333248 | bytes 32689288 | solution.py:243
  637.1 22.5 %collective-permute-done.40 = bf16[256,1024]{1,0:T(8,128)(2,1)S(1)} collective-permute-done((bf16[256,1024]{1,0:T(8,128)(2,1)S(1)}, bf16[256,1024]{1,0:T(8,128)(2,1)S(1)}, u32[]{:S(2)}, u32[]{:S(2)}) %collective-permute-start.40) | collective-permute-done | bytes 524320 | tf_op jit(solution)/shard_map/cond/branch_1_fun/ppermute | solution.py:27
  684.2 12.0 %collective-permute-done.96 = bf16[256,1024]{1,0:T(8,128)(2,1)S(1)} collective-permute-done((bf16[256,1024]{1,0:T(8,128)(2,1)S(1)}, bf16[256,1024]{1,0:T(8,128)(2,1)S(1)}, u32[]{:S(2)}, u32[]{:S(2)}) %collective-permute-start.96) | collective-permute-done | bytes 524320 | tf_op jit(solution)/shard_map/ppermute | solution.py:27
  (651 shorter events, 358.5 us)
Async XLA Ops:
  2.0 23.7 %collective-permute-start.48 = (bf16[256,768]{0,1:T(8,128)(2,1)S(1)}, bf16[256,768]{0,1:T(8,128)(2,1)}, u32[]{:S(2)}, u32[]{:S(2)}) collective-permute-start(bf16[256,768]{0,1:T(8,128)(2,1)S(1)} %bitcast.286), channel_id=1, source_target_pairs={{16,0},{18,2},{4,20},{6,22},{17,1},{19,3},{5,21},{7,23},{24,8},{26... | collective-permute-start | bytes 1179656 | tf_op jit(solution)/shard_map/ppermute | solution.py:337
  16.9 28.3 %collective-permute-start.54 = (bf16[256,2304]{1,0:T(8,128)(2,1)S(1)}, bf16[256,2304]{1,0:T(8,128)(2,1)}, u32[]{:S(2)}, u32[]{:S(2)}) collective-permute-start(bf16[256,2304]{1,0:T(8,128)(2,1)S(1)} %pad_maximum_fusion.28), channel_id=1, source_target_pairs={{16,0},{18,2},{4,20},{6,22},{17,1},{19,3},{5,21},{7,23},{24,8},{26... | collective-permute-start | bytes 3538952 | tf_op jit(solution)/shard_map/ppermute | solution.py:337
  39.5 23.7 %collective-permute-start.46 = (bf16[256,1024]{1,0:T(8,128)(2,1)S(1)}, bf16[256,1024]{1,0:T(8,128)(2,1)}, u32[]{:S(2)}, u32[]{:S(2)}) collective-permute-start(bf16[256,1024]{1,0:T(8,128)(2,1)S(1)} %get-tuple-element.1025), channel_id=1, source_target_pairs={{0,1},{1,0},{2,3},{3,2},{4,5},{5,4},{6,7},{7,6},{8,9},{9,8},{10,11... | collective-permute-start | bytes 1572872 | tf_op jit(solution)/shard_map/ppermute | solution.py:27
  47.6 24.9 %collective-permute-start.55 = (bf16[256,2304]{1,0:T(8,128)(2,1)}, bf16[256,2304]{1,0:T(8,128)(2,1)}, u32[]{:S(2)}, u32[]{:S(2)}) collective-permute-start(bf16[256,2304]{1,0:T(8,128)(2,1)} %get-tuple-element.603), channel_id=1, source_target_pairs={{0,0},{2,6},{20,16},{22,22},{1,1},{3,7},{21,17},{23,23},{8,8},{10,... | collective-permute-start | bytes 3538952 | tf_op jit(solution)/shard_map/ppermute | solution.py:348
  49.4 31.6 %collective-permute-start.56 = (bf16[256,2304]{1,0:T(8,128)(2,1)}, bf16[256,2304]{1,0:T(8,128)(2,1)}, u32[]{:S(2)}, u32[]{:S(2)}) collective-permute-start(bf16[256,2304]{1,0:T(8,128)(2,1)} %get-tuple-element.603), channel_id=1, source_target_pairs={{0,2},{2,4},{20,18},{22,20},{1,3},{3,5},{21,19},{23,21},{8,10},{10... | collective-permute-start | bytes 3538952 | tf_op jit(solution)/shard_map/ppermute | solution.py:348
  85.2 36.9 %collective-permute-start.60 = (bf16[256,3072]{1,0:T(8,128)(2,1)}, bf16[256,3072]{1,0:T(8,128)(2,1)}, u32[]{:S(2)}, u32[]{:S(2)}) collective-permute-start(bf16[256,3072]{1,0:T(8,128)(2,1)} %pad_maximum_fusion.26), channel_id=1, source_target_pairs={{0,0},{2,6},{20,16},{22,22},{1,1},{3,7},{21,17},{23,23},{8,8},{10,... | collective-permute-start | bytes 4718600 | tf_op jit(solution)/shard_map/ppermute | solution.py:348
  87.0 41.1 %collective-permute-start.61 = (bf16[256,3072]{1,0:T(8,128)(2,1)}, bf16[256,3072]{1,0:T(8,128)(2,1)}, u32[]{:S(2)}, u32[]{:S(2)}) collective-permute-start(bf16[256,3072]{1,0:T(8,128)(2,1)} %pad_maximum_fusion.26), channel_id=1, source_target_pairs={{0,2},{2,4},{20,18},{22,20},{1,3},{3,5},{21,19},{23,21},{8,10},{10... | collective-permute-start | bytes 4718600 | tf_op jit(solution)/shard_map/ppermute | solution.py:348
  93.9 37.1 %collective-permute-start.57 = (bf16[256,1280]{1,0:T(8,128)(2,1)S(1)}, bf16[256,1280]{1,0:T(8,128)(2,1)}, u32[]{:S(2)}, u32[]{:S(2)}) collective-permute-start(bf16[256,1280]{1,0:T(8,128)(2,1)S(1)} %slice.322), channel_id=1, source_target_pairs={{0,16},{8,24},{16,0},{24,8},{1,17},{9,25},{17,1},{25,9},{2,18},{10... | collective-permute-start | bytes 1966088 | tf_op jit(solution)/shard_map/ppermute | solution.py:366
  102.3 36.9 %collective-permute-start.58 = (bf16[256,1280]{1,0:T(8,128)(2,1)S(1)}, bf16[256,1280]{1,0:T(8,128)(2,1)}, u32[]{:S(2)}, u32[]{:S(2)}) collective-permute-start(bf16[256,1280]{1,0:T(8,128)(2,1)S(1)} %slice.322), channel_id=1, source_target_pairs={{0,8},{8,0},{16,24},{24,16},{1,9},{9,1},{17,25},{25,17},{2,10},{10... | collective-permute-start | bytes 1966088 | tf_op jit(solution)/shard_map/ppermute | solution.py:366
  103.6 35.5 %collective-permute-start.59 = (bf16[256,1280]{1,0:T(8,128)(2,1)S(1)}, bf16[256,1280]{1,0:T(8,128)(2,1)}, u32[]{:S(2)}, u32[]{:S(2)}) collective-permute-start(bf16[256,1280]{1,0:T(8,128)(2,1)S(1)} %slice.322), channel_id=1, source_target_pairs={{0,24},{8,16},{16,8},{24,0},{1,25},{9,17},{17,9},{25,1},{2,26},{10... | collective-permute-start | bytes 1966088 | tf_op jit(solution)/shard_map/ppermute | solution.py:366
  122.1 69.6 %collective-permute-start.62 = (bf16[256,1024]{1,0:T(8,128)(2,1)}, bf16[256,1024]{1,0:T(8,128)(2,1)}, u32[]{:S(2)}, u32[]{:S(2)}) collective-permute-start(bf16[256,1024]{1,0:T(8,128)(2,1)} %slice.329), channel_id=1, source_target_pairs={{0,16},{8,24},{16,0},{24,8},{1,17},{9,25},{17,1},{25,9},{2,18},{10... | collective-permute-start | bytes 1572872 | tf_op jit(solution)/shard_map/ppermute | solution.py:366
  128.1 63.8 %collective-permute-start.63 = (bf16[256,1024]{1,0:T(8,128)(2,1)}, bf16[256,1024]{1,0:T(8,128)(2,1)}, u32[]{:S(2)}, u32[]{:S(2)}) collective-permute-start(bf16[256,1024]{1,0:T(8,128)(2,1)} %slice.329), channel_id=1, source_target_pairs={{0,8},{8,0},{16,24},{24,16},{1,9},{9,1},{17,25},{25,17},{2,10},{10... | collective-permute-start | bytes 1572872 | tf_op jit(solution)/shard_map/ppermute | solution.py:366
  131.0 60.9 %collective-permute-start.64 = (bf16[256,1024]{1,0:T(8,128)(2,1)}, bf16[256,1024]{1,0:T(8,128)(2,1)}, u32[]{:S(2)}, u32[]{:S(2)}) collective-permute-start(bf16[256,1024]{1,0:T(8,128)(2,1)} %slice.329), channel_id=1, source_target_pairs={{0,24},{8,16},{16,8},{24,0},{1,25},{9,17},{17,9},{25,1},{2,26},{10... | collective-permute-start | bytes 1572872 | tf_op jit(solution)/shard_map/ppermute | solution.py:366
  186.8 55.5 %collective-permute-start.65 = (bf16[256,1024]{1,0:T(8,128)(2,1)}, bf16[256,1024]{1,0:T(8,128)(2,1)}, u32[]{:S(2)}, u32[]{:S(2)}) collective-permute-start(bf16[256,1024]{1,0:T(8,128)(2,1)} %slice.334), channel_id=1, source_target_pairs={{0,16},{8,24},{16,0},{24,8},{1,17},{9,25},{17,1},{25,9},{2,18},{10... | collective-permute-start | bytes 1572872 | tf_op jit(solution)/shard_map/ppermute | solution.py:366
  188.1 54.2 %collective-permute-start.66 = (bf16[256,1024]{1,0:T(8,128)(2,1)}, bf16[256,1024]{1,0:T(8,128)(2,1)}, u32[]{:S(2)}, u32[]{:S(2)}) collective-permute-start(bf16[256,1024]{1,0:T(8,128)(2,1)} %slice.334), channel_id=1, source_target_pairs={{0,8},{8,0},{16,24},{24,16},{1,9},{9,1},{17,25},{25,17},{2,10},{10... | collective-permute-start | bytes 1572872 | tf_op jit(solution)/shard_map/ppermute | solution.py:366
  191.7 50.6 %collective-permute-start.67 = (bf16[256,1024]{1,0:T(8,128)(2,1)S(1)}, bf16[256,1024]{1,0:T(8,128)(2,1)}, u32[]{:S(2)}, u32[]{:S(2)}) collective-permute-start(bf16[256,1024]{1,0:T(8,128)(2,1)S(1)} %copy-done.33), channel_id=1, source_target_pairs={{0,24},{8,16},{16,8},{24,0},{1,25},{9,17},{17,9},{25,1},{2,26},{10... | collective-permute-start | bytes 1572872 | tf_op jit(solution)/shard_map/ppermute | solution.py:366
  237.6 37.4 %collective-permute-start.68 = (bf16[256,2048]{1,0:T(8,128)(2,1)}, bf16[256,2048]{1,0:T(8,128)(2,1)}, u32[]{:S(2)}, u32[]{:S(2)}) collective-permute-start(bf16[256,2048]{1,0:T(8,128)(2,1)} %slice.336), channel_id=1, source_target_pairs={{0,16},{8,24},{16,0},{24,8},{1,17},{9,25},{17,1},{25,9},{2,18},{10... | collective-permute-start | bytes 3145736 | tf_op jit(solution)/shard_map/ppermute | solution.py:366
  238.9 36.1 %collective-permute-start.69 = (bf16[256,2048]{1,0:T(8,128)(2,1)}, bf16[256,2048]{1,0:T(8,128)(2,1)}, u32[]{:S(2)}, u32[]{:S(2)}) collective-permute-start(bf16[256,2048]{1,0:T(8,128)(2,1)} %slice.336), channel_id=1, source_target_pairs={{0,8},{8,0},{16,24},{24,16},{1,9},{9,1},{17,25},{25,17},{2,10},{10... | collective-permute-start | bytes 3145736 | tf_op jit(solution)/shard_map/ppermute | solution.py:366
  244.9 24.4 %collective-permute-start.70 = (bf16[256,1024]{1,0:T(8,128)(2,1)}, bf16[256,1024]{1,0:T(8,128)(2,1)S(1)}, u32[]{:S(2)}, u32[]{:S(2)}) collective-permute-start(bf16[256,1024]{1,0:T(8,128)(2,1)} %get-tuple-element.651), channel_id=1, source_target_pairs={{0,0},{2,4},{4,2},{6,6},{16,16},{18,20},{20,18},{22,22},{1,1},{3,5... | collective-permute-start | bytes 1572872 | tf_op jit(solution)/shard_map/ppermute | solution.py:447
  251.0 24.0 %collective-permute-start.71 = (bf16[256,1024]{1,0:T(8,128)(2,1)}, bf16[256,1024]{1,0:T(8,128)(2,1)S(1)}, u32[]{:S(2)}, u32[]{:S(2)}) collective-permute-start(bf16[256,1024]{1,0:T(8,128)(2,1)} %get-tuple-element.652), channel_id=1, source_target_pairs={{0,16},{2,20},{4,18},{6,22},{16,0},{18,4},{20,2},{22,6},{1,17},{3,... | collective-permute-start | bytes 1572872 | tf_op jit(solution)/shard_map/ppermute | solution.py:451
  275.8 48.1 %collective-permute-start.72 = (bf16[256,2048]{1,0:T(8,128)(2,1)}, bf16[256,2048]{1,0:T(8,128)(2,1)}, u32[]{:S(2)}, u32[]{:S(2)}) collective-permute-start(bf16[256,2048]{1,0:T(8,128)(2,1)} %slice.336), channel_id=1, source_target_pairs={{0,24},{8,16},{16,8},{24,0},{1,25},{9,17},{17,9},{25,1},{2,26},{10... | collective-permute-start | bytes 3145736 | tf_op jit(solution)/shard_map/ppermute | solution.py:366
  279.3 44.5 %collective-permute-start.73 = (bf16[256,1024]{1,0:T(8,128)(2,1)}, bf16[256,1024]{1,0:T(8,128)(2,1)}, u32[]{:S(2)}, u32[]{:S(2)}) collective-permute-start(bf16[256,1024]{1,0:T(8,128)(2,1)} %get-tuple-element.677), channel_id=1, source_target_pairs={{0,1},{1,0},{2,3},{3,2},{4,5},{5,4},{6,7},{7,6},{8,9},{9,8},{10,11... | collective-permute-start | bytes 1572872 | tf_op jit(solution)/shard_map/ppermute | solution.py:27
  323.9 30.4 %collective-permute-start.74 = (bf16[256,1024]{1,0:T(8,128)(2,1)}, bf16[256,1024]{1,0:T(8,128)(2,1)}, u32[]{:S(2)}, u32[]{:S(2)}) collective-permute-start(bf16[256,1024]{1,0:T(8,128)(2,1)} %get-tuple-element.677), channel_id=1, source_target_pairs={{0,4},{4,0},{1,5},{5,1},{2,6},{6,2},{3,7},{7,3},{8,12},{12,8},{9,1... | collective-permute-start | bytes 1572872 | tf_op jit(solution)/shard_map/ppermute | solution.py:27
  324.3 30.0 %collective-permute-start.75 = (bf16[256,1024]{1,0:T(8,128)(2,1)}, bf16[256,1024]{1,0:T(8,128)(2,1)}, u32[]{:S(2)}, u32[]{:S(2)}) collective-permute-start(bf16[256,1024]{1,0:T(8,128)(2,1)} %collective-permute-done.73), channel_id=1, source_target_pairs={{0,4},{4,0},{1,5},{5,1},{2,6},{6,2},{3,7},{7,3},{8,12},{12,8},{9,1... | collective-permute-start | bytes 1572872 | tf_op jit(solution)/shard_map/ppermute | solution.py:27
  385.3 58.4 %collective-permute-start.76 = (bf16[256,2048]{1,0:T(8,128)(2,1)}, bf16[256,2048]{1,0:T(8,128)(2,1)}, u32[]{:S(2)}, u32[]{:S(2)}) collective-permute-start(bf16[256,2048]{1,0:T(8,128)(2,1)} %get-tuple-element.1061), channel_id=1, source_target_pairs={{0,16},{8,24},{16,0},{24,8},{1,17},{9,25},{17,1},{25,9},{2,18},{10... | collective-permute-start | bytes 3145736 | tf_op jit(solution)/shard_map/ppermute | solution.py:366
  387.3 56.5 %collective-permute-start.77 = (bf16[256,2048]{1,0:T(8,128)(2,1)}, bf16[256,2048]{1,0:T(8,128)(2,1)}, u32[]{:S(2)}, u32[]{:S(2)}) collective-permute-start(bf16[256,2048]{1,0:T(8,128)(2,1)} %get-tuple-element.1060), channel_id=1, source_target_pairs={{0,8},{8,0},{16,24},{24,16},{1,9},{9,1},{17,25},{25,17},{2,10},{10... | collective-permute-start | bytes 3145736 | tf_op jit(solution)/shard_map/ppermute | solution.py:366
  387.7 56.0 %collective-permute-start.78 = (bf16[256,2048]{1,0:T(8,128)(2,1)}, bf16[256,2048]{1,0:T(8,128)(2,1)}, u32[]{:S(2)}, u32[]{:S(2)}) collective-permute-start(bf16[256,2048]{1,0:T(8,128)(2,1)} %get-tuple-element.1059), channel_id=1, source_target_pairs={{0,24},{8,16},{16,8},{24,0},{1,25},{9,17},{17,9},{25,1},{2,26},{10... | collective-permute-start | bytes 3145736 | tf_op jit(solution)/shard_map/ppermute | solution.py:366
  410.9 32.8 %collective-permute-start.79 = (bf16[256,1024]{1,0:T(8,128)(2,1)}, bf16[256,1024]{1,0:T(8,128)(2,1)}, u32[]{:S(2)}, u32[]{:S(2)}) collective-permute-start(bf16[256,1024]{1,0:T(8,128)(2,1)} %get-tuple-element.693), channel_id=1, source_target_pairs={{0,0},{2,4},{4,2},{6,6},{16,16},{18,20},{20,18},{22,22},{1,1},{3,5... | collective-permute-start | bytes 1572872 | tf_op jit(solution)/shard_map/ppermute | solution.py:447
  416.7 27.1 %collective-permute-start.80 = (bf16[256,1024]{1,0:T(8,128)(2,1)}, bf16[256,1024]{1,0:T(8,128)(2,1)}, u32[]{:S(2)}, u32[]{:S(2)}) collective-permute-start(bf16[256,1024]{1,0:T(8,128)(2,1)} %get-tuple-element.694), channel_id=1, source_target_pairs={{0,16},{2,20},{4,18},{6,22},{16,0},{18,4},{20,2},{22,6},{1,17},{3,... | collective-permute-start | bytes 1572872 | tf_op jit(solution)/shard_map/ppermute | solution.py:451
  446.8 45.6 %collective-permute-start.81 = (bf16[256,1024]{1,0:T(8,128)(2,1)}, bf16[256,1024]{1,0:T(8,128)(2,1)}, u32[]{:S(2)}, u32[]{:S(2)}) collective-permute-start(bf16[256,1024]{1,0:T(8,128)(2,1)} %get-tuple-element.1083), channel_id=1, source_target_pairs={{0,16},{8,24},{16,0},{24,8},{1,17},{9,25},{17,1},{25,9},{2,18},{10... | collective-permute-start | bytes 1572872 | tf_op jit(solution)/shard_map/ppermute | solution.py:366
  448.0 44.5 %collective-permute-start.82 = (bf16[256,1024]{1,0:T(8,128)(2,1)}, bf16[256,1024]{1,0:T(8,128)(2,1)}, u32[]{:S(2)}, u32[]{:S(2)}) collective-permute-start(bf16[256,1024]{1,0:T(8,128)(2,1)} %get-tuple-element.1082), channel_id=1, source_target_pairs={{0,8},{8,0},{16,24},{24,16},{1,9},{9,1},{17,25},{25,17},{2,10},{10... | collective-permute-start | bytes 1572872 | tf_op jit(solution)/shard_map/ppermute | solution.py:366
  448.5 44.0 %collective-permute-start.83 = (bf16[256,1024]{1,0:T(8,128)(2,1)}, bf16[256,1024]{1,0:T(8,128)(2,1)}, u32[]{:S(2)}, u32[]{:S(2)}) collective-permute-start(bf16[256,1024]{1,0:T(8,128)(2,1)} %get-tuple-element.1081), channel_id=1, source_target_pairs={{0,24},{8,16},{16,8},{24,0},{1,25},{9,17},{17,9},{25,1},{2,26},{10... | collective-permute-start | bytes 1572872 | tf_op jit(solution)/shard_map/ppermute | solution.py:366
  495.5 51.6 %collective-permute-start.84 = (bf16[256,3072]{1,0:T(8,128)(2,1)}, bf16[256,3072]{1,0:T(8,128)(2,1)}, u32[]{:S(2)}, u32[]{:S(2)}) collective-permute-start(bf16[256,3072]{1,0:T(8,128)(2,1)} %pad_maximum_fusion.27), channel_id=1, source_target_pairs={{0,16},{6,18},{16,20},{22,22},{1,17},{7,19},{17,21},{23,23},{8,24}... | collective-permute-start | bytes 4718600 | tf_op jit(solution)/shard_map/ppermute | solution.py:439
  497.4 49.7 %collective-permute-start.85 = (bf16[256,3072]{1,0:T(8,128)(2,1)}, bf16[256,3072]{1,0:T(8,128)(2,1)}, u32[]{:S(2)}, u32[]{:S(2)}) collective-permute-start(bf16[256,3072]{1,0:T(8,128)(2,1)} %pad_maximum_fusion.27), channel_id=1, source_target_pairs={{2,16},{4,18},{18,20},{20,22},{3,17},{5,19},{19,21},{21,23},{10,24... | collective-permute-start | bytes 4718600 | tf_op jit(solution)/shard_map/ppermute | solution.py:439
  516.5 30.4 %collective-permute-start.34 = (bf16[256,1024]{1,0:T(8,128)(2,1)S(1)}, bf16[256,1024]{1,0:T(8,128)(2,1)S(1)}, u32[]{:S(2)}, u32[]{:S(2)}) collective-permute-start(bf16[256,1024]{1,0:T(8,128)(2,1)S(1)} %fusion.116), channel_id=1, source_target_pairs={{0,1},{1,0},{2,3},{3,2},{4,5},{5,4},{6,7},{7,6},{8,9},{9,8},{10,11... | collective-permute-start | bytes 1572872 | tf_op jit(solution)/shard_map/cond/branch_1_fun/ppermute | solution.py:27
  549.4 66.8 %collective-permute-start.86 = (bf16[256,2048]{1,0:T(8,128)(2,1)}, bf16[256,2048]{1,0:T(8,128)(2,1)}, u32[]{:S(2)}, u32[]{:S(2)}) collective-permute-start(bf16[256,2048]{1,0:T(8,128)(2,1)} %get-tuple-element.1057), channel_id=1, source_target_pairs={{0,16},{8,24},{16,0},{24,8},{1,17},{9,25},{17,1},{25,9},{2,18},{10... | collective-permute-start | bytes 3145736 | tf_op jit(solution)/shard_map/ppermute | solution.py:366
  551.7 64.4 %collective-permute-start.87 = (bf16[256,2048]{1,0:T(8,128)(2,1)}, bf16[256,2048]{1,0:T(8,128)(2,1)}, u32[]{:S(2)}, u32[]{:S(2)}) collective-permute-start(bf16[256,2048]{1,0:T(8,128)(2,1)} %get-tuple-element.1056), channel_id=1, source_target_pairs={{0,8},{8,0},{16,24},{24,16},{1,9},{9,1},{17,25},{25,17},{2,10},{10... | collective-permute-start | bytes 3145736 | tf_op jit(solution)/shard_map/ppermute | solution.py:366
  552.2 64.0 %collective-permute-start.88 = (bf16[256,2048]{1,0:T(8,128)(2,1)}, bf16[256,2048]{1,0:T(8,128)(2,1)}, u32[]{:S(2)}, u32[]{:S(2)}) collective-permute-start(bf16[256,2048]{1,0:T(8,128)(2,1)} %get-tuple-element.1055), channel_id=1, source_target_pairs={{0,24},{8,16},{16,8},{24,0},{1,25},{9,17},{17,9},{25,1},{2,26},{10... | collective-permute-start | bytes 3145736 | tf_op jit(solution)/shard_map/ppermute | solution.py:366
  577.8 38.3 %collective-permute-start.89 = (bf16[256,1024]{1,0:T(8,128)(2,1)}, bf16[256,1024]{1,0:T(8,128)(2,1)}, u32[]{:S(2)}, u32[]{:S(2)}) collective-permute-start(bf16[256,1024]{1,0:T(8,128)(2,1)} %copy-done.75), channel_id=1, source_target_pairs={{16,16},{18,20},{20,18},{22,22},{17,17},{19,21},{21,19},{23,23},{2... | collective-permute-start | bytes 1572872 | tf_op jit(solution)/shard_map/ppermute | solution.py:455
  579.3 36.8 %collective-permute-start.90 = (bf16[256,1024]{1,0:T(8,128)(2,1)}, bf16[256,1024]{1,0:T(8,128)(2,1)}, u32[]{:S(2)}, u32[]{:S(2)}) collective-permute-start(bf16[256,1024]{1,0:T(8,128)(2,1)} %copy-done.75), channel_id=1, source_target_pairs={{0,16},{2,20},{4,18},{6,22},{1,17},{3,21},{5,19},{7,23},{8,24},{10... | collective-permute-start | bytes 1572872 | tf_op jit(solution)/shard_map/ppermute | solution.py:455
  620.1 43.7 %collective-permute-start.92 = (bf16[256,2048]{1,0:T(8,128)(2,1)}, bf16[256,2048]{1,0:T(8,128)(2,1)}, u32[]{:S(2)}, u32[]{:S(2)}) collective-permute-start(bf16[256,2048]{1,0:T(8,128)(2,1)} %add_convert_fusion.7), channel_id=1, source_target_pairs={{0,0},{6,2},{16,4},{22,6},{1,1},{7,3},{17,5},{23,7},{8,8},{14,10},... | collective-permute-start | bytes 3145736 | tf_op jit(solution)/shard_map/ppermute | solution.py:439
  621.4 42.4 %collective-permute-start.93 = (bf16[256,2048]{1,0:T(8,128)(2,1)}, bf16[256,2048]{1,0:T(8,128)(2,1)}, u32[]{:S(2)}, u32[]{:S(2)}) collective-permute-start(bf16[256,2048]{1,0:T(8,128)(2,1)} %add_convert_fusion.7), channel_id=1, source_target_pairs={{2,0},{4,2},{18,4},{20,6},{3,1},{5,3},{19,5},{21,7},{10,8},{12,10}... | collective-permute-start | bytes 3145736 | tf_op jit(solution)/shard_map/ppermute | solution.py:439
  627.5 36.3 %collective-permute-start.91 = (bf16[512,1024]{1,0:T(8,128)(2,1)}, bf16[512,1024]{1,0:T(8,128)(2,1)}, u32[]{:S(2)}, u32[]{:S(2)}) collective-permute-start(bf16[512,1024]{1,0:T(8,128)(2,1)} %get-tuple-element.1079), channel_id=1, source_target_pairs={{0,8},{8,0},{1,9},{9,1},{2,10},{10,2},{3,11},{11,3},{4,12},{12,4},... | collective-permute-start | bytes 3145736 | tf_op jit(solution)/shard_map/ppermute | solution.py:27
  635.4 24.2 %collective-permute-start.40 = (bf16[256,1024]{1,0:T(8,128)(2,1)S(1)}, bf16[256,1024]{1,0:T(8,128)(2,1)S(1)}, u32[]{:S(2)}, u32[]{:S(2)}) collective-permute-start(bf16[256,1024]{1,0:T(8,128)(2,1)S(1)} %fusion.138), channel_id=1, source_target_pairs={{0,1},{1,0},{2,3},{3,2},{4,5},{5,4},{6,7},{7,6},{8,9},{9,8},{10,11... | collective-permute-start | bytes 1572872 | tf_op jit(solution)/shard_map/cond/branch_1_fun/ppermute | solution.py:27
  668.6 37.8 %collective-permute-start.94 = (bf16[256,1024]{1,0:T(8,128)(2,1)}, bf16[256,1024]{1,0:T(8,128)(2,1)S(1)}, u32[]{:S(2)}, u32[]{:S(2)}) collective-permute-start(bf16[256,1024]{1,0:T(8,128)(2,1)} %get-tuple-element.749), channel_id=1, source_target_pairs={{0,0},{2,4},{4,2},{6,6},{1,1},{3,5},{5,3},{7,7},{8,8},{10,12},{12,... | collective-permute-start | bytes 1572872 | tf_op jit(solution)/shard_map/ppermute | solution.py:455
  671.9 34.5 %collective-permute-start.95 = (bf16[256,1024]{1,0:T(8,128)(2,1)}, bf16[256,1024]{1,0:T(8,128)(2,1)S(1)}, u32[]{:S(2)}, u32[]{:S(2)}) collective-permute-start(bf16[256,1024]{1,0:T(8,128)(2,1)} %get-tuple-element.749), channel_id=1, source_target_pairs={{16,0},{18,4},{20,2},{22,6},{17,1},{19,5},{21,3},{23,7},{24,8},{26... | collective-permute-start | bytes 1572872 | tf_op jit(solution)/shard_map/ppermute | solution.py:455
  675.9 20.2 %collective-permute-start.96 = (bf16[256,1024]{1,0:T(8,128)(2,1)S(1)}, bf16[256,1024]{1,0:T(8,128)(2,1)S(1)}, u32[]{:S(2)}, u32[]{:S(2)}) collective-permute-start(bf16[256,1024]{1,0:T(8,128)(2,1)S(1)} %fusion.148), channel_id=1, source_target_pairs={{0,16},{16,0},{1,17},{17,1},{2,18},{18,2},{3,19},{19,3},{4,20},{20... | collective-permute-start | bytes 1572872 | tf_op jit(solution)/shard_map/ppermute | solution.py:27
  681.4 21.4 %collective-permute-start.102 = (f32[8,4096]{1,0:T(8,128)S(1)}, f32[8,4096]{1,0:T(8,128)S(1)}, u32[]{:S(2)}, u32[]{:S(2)}) collective-permute-start(f32[8,4096]{1,0:T(8,128)S(1)} %add.468), channel_id=1, source_target_pairs={{0,2},{2,0},{1,3},{3,1},{4,6},{6,4},{5,7},{7,5},{8,10},{10,8},{9,1... | collective-permute-start | bytes 393224 | tf_op jit(solution)/shard_map/ppermute | solution.py:27
  (166 other events, 1349.8 us)
